TPU v7x, 512 devices: a whole 4x4x16 slice. The times are simulated.
512 devices in a mesh: fsdp: 128 (over z, x, core), mp: 4 (over y).
Axes of the slice: x: 4, y: 4, z: 16, core: 2. Of those that a mesh axis runs over, the one named last changes fastest.
Arguments:
- gradient: bfloat16 [128, 512, 512], P(None, 'fsdp', 'mp')
- owner_map: int32 [128], replicated, may hold values from 0 to 127, as said below
- left_stats: float32 [384, 512, 512], P('fsdp', 'mp'), as said below
- right_stats: float32 [384, 512, 512], P('fsdp', 'mp'), as said below
- left_root: float32 [384, 512, 512], P('fsdp', 'mp'), as said below
- right_root: float32 [384, 512, 512], P('fsdp', 'mp'), as said below
Outputs:
- update: bfloat16 [128, 512, 512], P(None, 'fsdp', 'mp')
- left_new: float32 [384, 512, 512], P('fsdp', 'mp')
- right_new: float32 [384, 512, 512], P('fsdp', 'mp')
Inputs may be any that keep to these rules, and one draw needn't show every extreme that they name: `owner_map`: no index is named by more than 3 entries, and some index by exactly 3. `left_stats`: every block is symmetric. `right_stats`: every block is symmetric. `left_root`: every block is symmetric. `right_root`: every block is symmetric.
All inputs are finite; a program needn't handle non-finite values.
Results may differ from a plain program's by a relative error of at most 0.0014.
Values may be sent and summed in bfloat16 or wider, within the bound.
No kernel may reach another device: no remote copies, remote signals or barrier semaphores. Data moves between devices by JAX's collectives and lax.ppermute only.
A program may use at most 64 MiB of HBM per device.

v0:
```python
import jax
import jax.numpy as jnp
from jax import lax
from jax.sharding import PartitionSpec as P

decay_rate = 0.95


def cell_index(owner_map, capacity):
    total_rows = owner_map.shape[0]
    positions = jnp.arange(total_rows, dtype=jnp.int32)
    same_owner = owner_map[None, :] == owner_map[:, None]
    earlier = positions[None, :] < positions[:, None]
    ranks = jnp.sum((same_owner & earlier).astype(jnp.int32), axis=1)
    return owner_map * capacity + ranks


def on_device(gradient, owner_map, left_stats, right_stats, left_root, right_root):
    fsdp_size = lax.axis_size("fsdp")
    block_count, row_share, col_share = gradient.shape
    capacity, part_rows, block_size = left_stats.shape
    highest = lax.Precision.HIGHEST
    my_owner = lax.axis_index("fsdp")
    my_part = lax.axis_index("mp")
    cell_ids = cell_index(owner_map, capacity)
    cell_count = fsdp_size * capacity
    one_hot = cell_ids[None, :] == jnp.arange(cell_count, dtype=jnp.int32)[:, None]
    up_block = jnp.arange(block_count, dtype=jnp.int32) >= block_count // 2
    grad_terms = jnp.sum(jnp.square(gradient.astype(jnp.float32)), axis=(1, 2))
    gate_grad = jnp.sum(jnp.where(up_block, 0.0, grad_terms))
    up_grad = jnp.sum(jnp.where(up_block, grad_terms, 0.0))
    flat_grad = gradient.reshape(block_count, row_share * col_share)
    packed = jnp.dot(
        one_hot.astype(jnp.bfloat16), flat_grad, preferred_element_type=jnp.float32
    ).astype(jnp.bfloat16)
    packed = packed.reshape(cell_count, row_share, col_share)
    owned_blocks = lax.all_to_all(packed, "fsdp", split_axis=0, concat_axis=1, tiled=True)
    my_cells = my_owner * capacity + jnp.arange(capacity, dtype=jnp.int32)
    holding = cell_ids[None, :] == my_cells[:, None]
    occupied = jnp.any(holding, axis=1)
    row_start = my_part * part_rows
    columns = lax.all_gather(owned_blocks, "mp", axis=2, tiled=True)
    top_rows = lax.dynamic_slice_in_dim(columns, row_start, part_rows, 1)
    left_acc = jnp.einsum("skc,sjc->skj", top_rows, columns, preferred_element_type=jnp.float32)
    right_part = jnp.einsum(
        "sik,sij->skj", owned_blocks, columns, preferred_element_type=jnp.float32
    )
    right_acc = right_part
    left_acc, right_acc = (left_acc, right_acc)
    product = jnp.einsum("sij,skj->sik", columns.astype(jnp.float32), right_root, precision=highest)
    left_acc, right_acc, halfway = (left_acc, right_acc, product)
    scaled_gain = (1.0 - decay_rate) / block_size
    filled = occupied[:, None, None]
    left_new = jnp.where(filled, decay_rate * left_stats + scaled_gain * left_acc, left_stats)
    right_new = jnp.where(filled, decay_rate * right_stats + scaled_gain * right_acc, right_stats)
    rows_result = jnp.einsum(
        "ski,sij->skj",
        left_root,
        lax.all_gather(halfway, "mp", axis=2, tiled=True),
        precision=highest,
    )
    result = lax.all_to_all(rows_result, "mp", split_axis=2, concat_axis=1, tiled=True)
    arrived = lax.all_to_all(result, "fsdp", split_axis=1, concat_axis=0, tiled=True)
    returned = jnp.dot(
        one_hot.T.astype(jnp.float32),
        arrived.reshape(cell_count, row_share * col_share),
        precision=highest,
    )
    returned = returned.reshape(block_count, row_share, col_share)
    home_terms = jnp.sum(jnp.square(returned), axis=(1, 2))
    gate_grad, up_grad, gate_upd, up_upd = lax.psum(
        (
            gate_grad,
            up_grad,
            jnp.sum(jnp.where(up_block, 0.0, home_terms)),
            jnp.sum(jnp.where(up_block, home_terms, 0.0)),
        ),
        ("fsdp", "mp"),
    )
    gate_scale = jnp.sqrt(gate_grad / gate_upd)
    up_scale = jnp.sqrt(up_grad / up_upd)
    scales = jnp.where(up_block, up_scale, gate_scale)
    update = (returned * scales[:, None, None]).astype(jnp.bfloat16)
    return (update, left_new, right_new)


def solution(mesh):
    placed = (
        P(None, "fsdp", "mp"),
        P(),
        P("fsdp", "mp", None),
        P("fsdp", "mp", None),
        P("fsdp", "mp", None),
        P("fsdp", "mp", None),
    )
    return jax.shard_map(
        on_device,
        mesh=mesh,
        in_specs=placed,
        out_specs=(P(None, "fsdp", "mp"), P("fsdp", "mp", None), P("fsdp", "mp", None)),
        check_vma=False,
    )
```

profile of v0, /device:TPU:6, one launch (start us, length us, event | category | flops | bytes accessed | tf_op | source)
XLA Modules:
  0.0 353.9 jit_solution(13516762269692489288)
XLA Ops:
  7.2 0.9 convert_reduce_fusion
  8.1 0.7 multiply_add_fusion
  8.8 1.1 convolution_convert_fusion
  10.1 46.7 %all_to_all.51 = bf16[384,4,128]{2,1,0:T(4,128)(2,1)S(1)} all-to-all(bf16[384,4,128]{2,1,0:T(4,128)(2,1)S(1)} %reshape.32), channel_id=1, replica_groups=mesh['fsdp'=128,'mp'=4] {'fsdp'}, dimensions={0} | all-to-all | bytes 786432 | tf_op jit(solution)/shard_map/all_to_all | solution.py:37
  56.8 0.9 copy.38
  57.7 29.9 %all-gather.3.cloned.1.call-done = bf16[3,512,512]{2,1,0:T(8,128)(2,1)} async-done(((bf16[3,512,128]{2,1,0:T(8,128)(2,1)}), bf16[3,512,512]{2,1,0:T(8,128)(2,1)}) %all-gather.3.cloned.1.call-update) | async-done | bytes 1572880 | tf_op jit(solution)/shard_map/all_gather | solution.py:42
  87.6 3.7 %fusion.15 = f32[3,512,128]{2,1,0:T(8,128)} fusion(bf16[3,512,512]{2,1,0:T(8,128)(2,1)} %all-gather.3.cloned.1.call-done, f32[3,128,512]{2,1,0:T(8,128)S(1)} %copy-done), kind=kOutput, calls=%fused_computation.33 | convolution fusion | flops 1207959552 | bytes 3145728 | tf_op jit(solution)/shard_map/sij,skj->sik/dot_general | solution.py:50
  91.3 52.1 %all-gather.5.cloned.1.call-done = f32[3,512,512]{2,1,0:T(8,128)} async-done(((f32[3,512,128]{2,1,0:T(8,128)}), f32[3,512,512]{2,1,0:T(8,128)}) %all-gather.5.cloned.1.call-update) | async-done | bytes 3145744 | tf_op jit(solution)/shard_map/all_gather | solution.py:59
  143.4 6.9 %convolution_bitcast_fusion = f32[3,128,512]{1,2,0:T(8,128)S(1)} fusion(f32[3,512,512]{2,1,0:T(8,128)} %all-gather.5.cloned.1.call-done, f32[3,128,512]{2,1,0:T(8,128)S(1)} %copy-done.3), kind=kOutput, calls=%fused_computation.6 | convolution fusion | flops 1207959552 | bytes 4718592 | tf_op jit(solution)/shard_map/ski,sij->skj/dot_general | solution.py:56
  150.4 0.5 copy.40
  150.9 18.0 %all_to_all.52 = f32[3,128,512]{1,0,2:T(4,128)S(1)} all-to-all(f32[3,128,512]{1,0,2:T(4,128)S(1)} %copy.40), channel_id=1, replica_groups=mesh['fsdp'=128,'mp'=4] {'mp'}, dimensions={2} | all-to-all | bytes 1572864 | tf_op jit(solution)/shard_map/all_to_all | solution.py:62
  169.0 0.3 copy.42
  169.3 1.5 copy.43
  170.8 16.6 %all-to-all-start.2 = ((f32[3,512,128]{2,0,1:T(4,128)}), f32[3,512,128]{2,0,1:T(4,128)S(1)}, u32[]{:S(2)}, u32[]{:S(2)}) async-start(f32[3,512,128]{2,0,1:T(4,128)} %copy.43), calls=%async_computation.2 | async-start | bytes 2097152 | tf_op jit(solution)/shard_map/all_to_all | solution.py:63
  187.5 1.0 multiply_reduce_fusion.1
  188.5 0.7 select_reduce_fusion.3
  189.4 2.8 fusion.2
  192.2 1.3 fusion.3
  193.5 48.5 %all-to-all-done.2 = f32[3,512,128]{2,0,1:T(4,128)S(1)} async-done(((f32[3,512,128]{2,0,1:T(4,128)}), f32[3,512,128]{2,0,1:T(4,128)S(1)}, u32[]{:S(2)}, u32[]{:S(2)}) %all-to-all-start.2) | async-done | bytes 786464 | tf_op jit(solution)/shard_map/all_to_all | solution.py:63
  242.2 0.3 copy.46
  242.5 0.5 multiply_reduce_fusion
  243.0 0.7 select_reduce_fusion.2
  243.7 99.8 %all-reduce = (f32[]{:T(128)}, f32[]{:T(128)}, f32[]{:T(128)}, f32[]{:T(128)}) all-reduce(f32[]{:T(128)} %get-tuple-element.21, f32[]{:T(128)} %get-tuple-element.19, f32[]{:T(128)} %get-tuple-element.20, f32[]{:T(128)} %get-tuple-element.18), channel_id=1, replica_groups=mesh['fsdp'=128,'mp'=4] {'fsdp','mp'}, use_global_device_ids=true, to_apply=%region_8.9 | all-reduce | flops 4 | bytes 32 | tf_op jit(solution)/shard_map/psum | solution.py:71
  346.3 0.8 copy.48
  (25 shorter events, 0.8 us)
Async XLA Ops:
  7.2 80.4 %copy-start = (f32[3,128,512]{2,1,0:T(8,128)S(1)}, f32[3,128,512]{2,1,0:T(8,128)}, u32[]{:S(2)}) copy-start(f32[3,128,512]{2,1,0:T(8,128)} %param.11) | copy-start | bytes 2359300
  7.2 80.4 %all-gather.3.cloned.1.call-start = ((), (), s32[]{:S(2)}) async-start(), calls=%async_computation.3 | async-start | bytes 1966080 | tf_op jit(solution)/shard_map/all_gather | solution.py:42
  57.7 85.7 %copy-start.3 = (f32[3,128,512]{2,1,0:T(8,128)S(1)}, f32[3,128,512]{2,1,0:T(8,128)}, u32[]{:S(2)}) copy-start(f32[3,128,512]{2,1,0:T(8,128)} %param.10) | copy-start | bytes 2359300
  57.7 85.7 %all-gather.5.cloned.1.call-start = ((), (), s32[]{:S(2)}) async-start(), calls=%async_computation.4 | async-start | bytes 3932160 | tf_op jit(solution)/shard_map/all_gather | solution.py:59
  169.3 18.2 %copy-start.5 = (bf16[128,4,128]{2,1,0:T(4,128)(2,1)S(1)}, bf16[128,4,128]{2,1,0:T(4,128)(2,1)}, u32[]{:S(2)}) copy-start(bf16[128,4,128]{2,1,0:T(4,128)(2,1)} %param.6) | copy-start | bytes 393220
  170.8 18.6 %copy-start.1 = (bf16[3,512,512]{2,1,0:T(8,128)(2,1)S(1)}, bf16[3,512,512]{2,1,0:T(8,128)(2,1)}, u32[]{:S(2)}) copy-start(bf16[3,512,512]{2,1,0:T(8,128)(2,1)} %all-gather.3.cloned.1.call-done) | copy-start | bytes 4718596
  170.8 71.2 %all-to-all-start.2 = ((f32[3,512,128]{2,0,1:T(4,128)}), f32[3,512,128]{2,0,1:T(4,128)S(1)}, u32[]{:S(2)}, u32[]{:S(2)}) async-start(f32[3,512,128]{2,0,1:T(4,128)} %copy.43), calls=%async_computation.2 | async-start | bytes 2097152 | tf_op jit(solution)/shard_map/all_to_all | solution.py:63
  189.4 2.8 copy-start.2
  189.4 2.8 copy-start.4
Sparse Core Ops, SparseCore 0:
  57.8 29.7 all-gather.2
  91.4 51.9 all-gather.4
where the time goes:
time: 356 us; the launch traced here: 354 us
  blocking collectives  165 us (46%)
  waiting for transfers between devices  130 us (37%)
  between operations  16.9 us (5%)
  starting transfers between devices  16.7 us (5%)
  matrix products  16.4 us (5%)
  local copies, waits for them, and re-layouts  4.71 us (1%)
  other arithmetic  4.18 us (1%)
    psum x1, blocking collectives, on_device(): lax.psum((gate_grad, up_grad, jnp.sum(jnp.where(up_block, 0.0, home_terms...  99.8 us
    all_gather x1, waiting for transfers between devices, on_device(): lax.all_gather(halfway, 'mp', axis=2, tiled=True)  52.1 us
    all_to_all x1, waiting for transfers between devices, on_device(): lax.all_to_all(result, 'fsdp', split_axis=1, concat_axis=0, tiled=True)  48.5 us
    all_to_all x1, blocking collectives, on_device(): lax.all_to_all(packed, 'fsdp', split_axis=0, concat_axis=1, tiled=True)  46.7 us
    all_gather x1, waiting for transfers between devices, on_device(): columns = lax.all_gather(owned_blocks, 'mp', axis=2, tiled=True)  29.9 us
    all_to_all x1, blocking collectives, on_device(): lax.all_to_all(rows_result, 'mp', split_axis=2, concat_axis=1, tiled=True)  18 us
    all_to_all x1, starting transfers between devices, on_device(): lax.all_to_all(result, 'fsdp', split_axis=1, concat_axis=0, tiled=True)  16.6 us
  transfers between devices with their start and end apart: 3, of which 3 were waited for; matrix products, arithmetic and copies ran while one was open for 2% of the time, Pallas kernels for 0%

commit v1 on v0

v1 whole, which is shorter than its diff:
```python
import jax
import jax.numpy as jnp
from jax import lax
from jax.sharding import PartitionSpec as P

decay_rate = 0.95
code_top = 32767.0


def cell_index(owner_map, capacity):
    total_rows = owner_map.shape[0]
    positions = jnp.arange(total_rows, dtype=jnp.int32)
    same_owner = owner_map[None, :] == owner_map[:, None]
    earlier = positions[None, :] < positions[:, None]
    ranks = jnp.sum((same_owner & earlier).astype(jnp.int32), axis=1)
    return owner_map * capacity + ranks


def ring_gather(own, axis_name, split_axis):
    up = [(i, (i + 1) % 4) for i in range(4)]
    down = [(i, (i - 1) % 4) for i in range(4)]
    first, second = jnp.split(own, 2, axis=split_axis)
    prev_a = lax.ppermute(first, axis_name, up)
    next_b = lax.ppermute(second, axis_name, down)
    prev_b = lax.ppermute(second, axis_name, up)
    next_a = lax.ppermute(first, axis_name, down)
    far_a = lax.ppermute(prev_a, axis_name, up)
    far_b = lax.ppermute(next_b, axis_name, down)
    join = lambda a, b: jnp.concatenate([a, b], axis=split_axis)
    return [own, join(next_a, next_b), join(far_a, far_b), join(prev_a, prev_b)]


def direct_gather(own, axis_name):
    shift = lambda k: lax.ppermute(own, axis_name, [(i, (i - k) % 4) for i in range(4)])
    return [own, shift(1), shift(2), shift(3)]


def rolled(array, start, axis):
    twice = jnp.concatenate([array, array], axis=axis)
    return lax.dynamic_slice_in_dim(twice, start, array.shape[axis], axis)


def fsdp_shift(delta, stride, size):
    pairs = []
    for i in range(128):
        place = i // stride % size
        pairs.append((i, i + ((place + delta) % size - place) * stride))
    return pairs


def part_gather(array, stride, size):
    place = lax.axis_index("fsdp") // stride % size
    got = [array]
    for delta in range(1, size):
        got.append(lax.ppermute(array, "fsdp", fsdp_shift(-delta, stride, size)))
    return rolled(jnp.stack(got), (size - place) % size, 0)


def split_two(array):
    high = lax.reduce_precision(array, 8, 7)
    return high.astype(jnp.bfloat16), (array - high).astype(jnp.bfloat16)


def dot32(spec, a, b):
    return jnp.einsum(spec, a, b, preferred_element_type=jnp.float32)


def on_device(gradient, owner_map, left_stats, right_stats, left_root, right_root):
    fsdp_size = lax.axis_size("fsdp")
    block_count, row_share, col_share = gradient.shape
    capacity, part_rows, block_size = left_stats.shape
    my_owner = lax.axis_index("fsdp")
    my_part = lax.axis_index("mp")
    row_start = my_part * part_rows
    left_parts = direct_gather(left_root, "mp")

    cell_ids = cell_index(owner_map, capacity)
    cell_count = fsdp_size * capacity
    one_hot = cell_ids[None, :] == jnp.arange(cell_count, dtype=jnp.int32)[:, None]
    flat_grad = gradient.reshape(block_count, row_share * col_share)
    packed = jnp.dot(
        one_hot.astype(jnp.bfloat16), flat_grad, preferred_element_type=jnp.float32
    ).astype(jnp.bfloat16)
    packed = packed.reshape(cell_count, row_share, col_share)
    owned = lax.all_to_all(packed, "fsdp", split_axis=0, concat_axis=1, tiled=True)

    up_block = jnp.arange(block_count, dtype=jnp.int32) >= block_count // 2
    my_cells = my_owner * capacity + jnp.arange(capacity, dtype=jnp.int32)
    holding = cell_ids[None, :] == my_cells[:, None]
    occupied = jnp.any(holding, axis=1)
    cell_up = jnp.any(holding & up_block[None, :], axis=1)

    turned = jnp.concatenate(ring_gather(owned, "mp", 1), axis=2)
    right_high, right_low = split_two(rolled(right_root, row_start, 2))
    half = dot32("sij,skj->sik", turned, right_high) + dot32("sij,skj->sik", turned, right_low)
    half_high, half_low = split_two(half)
    left_high, left_low = split_two(jnp.concatenate(left_parts, axis=1))
    result = (
        dot32("ski,sij->skj", left_high, half_high)
        + dot32("ski,sij->skj", left_high, half_low)
        + dot32("ski,sij->skj", left_low, half_high)
    )
    result = rolled(result, block_size - row_start, 1)
    result = jnp.where(occupied[:, None, None], result, 0.0)

    top = jnp.maximum(jnp.max(jnp.abs(result), axis=(1, 2)), 1e-30)
    root = jnp.sqrt(jnp.abs(result) * (code_top * code_top / top)[:, None, None])
    code = jnp.round(jnp.where(result < 0, -root, root)).astype(jnp.int16)

    upd_terms = jnp.sum(jnp.square(result), axis=(1, 2))
    owned_terms = jnp.sum(jnp.square(owned.astype(jnp.float32)), axis=(1, 2))
    owned_terms = jnp.where(occupied, owned_terms, 0.0)
    sums = jnp.stack(
        [
            jnp.sum(jnp.where(cell_up, 0.0, owned_terms)),
            jnp.sum(jnp.where(cell_up, owned_terms, 0.0)),
            jnp.sum(jnp.where(cell_up, 0.0, upd_terms)),
            jnp.sum(jnp.where(cell_up, upd_terms, 0.0)),
        ]
    )
    sums = sum(direct_gather(sums, "mp"))
    facts = jnp.concatenate([sums, top, jnp.zeros((1,), jnp.float32)])
    all_facts = part_gather(part_gather(facts, 1, 8), 8, 16)
    all_facts = all_facts.reshape(fsdp_size, 8)

    message = code.reshape(capacity, fsdp_size, row_share, col_share)
    arrived = lax.all_to_all(message, "fsdp", split_axis=1, concat_axis=1, tiled=True)

    top_rows = lax.dynamic_slice_in_dim(turned, row_start, part_rows, 1)
    left_acc = dot32("skc,sjc->skj", top_rows, turned)
    right_acc = rolled(dot32("sik,sij->skj", owned, turned), block_size - row_start, 2)
    scaled_gain = (1.0 - decay_rate) / block_size
    filled = occupied[:, None, None]
    left_new = jnp.where(filled, decay_rate * left_stats + scaled_gain * left_acc, left_stats)
    right_new = jnp.where(filled, decay_rate * right_stats + scaled_gain * right_acc, right_stats)

    sums = jnp.sum(all_facts[:, :4], axis=0)
    gate_scale = jnp.sqrt(sums[0] / sums[2])
    up_scale = jnp.sqrt(sums[1] / sums[3])
    my_tops = all_facts[:, 4 : 4 + capacity].reshape(cell_count)
    code_step = my_tops[cell_ids] / (code_top * code_top)

    slot = cell_ids % capacity
    picked = arrived[slot, cell_ids // capacity].astype(jnp.float32)
    returned = picked * jnp.abs(picked) * code_step[:, None, None]
    scales = jnp.where(up_block, up_scale, gate_scale)
    update = (returned * scales[:, None, None]).astype(jnp.bfloat16)
    return (update, left_new, right_new)


def solution(mesh):
    placed = (
        P(None, "fsdp", "mp"),
        P(),
        P("fsdp", "mp", None),
        P("fsdp", "mp", None),
        P("fsdp", "mp", None),
        P("fsdp", "mp", None),
    )
    return jax.shard_map(
        on_device,
        mesh=mesh,
        in_specs=placed,
        out_specs=(P(None, "fsdp", "mp"), P("fsdp", "mp", None), P("fsdp", "mp", None)),
        check_vma=False,
    )
```

time: 356 us -> 241 us (0.68)
  blocking collectives: 165 us -> 0 us
  starting transfers between devices: 16.7 us -> 173 us
  waiting for transfers between devices: 130 us -> 29.8 us
  between operations: 16.9 us -> 3.9 us
  matrix products: 16.4 us -> 6.1 us
  other arithmetic: 4.18 us -> 12.7 us
  local copies, waits for them, and re-layouts: 4.71 us -> 12.9 us
    ppermute x0 -> x34, starting transfers between devices: none -> 137 us  [the longest x22 97.6 us: part_gather(): got.append(lax.ppermute(array, 'fsdp', fsdp_shift(-delta, stride, size)))]
    psum x1 -> x0, blocking collectives: 99.8 us -> none  [on_device(): lax.psum((gate_grad, up_grad, jnp.sum(jnp.where(up_block, 0.0, home_terms...]
    all_gather x2 -> x0, waiting for transfers between devices: 81.9 us -> none  [the longest x1 52.1 us: on_device(): lax.all_gather(halfway, 'mp', axis=2, tiled=True)]
    all_to_all x2 -> x0, blocking collectives: 64.7 us -> none  [the longest x1 46.7 us: on_device(): lax.all_to_all(packed, 'fsdp', split_axis=0, concat_axis=1, tiled=True)]
    all_to_all x1 -> x2, waiting for transfers between devices: 48.5 us -> 15.1 us  [the longest x1 15.1 us: on_device(): lax.all_to_all(packed, 'fsdp', split_axis=0, concat_axis=1, tiled=True)]
    all_to_all x1 -> x2, starting transfers between devices: 16.6 us -> 35.6 us  [the longest x1 19.4 us: on_device(): lax.all_to_all(packed, 'fsdp', split_axis=0, concat_axis=1, tiled=True)]
    ppermute x0 -> x34, waiting for transfers between devices: none -> 14.7 us  [the longest x6 5.23 us: direct_gather(): lax.ppermute(own, axis_name, [(i, (i - k) % 4) for i in range(4)])]
    dot_general x5 -> x7, matrix products: 15.2 us -> 4.95 us  [dot32(): return jnp.einsum(spec, a, b, preferred_element_type=jnp.float32)]
  transfers between devices with their start and end apart: 3 -> 36, of which waited for: 3 -> 6; matrix products, arithmetic and copies ran while one was open for 2% -> 8% of each run, Pallas kernels for 0% -> 0%
where the time goes in v1:
time: 241 us; the launch traced here: 238 us
  starting transfers between devices  173 us (72%)
  waiting for transfers between devices  29.8 us (12%)
  local copies, waits for them, and re-layouts  12.9 us (5%)
  other arithmetic  12.7 us (5%)
  matrix products  6.1 us (3%)
  between operations  3.9 us (2%)
    ppermute x22, starting transfers between devices, part_gather(): got.append(lax.ppermute(array, 'fsdp', fsdp_shift(-delta, stride, size)))  97.6 us
    all_to_all x1, starting transfers between devices, on_device(): lax.all_to_all(packed, 'fsdp', split_axis=0, concat_axis=1, tiled=True)  19.4 us
    ppermute x6, starting transfers between devices, direct_gather(): lax.ppermute(own, axis_name, [(i, (i - k) % 4) for i in range(4)])  19.3 us
    all_to_all x1, starting transfers between devices, on_device(): lax.all_to_all(message, 'fsdp', split_axis=1, concat_axis=1, tiled=True)  16.2 us
    all_to_all x1, waiting for transfers between devices, on_device(): lax.all_to_all(packed, 'fsdp', split_axis=0, concat_axis=1, tiled=True)  15.1 us
    ppermute x6, waiting for transfers between devices, direct_gather(): lax.ppermute(own, axis_name, [(i, (i - k) % 4) for i in range(4)])  5.23 us
    ppermute x1, waiting for transfers between devices, ring_gather(): far_a = lax.ppermute(prev_a, axis_name, up)  5.15 us
    dot_general x7, matrix products, dot32(): return jnp.einsum(spec, a, b, preferred_element_type=jnp.float32)  4.95 us
  transfers between devices with their start and end apart: 36, of which 6 were waited for; matrix products, arithmetic and copies ran while one was open for 8% of the time, Pallas kernels for 0%

profile of v1, /device:TPU:6, one launch (start us, length us, event | category | flops | bytes accessed | tf_op | source)
XLA Modules:
  0.0 238.4 jit_solution(15576091959465600352)
XLA Ops:
  4.2 19.4 %all-to-all-start = ((bf16[384,4,128]{2,1,0:T(4,128)(2,1)}), bf16[384,4,128]{2,1,0:T(4,128)(2,1)S(1)}, u32[]{:S(2)}, u32[]{:S(2)}) async-start(bf16[384,4,128]{2,1,0:T(4,128)(2,1)} %reshape.50), calls=%async_computation | async-start | bytes 786432 | tf_op jit(solution)/shard_map/all_to_all | solution.py:85
  23.6 4.9 %collective-permute-start = (f32[3,128,512]{2,1,0:T(8,128)}, f32[3,128,512]{2,1,0:T(8,128)}, u32[]{:S(2)}, u32[]{:S(2)}) collective-permute-start(f32[3,128,512]{2,1,0:T(8,128)} %param.10), channel_id=1, source_target_pairs={{0,3},{1,0},{2,1},{3,2},{4,7},{5,4},{6,5},{7,6},{8,11},{9,8},{10,9... | collective-permute-start | bytes 2359304 | tf_op jit(solution)/shard_map/ppermute | solution.py:34
  36.0 15.1 %all-to-all-done = bf16[384,4,128]{2,1,0:T(4,128)(2,1)S(1)} async-done(((bf16[384,4,128]{2,1,0:T(4,128)(2,1)}), bf16[384,4,128]{2,1,0:T(4,128)(2,1)S(1)}, u32[]{:S(2)}, u32[]{:S(2)}) %all-to-all-start) | async-done | bytes 393248 | tf_op jit(solution)/shard_map/all_to_all | solution.py:85
  58.3 5.2 %collective-permute-done = f32[3,128,512]{2,1,0:T(8,128)} collective-permute-done((f32[3,128,512]{2,1,0:T(8,128)}, f32[3,128,512]{2,1,0:T(8,128)}, u32[]{:S(2)}, u32[]{:S(2)}) %collective-permute-start) | collective-permute-done | bytes 786464 | tf_op jit(solution)/shard_map/ppermute | solution.py:34
  68.8 4.7 %collective-permute-start.3 = (bf16[3,256,128]{2,1,0:T(8,128)(2,1)S(1)}, bf16[3,256,128]{2,1,0:T(8,128)(2,1)S(1)}, u32[]{:S(2)}, u32[]{:S(2)}) collective-permute-start(bf16[3,256,128]{2,1,0:T(8,128)(2,1)S(1)} %get-tuple-element.16), channel_id=1, source_target_pairs={{0,3},{1,0},{2,1},{3,2},{4,7},{5,4},{6,5},{7,6},{8,11},{9,8},{10,9... | collective-permute-start | bytes 589832 | tf_op jit(solution)/shard_map/ppermute | solution.py:26
  73.5 3.9 %collective-permute-start.7 = (bf16[3,256,128]{2,1,0:T(8,128)(2,1)S(1)}, bf16[3,256,128]{2,1,0:T(8,128)(2,1)S(1)}, u32[]{:S(2)}, u32[]{:S(2)}) collective-permute-start(bf16[3,256,128]{2,1,0:T(8,128)(2,1)S(1)} %collective-permute-done.4), channel_id=1, source_target_pairs={{0,3},{1,0},{2,1},{3,2},{4,7},{5,4},{6,5},{7,6},{8,11},{9,8},{10,9... | collective-permute-start | bytes 589832 | tf_op jit(solution)/shard_map/ppermute | solution.py:28
  81.1 5.2 %collective-permute-done.6 = bf16[3,256,128]{2,1,0:T(8,128)(2,1)S(1)} collective-permute-done((bf16[3,256,128]{2,1,0:T(8,128)(2,1)S(1)}, bf16[3,256,128]{2,1,0:T(8,128)(2,1)S(1)}, u32[]{:S(2)}, u32[]{:S(2)}) %collective-permute-start.6) | collective-permute-done | bytes 196640 | tf_op jit(solution)/shard_map/ppermute | solution.py:27
  98.0 4.1 %collective-permute-start.9 = (f32[4]{0:T(128)S(1)}, f32[4]{0:T(128)}, u32[]{:S(2)}, u32[]{:S(2)}) collective-permute-start(f32[4]{0:T(128)S(1)} %pad_maximum_fusion), channel_id=1, source_target_pairs={{0,3},{1,0},{2,1},{3,2},{4,7},{5,4},{6,5},{7,6},{8,11},{9,8},{10,9... | collective-permute-start | bytes 56 | tf_op jit(solution)/shard_map/ppermute | solution.py:34
  104.5 16.2 %all-to-all-start.1 = ((s16[3,128,4,128]{3,2,0,1:T(4,128)(2,1)}), s16[3,128,4,128]{3,2,0,1:T(4,128)(2,1)S(1)}, u32[]{:S(2)}, u32[]{:S(2)}) async-start(s16[3,128,4,128]{3,2,0,1:T(4,128)(2,1)} %copy.88), calls=%async_computation.1 | async-start | bytes 786432 | tf_op jit(solution)/shard_map/all_to_all | solution.py:127
  132.7 4.2 %collective-permute-start.15 = (f32[8]{0:T(128)S(1)}, f32[8]{0:T(128)S(1)}, u32[]{:S(2)}, u32[]{:S(2)}) collective-permute-start(f32[8]{0:T(128)S(1)} %pad_maximum_fusion.1), channel_id=1, source_target_pairs={{0,16},{4,20},{8,24},{12,28},{16,0},{20,4},{24,8},{28,12},{32,48},... | collective-permute-start | bytes 104 | tf_op jit(solution)/shard_map/ppermute | solution.py:55
  136.9 4.0 %collective-permute-start.16 = (f32[8]{0:T(128)S(1)}, f32[8]{0:T(128)S(1)}, u32[]{:S(2)}, u32[]{:S(2)}) collective-permute-start(f32[8]{0:T(128)S(1)} %pad_maximum_fusion.1), channel_id=1, source_target_pairs={{0,12},{4,16},{8,20},{12,24},{16,28},{20,0},{24,4},{28,8},{32,44},... | collective-permute-start | bytes 104 | tf_op jit(solution)/shard_map/ppermute | solution.py:55
  146.4 5.3 %collective-permute-start.19 = (f32[8,8]{1,0:T(8,128)S(1)}, f32[8,8]{1,0:T(8,128)S(1)}, u32[]{:S(2)}, u32[]{:S(2)}) collective-permute-start(f32[8,8]{1,0:T(8,128)S(1)} %constant_dynamic-slice_fusion.1), channel_id=1, source_target_pairs={{0,480},{4,484},{8,488},{12,492},{16,496},{20,500},{24,504},{28,50... | collective-permute-start | bytes 776 | tf_op jit(solution)/shard_map/ppermute | solution.py:55
  151.7 4.2 %collective-permute-start.20 = (f32[8,8]{1,0:T(8,128)S(1)}, f32[8,8]{1,0:T(8,128)S(1)}, u32[]{:S(2)}, u32[]{:S(2)}) collective-permute-start(f32[8,8]{1,0:T(8,128)S(1)} %constant_dynamic-slice_fusion.1), channel_id=1, source_target_pairs={{0,448},{4,452},{8,456},{12,460},{16,464},{20,468},{24,472},{28,47... | collective-permute-start | bytes 776 | tf_op jit(solution)/shard_map/ppermute | solution.py:55
  155.9 6.2 %collective-permute-start.21 = (f32[8,8]{1,0:T(8,128)S(1)}, f32[8,8]{1,0:T(8,128)S(1)}, u32[]{:S(2)}, u32[]{:S(2)}) collective-permute-start(f32[8,8]{1,0:T(8,128)S(1)} %constant_dynamic-slice_fusion.1), channel_id=1, source_target_pairs={{0,416},{4,420},{8,424},{12,428},{16,432},{20,436},{24,440},{28,44... | collective-permute-start | bytes 776 | tf_op jit(solution)/shard_map/ppermute | solution.py:55
  162.1 4.1 %collective-permute-start.22 = (f32[8,8]{1,0:T(8,128)S(1)}, f32[8,8]{1,0:T(8,128)S(1)}, u32[]{:S(2)}, u32[]{:S(2)}) collective-permute-start(f32[8,8]{1,0:T(8,128)S(1)} %constant_dynamic-slice_fusion.1), channel_id=1, source_target_pairs={{0,384},{4,388},{8,392},{12,396},{16,400},{20,404},{24,408},{28,41... | collective-permute-start | bytes 776 | tf_op jit(solution)/shard_map/ppermute | solution.py:55
  168.5 9.9 %collective-permute-start.24 = (f32[8,8]{1,0:T(8,128)S(1)}, f32[8,8]{1,0:T(8,128)S(1)}, u32[]{:S(2)}, u32[]{:S(2)}) collective-permute-start(f32[8,8]{1,0:T(8,128)S(1)} %constant_dynamic-slice_fusion.1), channel_id=1, source_target_pairs={{0,320},{4,324},{8,328},{12,332},{16,336},{20,340},{24,344},{28,34... | collective-permute-start | bytes 776 | tf_op jit(solution)/shard_map/ppermute | solution.py:55
  178.6 4.8 %collective-permute-start.25 = (f32[8,8]{1,0:T(8,128)S(1)}, f32[8,8]{1,0:T(8,128)S(1)}, u32[]{:S(2)}, u32[]{:S(2)}) collective-permute-start(f32[8,8]{1,0:T(8,128)S(1)} %constant_dynamic-slice_fusion.1), channel_id=1, source_target_pairs={{0,288},{4,292},{8,296},{12,300},{16,304},{20,308},{24,312},{28,31... | collective-permute-start | bytes 776 | tf_op jit(solution)/shard_map/ppermute | solution.py:55
  183.5 7.9 %collective-permute-start.26 = (f32[8,8]{1,0:T(8,128)S(1)}, f32[8,8]{1,0:T(8,128)S(1)}, u32[]{:S(2)}, u32[]{:S(2)}) collective-permute-start(f32[8,8]{1,0:T(8,128)S(1)} %constant_dynamic-slice_fusion.1), channel_id=1, source_target_pairs={{0,256},{4,260},{8,264},{12,268},{16,272},{20,276},{24,280},{28,28... | collective-permute-start | bytes 776 | tf_op jit(solution)/shard_map/ppermute | solution.py:55
  191.5 4.7 %collective-permute-start.27 = (f32[8,8]{1,0:T(8,128)S(1)}, f32[8,8]{1,0:T(8,128)S(1)}, u32[]{:S(2)}, u32[]{:S(2)}) collective-permute-start(f32[8,8]{1,0:T(8,128)S(1)} %constant_dynamic-slice_fusion.1), channel_id=1, source_target_pairs={{0,224},{4,228},{8,232},{12,236},{16,240},{20,244},{24,248},{28,25... | collective-permute-start | bytes 776 | tf_op jit(solution)/shard_map/ppermute | solution.py:55
  196.3 9.7 %collective-permute-start.28 = (f32[8,8]{1,0:T(8,128)S(1)}, f32[8,8]{1,0:T(8,128)S(1)}, u32[]{:S(2)}, u32[]{:S(2)}) collective-permute-start(f32[8,8]{1,0:T(8,128)S(1)} %constant_dynamic-slice_fusion.1), channel_id=1, source_target_pairs={{0,192},{4,196},{8,200},{12,204},{16,208},{20,212},{24,216},{28,22... | collective-permute-start | bytes 776 | tf_op jit(solution)/shard_map/ppermute | solution.py:55
  209.0 3.6 %collective-permute-start.30 = (f32[8,8]{1,0:T(8,128)S(1)}, f32[8,8]{1,0:T(8,128)S(1)}, u32[]{:S(2)}, u32[]{:S(2)}) collective-permute-start(f32[8,8]{1,0:T(8,128)S(1)} %constant_dynamic-slice_fusion.1), channel_id=1, source_target_pairs={{0,128},{4,132},{8,136},{12,140},{16,144},{20,148},{24,152},{28,15... | collective-permute-start | bytes 776 | tf_op jit(solution)/shard_map/ppermute | solution.py:55
  212.8 6.5 %collective-permute-start.31 = (f32[8,8]{1,0:T(8,128)S(1)}, f32[8,8]{1,0:T(8,128)S(1)}, u32[]{:S(2)}, u32[]{:S(2)}) collective-permute-start(f32[8,8]{1,0:T(8,128)S(1)} %constant_dynamic-slice_fusion.1), channel_id=1, source_target_pairs={{0,96},{4,100},{8,104},{12,108},{16,112},{20,116},{24,120},{28,124... | collective-permute-start | bytes 776 | tf_op jit(solution)/shard_map/ppermute | solution.py:55
  219.4 4.4 %collective-permute-start.32 = (f32[8,8]{1,0:T(8,128)S(1)}, f32[8,8]{1,0:T(8,128)S(1)}, u32[]{:S(2)}, u32[]{:S(2)}) collective-permute-start(f32[8,8]{1,0:T(8,128)S(1)} %constant_dynamic-slice_fusion.1), channel_id=1, source_target_pairs={{0,64},{4,68},{8,72},{12,76},{16,80},{20,84},{24,88},{28,92},{32,9... | collective-permute-start | bytes 776 | tf_op jit(solution)/shard_map/ppermute | solution.py:55
  223.9 4.6 %collective-permute-start.33 = (f32[8,8]{1,0:T(8,128)S(1)}, f32[8,8]{1,0:T(8,128)S(1)}, u32[]{:S(2)}, u32[]{:S(2)}) collective-permute-start(f32[8,8]{1,0:T(8,128)S(1)} %constant_dynamic-slice_fusion.1), channel_id=1, source_target_pairs={{0,32},{4,36},{8,40},{12,44},{16,48},{20,52},{24,56},{28,60},{32,6... | collective-permute-start | bytes 776 | tf_op jit(solution)/shard_map/ppermute | solution.py:55
  (128 shorter events, 71.7 us)
Async XLA Ops:
  4.2 46.9 %all-to-all-start = ((bf16[384,4,128]{2,1,0:T(4,128)(2,1)}), bf16[384,4,128]{2,1,0:T(4,128)(2,1)S(1)}, u32[]{:S(2)}, u32[]{:S(2)}) async-start(bf16[384,4,128]{2,1,0:T(4,128)(2,1)} %reshape.50), calls=%async_computation | async-start | bytes 786432 | tf_op jit(solution)/shard_map/all_to_all | solution.py:85
  23.6 40.0 %collective-permute-start = (f32[3,128,512]{2,1,0:T(8,128)}, f32[3,128,512]{2,1,0:T(8,128)}, u32[]{:S(2)}, u32[]{:S(2)}) collective-permute-start(f32[3,128,512]{2,1,0:T(8,128)} %param.10), channel_id=1, source_target_pairs={{0,3},{1,0},{2,1},{3,2},{4,7},{5,4},{6,5},{7,6},{8,11},{9,8},{10,9... | collective-permute-start | bytes 2359304 | tf_op jit(solution)/shard_map/ppermute | solution.py:34
  28.5 36.2 %collective-permute-start.1 = (f32[3,128,512]{2,1,0:T(8,128)}, f32[3,128,512]{2,1,0:T(8,128)}, u32[]{:S(2)}, u32[]{:S(2)}) collective-permute-start(f32[3,128,512]{2,1,0:T(8,128)} %param.10), channel_id=1, source_target_pairs={{0,2},{1,3},{2,0},{3,1},{4,6},{5,7},{6,4},{7,5},{8,10},{9,11},{10,... | collective-permute-start | bytes 2359304 | tf_op jit(solution)/shard_map/ppermute | solution.py:34
  31.1 48.3 %collective-permute-start.2 = (f32[3,128,512]{2,1,0:T(8,128)}, f32[3,128,512]{2,1,0:T(8,128)}, u32[]{:S(2)}, u32[]{:S(2)}) collective-permute-start(f32[3,128,512]{2,1,0:T(8,128)} %param.10), channel_id=1, source_target_pairs={{0,1},{1,2},{2,3},{3,0},{4,5},{5,6},{6,7},{7,4},{8,9},{9,10},{10,1... | collective-permute-start | bytes 2359304 | tf_op jit(solution)/shard_map/ppermute | solution.py:34
  51.3 26.2 %collective-permute-start.5 = (bf16[3,256,128]{2,1,0:T(8,128)(2,1)S(1)}, bf16[3,256,128]{2,1,0:T(8,128)(2,1)S(1)}, u32[]{:S(2)}, u32[]{:S(2)}) collective-permute-start(bf16[3,256,128]{2,1,0:T(8,128)(2,1)S(1)} %get-tuple-element.16), channel_id=1, source_target_pairs={{0,1},{1,2},{2,3},{3,0},{4,5},{5,6},{6,7},{7,4},{8,9},{9,10},{10,1... | collective-permute-start | bytes 589832 | tf_op jit(solution)/shard_map/ppermute | solution.py:23
  54.8 18.7 %collective-permute-start.4 = (bf16[3,256,128]{2,1,0:T(8,128)(2,1)S(1)}, bf16[3,256,128]{2,1,0:T(8,128)(2,1)S(1)}, u32[]{:S(2)}, u32[]{:S(2)}) collective-permute-start(bf16[3,256,128]{2,1,0:T(8,128)(2,1)S(1)} %get-tuple-element.17), channel_id=1, source_target_pairs={{0,3},{1,0},{2,1},{3,2},{4,7},{5,4},{6,5},{7,6},{8,11},{9,8},{10,9... | collective-permute-start | bytes 589832 | tf_op jit(solution)/shard_map/ppermute | solution.py:24
  93.1 30.4 %collective-permute-start.11 = (f32[4]{0:T(128)S(1)}, f32[4]{0:T(128)}, u32[]{:S(2)}, u32[]{:S(2)}) collective-permute-start(f32[4]{0:T(128)S(1)} %pad_maximum_fusion), channel_id=1, source_target_pairs={{0,1},{1,2},{2,3},{3,0},{4,5},{5,6},{6,7},{7,4},{8,9},{9,10},{10,1... | collective-permute-start | bytes 56 | tf_op jit(solution)/shard_map/ppermute | solution.py:34
  95.1 28.5 %collective-permute-start.10 = (f32[4]{0:T(128)S(1)}, f32[4]{0:T(128)}, u32[]{:S(2)}, u32[]{:S(2)}) collective-permute-start(f32[4]{0:T(128)S(1)} %pad_maximum_fusion), channel_id=1, source_target_pairs={{0,2},{1,3},{2,0},{3,1},{4,6},{5,7},{6,4},{7,5},{8,10},{9,11},{10,... | collective-permute-start | bytes 56 | tf_op jit(solution)/shard_map/ppermute | solution.py:34
  98.0 25.5 %collective-permute-start.9 = (f32[4]{0:T(128)S(1)}, f32[4]{0:T(128)}, u32[]{:S(2)}, u32[]{:S(2)}) collective-permute-start(f32[4]{0:T(128)S(1)} %pad_maximum_fusion), channel_id=1, source_target_pairs={{0,3},{1,0},{2,1},{3,2},{4,7},{5,4},{6,5},{7,6},{8,11},{9,8},{10,9... | collective-permute-start | bytes 56 | tf_op jit(solution)/shard_map/ppermute | solution.py:34
  104.5 131.9 %all-to-all-start.1 = ((s16[3,128,4,128]{3,2,0,1:T(4,128)(2,1)}), s16[3,128,4,128]{3,2,0,1:T(4,128)(2,1)S(1)}, u32[]{:S(2)}, u32[]{:S(2)}) async-start(s16[3,128,4,128]{3,2,0,1:T(4,128)(2,1)} %copy.88), calls=%async_computation.1 | async-start | bytes 786432 | tf_op jit(solution)/shard_map/all_to_all | solution.py:127
  127.3 15.6 %collective-permute-start.13 = (f32[8]{0:T(128)S(1)}, f32[8]{0:T(128)S(1)}, u32[]{:S(2)}, u32[]{:S(2)}) collective-permute-start(f32[8]{0:T(128)S(1)} %pad_maximum_fusion.1), channel_id=1, source_target_pairs={{0,24},{4,28},{8,0},{12,4},{16,8},{20,12},{24,16},{28,20},{32,56},... | collective-permute-start | bytes 104 | tf_op jit(solution)/shard_map/ppermute | solution.py:55
  146.4 22.2 %collective-permute-start.19 = (f32[8,8]{1,0:T(8,128)S(1)}, f32[8,8]{1,0:T(8,128)S(1)}, u32[]{:S(2)}, u32[]{:S(2)}) collective-permute-start(f32[8,8]{1,0:T(8,128)S(1)} %constant_dynamic-slice_fusion.1), channel_id=1, source_target_pairs={{0,480},{4,484},{8,488},{12,492},{16,496},{20,500},{24,504},{28,50... | collective-permute-start | bytes 776 | tf_op jit(solution)/shard_map/ppermute | solution.py:55
  151.7 26.8 %collective-permute-start.20 = (f32[8,8]{1,0:T(8,128)S(1)}, f32[8,8]{1,0:T(8,128)S(1)}, u32[]{:S(2)}, u32[]{:S(2)}) collective-permute-start(f32[8,8]{1,0:T(8,128)S(1)} %constant_dynamic-slice_fusion.1), channel_id=1, source_target_pairs={{0,448},{4,452},{8,456},{12,460},{16,464},{20,468},{24,472},{28,47... | collective-permute-start | bytes 776 | tf_op jit(solution)/shard_map/ppermute | solution.py:55
  155.9 27.6 %collective-permute-start.21 = (f32[8,8]{1,0:T(8,128)S(1)}, f32[8,8]{1,0:T(8,128)S(1)}, u32[]{:S(2)}, u32[]{:S(2)}) collective-permute-start(f32[8,8]{1,0:T(8,128)S(1)} %constant_dynamic-slice_fusion.1), channel_id=1, source_target_pairs={{0,416},{4,420},{8,424},{12,428},{16,432},{20,436},{24,440},{28,44... | collective-permute-start | bytes 776 | tf_op jit(solution)/shard_map/ppermute | solution.py:55
  162.1 29.4 %collective-permute-start.22 = (f32[8,8]{1,0:T(8,128)S(1)}, f32[8,8]{1,0:T(8,128)S(1)}, u32[]{:S(2)}, u32[]{:S(2)}) collective-permute-start(f32[8,8]{1,0:T(8,128)S(1)} %constant_dynamic-slice_fusion.1), channel_id=1, source_target_pairs={{0,384},{4,388},{8,392},{12,396},{16,400},{20,404},{24,408},{28,41... | collective-permute-start | bytes 776 | tf_op jit(solution)/shard_map/ppermute | solution.py:55
  166.2 30.1 %collective-permute-start.23 = (f32[8,8]{1,0:T(8,128)S(1)}, f32[8,8]{1,0:T(8,128)S(1)}, u32[]{:S(2)}, u32[]{:S(2)}) collective-permute-start(f32[8,8]{1,0:T(8,128)S(1)} %constant_dynamic-slice_fusion.1), channel_id=1, source_target_pairs={{0,352},{4,356},{8,360},{12,364},{16,368},{20,372},{24,376},{28,38... | collective-permute-start | bytes 776 | tf_op jit(solution)/shard_map/ppermute | solution.py:55
  168.5 37.6 %collective-permute-start.24 = (f32[8,8]{1,0:T(8,128)S(1)}, f32[8,8]{1,0:T(8,128)S(1)}, u32[]{:S(2)}, u32[]{:S(2)}) collective-permute-start(f32[8,8]{1,0:T(8,128)S(1)} %constant_dynamic-slice_fusion.1), channel_id=1, source_target_pairs={{0,320},{4,324},{8,328},{12,332},{16,336},{20,340},{24,344},{28,34... | collective-permute-start | bytes 776 | tf_op jit(solution)/shard_map/ppermute | solution.py:55
  178.6 30.4 %collective-permute-start.25 = (f32[8,8]{1,0:T(8,128)S(1)}, f32[8,8]{1,0:T(8,128)S(1)}, u32[]{:S(2)}, u32[]{:S(2)}) collective-permute-start(f32[8,8]{1,0:T(8,128)S(1)} %constant_dynamic-slice_fusion.1), channel_id=1, source_target_pairs={{0,288},{4,292},{8,296},{12,300},{16,304},{20,308},{24,312},{28,31... | collective-permute-start | bytes 776 | tf_op jit(solution)/shard_map/ppermute | solution.py:55
  183.5 29.3 %collective-permute-start.26 = (f32[8,8]{1,0:T(8,128)S(1)}, f32[8,8]{1,0:T(8,128)S(1)}, u32[]{:S(2)}, u32[]{:S(2)}) collective-permute-start(f32[8,8]{1,0:T(8,128)S(1)} %constant_dynamic-slice_fusion.1), channel_id=1, source_target_pairs={{0,256},{4,260},{8,264},{12,268},{16,272},{20,276},{24,280},{28,28... | collective-permute-start | bytes 776 | tf_op jit(solution)/shard_map/ppermute | solution.py:55
  191.5 27.9 %collective-permute-start.27 = (f32[8,8]{1,0:T(8,128)S(1)}, f32[8,8]{1,0:T(8,128)S(1)}, u32[]{:S(2)}, u32[]{:S(2)}) collective-permute-start(f32[8,8]{1,0:T(8,128)S(1)} %constant_dynamic-slice_fusion.1), channel_id=1, source_target_pairs={{0,224},{4,228},{8,232},{12,236},{16,240},{20,244},{24,248},{28,25... | collective-permute-start | bytes 776 | tf_op jit(solution)/shard_map/ppermute | solution.py:55
  196.3 27.6 %collective-permute-start.28 = (f32[8,8]{1,0:T(8,128)S(1)}, f32[8,8]{1,0:T(8,128)S(1)}, u32[]{:S(2)}, u32[]{:S(2)}) collective-permute-start(f32[8,8]{1,0:T(8,128)S(1)} %constant_dynamic-slice_fusion.1), channel_id=1, source_target_pairs={{0,192},{4,196},{8,200},{12,204},{16,208},{20,212},{24,216},{28,22... | collective-permute-start | bytes 776 | tf_op jit(solution)/shard_map/ppermute | solution.py:55
  206.1 22.5 %collective-permute-start.29 = (f32[8,8]{1,0:T(8,128)S(1)}, f32[8,8]{1,0:T(8,128)S(1)}, u32[]{:S(2)}, u32[]{:S(2)}) collective-permute-start(f32[8,8]{1,0:T(8,128)S(1)} %constant_dynamic-slice_fusion.1), channel_id=1, source_target_pairs={{0,160},{4,164},{8,168},{12,172},{16,176},{20,180},{24,184},{28,18... | collective-permute-start | bytes 776 | tf_op jit(solution)/shard_map/ppermute | solution.py:55
  209.0 19.8 %collective-permute-start.30 = (f32[8,8]{1,0:T(8,128)S(1)}, f32[8,8]{1,0:T(8,128)S(1)}, u32[]{:S(2)}, u32[]{:S(2)}) collective-permute-start(f32[8,8]{1,0:T(8,128)S(1)} %constant_dynamic-slice_fusion.1), channel_id=1, source_target_pairs={{0,128},{4,132},{8,136},{12,140},{16,144},{20,148},{24,152},{28,15... | collective-permute-start | bytes 776 | tf_op jit(solution)/shard_map/ppermute | solution.py:55
  212.8 16.2 %collective-permute-start.31 = (f32[8,8]{1,0:T(8,128)S(1)}, f32[8,8]{1,0:T(8,128)S(1)}, u32[]{:S(2)}, u32[]{:S(2)}) collective-permute-start(f32[8,8]{1,0:T(8,128)S(1)} %constant_dynamic-slice_fusion.1), channel_id=1, source_target_pairs={{0,96},{4,100},{8,104},{12,108},{16,112},{20,116},{24,120},{28,124... | collective-permute-start | bytes 776 | tf_op jit(solution)/shard_map/ppermute | solution.py:55
  (19 other events, 177.8 us)

commit v2 on v0

v2 whole, which is shorter than its diff:
```python
import functools

import jax
import jax.numpy as jnp
from jax import lax
from jax.experimental import pallas as pl
from jax.experimental.pallas import tpu as pltpu
from jax.sharding import PartitionSpec as P

decay_rate = 0.95
code_top = 32767.0
parts = 4
near = 8
far = 16


def cell_index(owner_map, capacity):
    total_rows = owner_map.shape[0]
    positions = jnp.arange(total_rows, dtype=jnp.int32)
    same_owner = owner_map[None, :] == owner_map[:, None]
    earlier = positions[None, :] < positions[:, None]
    ranks = jnp.sum((same_owner & earlier).astype(jnp.int32), axis=1)
    return owner_map * capacity + ranks


far_groups = [[z * near + n for z in range(far)] for n in range(near)]
plane_groups = [[(z * near + n) * parts + m for n in range(near) for m in range(parts)] for z in range(far)]


def exchange(array, axis_name, groups):
    return lax.all_to_all(
        array, axis_name, split_axis=0, concat_axis=0, axis_index_groups=groups, tiled=True
    )


def dot32(spec, a, b):
    return jnp.einsum(spec, a, b, preferred_element_type=jnp.float32)


def split_two(array):
    high = array.astype(jnp.bfloat16)
    return high, (array - high.astype(jnp.float32)).astype(jnp.bfloat16)


def roots_kernel(
    part_ref, left_ref, own_ref, one_ref, two_ref, three_ref,
    left_high_ref, left_low_ref, right_high_ref, right_low_ref,
):
    part = part_ref[0]
    width = own_ref.shape[1]

    def span(step):
        at = lax.rem(part + step, parts)
        return pl.ds(pl.multiple_of(at * width, width), width)

    def put(row, col, block):
        high, low = split_two(block)
        right_high_ref[0, span(row), span(col)] = high
        right_low_ref[0, span(row), span(col)] = low

    def put_pair(row, col, block):
        put(row, col, block)
        put(col, row, block.T)

    put(0, 0, own_ref[0, :, span(0)])
    for step in range(1, parts):
        put_pair(0, step, own_ref[0, :, span(step)])
    put(1, 1, one_ref[0, :, :width])
    put_pair(1, 3, one_ref[0, :, width:])
    put(2, 2, two_ref[0, :, :width])
    put_pair(2, 1, two_ref[0, :, width:])
    put(3, 3, three_ref[0, :, :width])
    put_pair(3, 2, three_ref[0, :, width:])
    left_high_ref[0], left_low_ref[0] = split_two(left_ref[0].T)


def spread_roots(part, left_root, right_root, others):
    slots, width, order = right_root.shape
    by_slot = lambda *shape: pl.BlockSpec((1,) + shape, lambda s, *_: (s, 0, 0))
    of = lambda *shape: jax.ShapeDtypeStruct((slots,) + shape, jnp.bfloat16)
    return pl.pallas_call(
        roots_kernel,
        grid_spec=pltpu.PrefetchScalarGridSpec(
            num_scalar_prefetch=1,
            grid=(slots,),
            in_specs=[by_slot(width, order)] * 2 + [by_slot(width, 2 * width)] * 3,
            out_specs=[by_slot(order, width)] * 2 + [by_slot(order, order)] * 2,
        ),
        out_shape=[of(order, width)] * 2 + [of(order, order)] * 2,
        compiler_params=pltpu.CompilerParams(vmem_limit_bytes=32 * 1024 * 1024),
        cost_estimate=pl.CostEstimate(flops=0, bytes_accessed=8 * 1024 * 1024, transcendentals=0),
    )(part.reshape(1), left_root, right_root, *others)


def power(exponent):
    half = jnp.floor(exponent * 0.5)
    return jnp.exp2(half), jnp.exp2(exponent - half)


def coded(value):
    value = jnp.maximum(value, 1e-37)
    exponent = jnp.floor(jnp.log2(value)) + 1.0
    one, two = power(-exponent)
    share = value * one * two * 16384.0
    high = jnp.floor(share)
    return exponent, high, jnp.floor((share - high) * 16384.0)


def decoded(exponent, high, low):
    one, two = power(exponent - 14.0)
    return jnp.where(high > 0, (high + low * (1.0 / 16384.0)) * one * two, 0.0)


def precondition_kernel(
    place_ref, taken_ref, grad_ref, left_high_ref, left_low_ref, right_high_ref, right_low_ref,
    message_ref, line_ref,
):
    slot = pl.program_id(0)
    tn = (((0,), (0,)), ((), ()))
    nn = (((1,), (0,)), ((), ()))
    dot = functools.partial(lax.dot_general, preferred_element_type=jnp.float32)
    order = left_high_ref.shape[1]
    grad = jnp.concatenate([grad_ref[:, m].reshape(order, -1) for m in range(parts)], axis=1)
    half = dot(left_high_ref[0], grad, tn) + dot(left_low_ref[0], grad, tn)
    half_high, half_low = split_two(half)
    right_high = right_high_ref[0]
    result = dot(half_high, right_high, nn) + dot(half_low, right_high, nn) + dot(half_high, right_low_ref[0], nn)
    taken = taken_ref[slot]
    result = jnp.where(taken > 0, result, 0.0)
    size = jnp.abs(result)
    top = jnp.maximum(jnp.max(size), 1e-30)
    root = jnp.sqrt(size * (code_top * code_top / top))
    code = jnp.round(jnp.where(result < 0, -root, root)).astype(jnp.int32)
    wide_rows, deep = message_ref.shape[3], message_ref.shape[2]
    for step in range(far // parts):
        for device in range(near):
            for m in range(parts):
                row = (step * near + device) * deep
                message_ref[device * parts + m, step * 3 + slot] = code[
                    row : row + deep, m * wide_rows : (m + 1) * wide_rows
                ].astype(jnp.int16)

    wide = grad.astype(jnp.float32)
    grad_sum = jnp.where(taken > 0, jnp.sum(wide * wide), 0.0) * (1.0 / parts)
    upd_sum = jnp.sum(result * result)

    @pl.when(slot == 0)
    def _():
        line_ref[...] = jnp.zeros_like(line_ref)

    lane = lax.broadcasted_iota(jnp.int32, (8, 128), 1)
    at = lane - place_ref[0] * 16
    sum_at = at - place_ref[1] * 4
    is_up = jnp.where(taken > 1, 1, 0)
    line_ref[0] += jnp.where(sum_at == is_up, grad_sum, 0.0) + jnp.where(sum_at == 2 + is_up, upd_sum, 0.0)
    line_ref[1] += jnp.where((at >= 3 * slot) & (at < 3 * slot + 3), top, 0.0)

    @pl.when(slot == pl.num_programs(0) - 1)
    def _():
        row = lax.broadcasted_iota(jnp.int32, (8, 128), 0)
        in_sums = (sum_at >= 0) & (sum_at < 4)
        in_tops = (at >= 0) & (at < 9)
        exponent, high, low = coded(line_ref[0])
        sums = jnp.where(in_sums, jnp.where(row == 0, exponent, jnp.where(row == 1, high, low)), 0.0)
        exponent, high, low = coded(line_ref[1])
        step = at - 3 * jnp.where(at >= 6, 2, jnp.where(at >= 3, 1, 0))
        tops = jnp.where(in_tops, jnp.where(step == 0, exponent, jnp.where(step == 1, high, low)), 0.0)
        facts = jnp.where(row < 3, sums, tops)[:deep].astype(jnp.int32).astype(jnp.int16)
        for device in range(near * parts):
            message_ref[device, message_ref.shape[1] - 1] = facts


def precondition(place, taken, landed, roots):
    slots, width = taken.shape[0], landed.shape[2]
    rows = landed.shape[1] // slots
    order = near * rows
    message = (near * parts, slots * far // parts + 1, rows // far, width)
    by_slot = lambda *shape: pl.BlockSpec((1,) + shape, lambda s, *_: (s, 0, 0))
    return pl.pallas_call(
        precondition_kernel,
        grid_spec=pltpu.PrefetchScalarGridSpec(
            num_scalar_prefetch=2,
            grid=(slots,),
            in_specs=[pl.BlockSpec((near, parts, rows, width), lambda s, *_: (0, 0, s, 0))]
            + [by_slot(order, width)] * 2
            + [by_slot(order, order)] * 2,
            out_specs=pl.BlockSpec(message, lambda s, *_: (0, 0, 0, 0)),
            scratch_shapes=[pltpu.VMEM((2, 8, 128), jnp.float32)],
        ),
        out_shape=jax.ShapeDtypeStruct(message, jnp.int16),
        compiler_params=pltpu.CompilerParams(vmem_limit_bytes=32 * 1024 * 1024),
        cost_estimate=pl.CostEstimate(
            flops=10 * slots * order * order * width, bytes_accessed=6 * 1024 * 1024, transcendentals=0
        ),
    )(place, taken, landed.reshape(near, parts, slots * rows, width), *roots)


def repack_kernel(back_ref, ahead_ref):
    cells = ahead_ref.shape[1] - 1
    slots = cells // near
    last = back_ref.shape[1] - 1
    for m in range(parts):
        for step in range(far // parts):
            for device in range(near):
                ahead_ref[m * (far // parts) + step, device * slots : (device + 1) * slots] = back_ref[
                    device * parts + m, step * slots : (step + 1) * slots
                ]
    wide = lambda device, m: back_ref[device * parts + m, last].astype(jnp.int32)
    by_part = [functools.reduce(jnp.add, [wide(device, m) for device in range(near)]) for m in range(parts)]
    plane = functools.reduce(jnp.add, by_part)
    row = lax.broadcasted_iota(jnp.int32, plane.shape, 0)
    for m in range(parts):
        facts = jnp.where(row < 3, plane, by_part[m]).astype(jnp.int16)
        for step in range(far // parts):
            ahead_ref[m * (far // parts) + step, cells] = facts


def repack(back):
    slots = (back.shape[1] - 1) // (far // parts)
    return pl.pallas_call(
        repack_kernel,
        out_shape=jax.ShapeDtypeStruct((far, near * slots + 1) + back.shape[2:], back.dtype),
        in_specs=[pl.BlockSpec(memory_space=pltpu.VMEM)],
        out_specs=pl.BlockSpec(memory_space=pltpu.VMEM),
        compiler_params=pltpu.CompilerParams(vmem_limit_bytes=16 * 1024 * 1024),
        cost_estimate=pl.CostEstimate(flops=0, bytes_accessed=1 << 20, transcendentals=0),
    )(back)


def finish_kernel(at_ref, spot_ref, up_ref, arrived_ref, update_ref, factor_ref):
    cells = arrived_ref.shape[1] - 1
    facts = [arrived_ref[z, cells].astype(jnp.int32).astype(jnp.float32) for z in range(far)]
    row = lambda r: jnp.concatenate([fact[r : r + 1] for fact in facts], axis=0)
    sums = jnp.sum(decoded(row(0), row(1), row(2)), axis=0, keepdims=True)
    kind = lax.rem(lax.broadcasted_iota(jnp.int32, sums.shape, 1), 4)
    total = lambda k: jnp.sum(jnp.where(kind == k, sums, 0.0), axis=1, keepdims=True)
    gate_scale = jnp.sqrt(total(0) / total(2))
    up_scale = jnp.sqrt(total(1) / total(3))
    tops = row(3)
    lanes = tops.shape[1]
    steps = decoded(tops, pltpu.roll(tops, lanes - 1, 1), pltpu.roll(tops, lanes - 2, 1))
    steps = steps * (1.0 / (code_top * code_top))
    spot = spot_ref[...]
    lane = lax.broadcasted_iota(jnp.int32, spot.shape, 1)
    mine = jnp.zeros(spot.shape, jnp.float32)
    for z in range(far):
        mine += jnp.where(spot == lane + z * lanes, steps[z : z + 1], 0.0)
    step = jnp.sum(mine, axis=1, keepdims=True)
    factor_ref[...] = jnp.where(up_ref[...] > 0, up_scale, gate_scale) * step

    for b in range(update_ref.shape[0]):
        at = at_ref[b]
        code = arrived_ref[at // cells, lax.rem(at, cells)].astype(jnp.int32).astype(jnp.float32)
        update_ref[b] = (code * jnp.abs(code) * factor_ref[b : b + 1, :]).astype(jnp.bfloat16)


def finish(cell_ids, spot, up, arrived):
    blocks = cell_ids.shape[0]
    whole = lambda shape: pl.BlockSpec(shape, lambda i, *_: (0,) * len(shape))
    return pl.pallas_call(
        finish_kernel,
        grid_spec=pltpu.PrefetchScalarGridSpec(
            num_scalar_prefetch=1,
            grid=(1,),
            in_specs=[whole(spot.shape), whole(up.shape), whole(arrived.shape)],
            out_specs=whole((blocks,) + arrived.shape[2:]),
            scratch_shapes=[pltpu.VMEM((blocks, arrived.shape[3]), jnp.float32)],
        ),
        out_shape=jax.ShapeDtypeStruct((blocks,) + arrived.shape[2:], jnp.bfloat16),
        compiler_params=pltpu.CompilerParams(vmem_limit_bytes=16 * 1024 * 1024),
        cost_estimate=pl.CostEstimate(flops=0, bytes_accessed=1 << 20, transcendentals=0),
    )(cell_ids, spot, up, arrived)


def on_device(gradient, owner_map, left_stats, right_stats, left_root, right_root):
    fsdp_size = lax.axis_size("fsdp")
    block_count, row_share, col_share = gradient.shape
    capacity, part_rows, block_size = left_stats.shape
    my_owner = lax.axis_index("fsdp")
    my_part = lax.axis_index("mp")
    row_start = my_part * part_rows
    cell_count = fsdp_size * capacity

    cell_ids = cell_index(owner_map, capacity)
    one_hot = cell_ids[None, :] == jnp.arange(cell_count, dtype=jnp.int32)[:, None]
    flat_grad = gradient.reshape(block_count, row_share * col_share)
    packed = jnp.dot(
        one_hot.astype(jnp.bfloat16), flat_grad, preferred_element_type=jnp.float32
    ).astype(jnp.bfloat16)
    packed = packed.reshape(far, near, capacity, row_share, col_share)
    in_plane = exchange(packed, "fsdp", far_groups)

    def column(step):
        start = (my_part + step) % parts * part_rows
        return lax.dynamic_slice_in_dim(right_root, start, part_rows, 2)

    pair = lambda step: jnp.concatenate([column(0), column(step)], axis=2)
    send = lambda array, k: lax.ppermute(array, "mp", [(i, (i + k) % parts) for i in range(parts)])
    three = send(pair(3), 1)
    two = send(pair(3), 2)
    one = send(pair(2), 3)
    in_plane, one, two, three = lax.optimization_barrier((in_plane, one, two, three))

    fanned = jnp.broadcast_to(
        in_plane.transpose(1, 2, 0, 3, 4)[:, None], (near, parts, capacity, far, row_share, col_share)
    ).reshape(near * parts, capacity * far * row_share, col_share)
    landed = exchange(fanned, ("fsdp", "mp"), plane_groups)

    up_block = jnp.arange(block_count, dtype=jnp.int32) >= block_count // 2
    my_cells = my_owner * capacity + jnp.arange(capacity, dtype=jnp.int32)
    holding = cell_ids[None, :] == my_cells[:, None]
    taken = jnp.max(jnp.where(holding, 1 + up_block.astype(jnp.int32)[None, :], 0), axis=1)

    left_high, left_low, right_high, right_low = spread_roots(my_part, left_root, right_root, (one, two, three))

    def landed_order(array):
        split = array.reshape(capacity, far, near, row_share, part_rows)
        return jnp.swapaxes(split, 1, 2).reshape(capacity, block_size, part_rows)

    place = jnp.stack([my_owner % near, my_part])
    message = precondition(
        place, taken, landed, (landed_order(left_high), landed_order(left_low), right_high, right_low)
    )
    landed, message = lax.optimization_barrier((landed, message))
    back = exchange(message, ("fsdp", "mp"), plane_groups)
    arrived = exchange(repack(back), "fsdp", far_groups)

    landed = landed.reshape(near, parts, capacity, far, row_share, col_share)
    blocks = landed.transpose(2, 3, 0, 4, 1, 5).reshape(capacity, block_size, block_size)
    top_rows = lax.dynamic_slice_in_dim(blocks, row_start, part_rows, 1)
    my_columns = lax.dynamic_slice_in_dim(blocks, row_start, part_rows, 2)
    left_acc = dot32("skc,sjc->skj", top_rows, blocks)
    right_acc = dot32("sik,sij->skj", my_columns, blocks)
    scaled_gain = (1.0 - decay_rate) / block_size
    filled = (taken > 0)[:, None, None]
    left_new = jnp.where(filled, decay_rate * left_stats + scaled_gain * left_acc, left_stats)
    right_new = jnp.where(filled, decay_rate * right_stats + scaled_gain * right_acc, right_stats)

    cells = near * capacity
    spot = cell_ids // cells * 128 + cell_ids % cells // capacity * 16 + cell_ids % capacity * 3
    across = lambda array: jnp.broadcast_to(array.astype(jnp.int32)[:, None], (block_count, 128))
    update = finish(cell_ids, across(spot), across(up_block), arrived)
    return (update, left_new, right_new)


def solution(mesh):
    placed = (
        P(None, "fsdp", "mp"),
        P(),
        P("fsdp", "mp", None),
        P("fsdp", "mp", None),
        P("fsdp", "mp", None),
        P("fsdp", "mp", None),
    )
    return jax.shard_map(
        on_device,
        mesh=mesh,
        in_specs=placed,
        out_specs=(P(None, "fsdp", "mp"), P("fsdp", "mp", None), P("fsdp", "mp", None)),
        check_vma=False,
    )
```

time: 356 us -> 137 us (0.38)
  blocking collectives: 165 us -> 14.1 us
  waiting for transfers between devices: 130 us -> 48 us
  starting transfers between devices: 16.7 us -> 42.4 us
  between operations: 16.9 us -> 0.91 us
  matrix products: 16.4 us -> 4.03 us
  local copies, waits for them, and re-layouts: 4.71 us -> 16.5 us
  Pallas kernels: 0 us -> 7.89 us
    psum x1 -> x0, blocking collectives: 99.8 us -> none  [on_device(): lax.psum((gate_grad, up_grad, jnp.sum(jnp.where(up_block, 0.0, home_terms...]
    all_gather x2 -> x0, waiting for transfers between devices: 81.9 us -> none  [the longest x1 52.1 us: on_device(): lax.all_gather(halfway, 'mp', axis=2, tiled=True)]
    all_to_all x2 -> x1, blocking collectives: 64.7 us -> 14.1 us  [exchange(): lax.all_to_all(array, axis_name, split_axis=0, concat_axis=0, axis_index_...]
    all_to_all x1 -> x3, waiting for transfers between devices: 48.5 us -> 31.3 us  [exchange(): lax.all_to_all(array, axis_name, split_axis=0, concat_axis=0, axis_index_...]
    ppermute x0 -> x3, waiting for transfers between devices: none -> 16.7 us  [on_device(): lax.ppermute(array, 'mp', [(i, (i + k) % parts) for i in range(parts)])]
    all_to_all x1 -> x3, starting transfers between devices: 16.6 us -> 32 us  [exchange(): lax.all_to_all(array, axis_name, split_axis=0, concat_axis=0, axis_index_...]
    dot_general x5 -> x2, matrix products: 15.2 us -> 2.87 us  [dot32(): return jnp.einsum(spec, a, b, preferred_element_type=jnp.float32)]
    ppermute x0 -> x3, starting transfers between devices: none -> 10.3 us  [on_device(): lax.ppermute(array, 'mp', [(i, (i + k) % parts) for i in range(parts)])]
  transfers between devices with their start and end apart: 3 -> 6, of which waited for: 3 -> 4; matrix products, arithmetic and copies ran while one was open for 2% -> 7% of each run, Pallas kernels for 0% -> 1%
where the time goes in v2:
time: 137 us; the launch traced here: 136 us
  waiting for transfers between devices  48 us (35%)
  starting transfers between devices  42.4 us (31%)
  local copies, waits for them, and re-layouts  16.5 us (12%)
  blocking collectives  14.1 us (10%)
  Pallas kernels  7.89 us (6%)
  matrix products  4.03 us (3%)
  other arithmetic  1.94 us (1%)
    all_to_all x3, starting transfers between devices, exchange(): lax.all_to_all(array, axis_name, split_axis=0, concat_axis=0, axis_index_...  32 us
    all_to_all x3, waiting for transfers between devices, exchange(): lax.all_to_all(array, axis_name, split_axis=0, concat_axis=0, axis_index_...  31.3 us
    ppermute x3, waiting for transfers between devices, on_device(): lax.ppermute(array, 'mp', [(i, (i + k) % parts) for i in range(parts)])  16.7 us
    all_to_all x1, blocking collectives, exchange(): lax.all_to_all(array, axis_name, split_axis=0, concat_axis=0, axis_index_...  14.1 us
    ppermute x3, starting transfers between devices, on_device(): lax.ppermute(array, 'mp', [(i, (i + k) % parts) for i in range(parts)])  10.3 us
    unnamed x24, local copies, waits for them, and re-layouts  7.11 us
    pallas_call x1, Pallas kernels, precondition(): pl.pallas_call(precondition_kernel, grid_spec=pltpu.PrefetchScalarGridSpe...  3.77 us
    reshape x1, local copies, waits for them, and re-layouts, on_device(): landed = landed.reshape(near, parts, capacity, far, row_share, col_share)  3.21 us
  transfers between devices with their start and end apart: 6, of which 4 were waited for; matrix products, arithmetic and copies ran while one was open for 7% of the time, Pallas kernels for 1%

profile of v2, /device:TPU:6, one launch (start us, length us, event | category | flops | bytes accessed | tf_op | source)
XLA Modules:
  0.0 135.8 jit_solution(15887691707570762433)
XLA Ops:
  2.2 1.2 convolution_convert_fusion
  4.3 15.2 %all-to-all-start = ((bf16[16,8,3,4,128]{4,3,2,1,0:T(4,128)(2,1)}), bf16[16,8,3,4,128]{4,3,2,1,0:T(4,128)(2,1)S(1)}, u32[]{:S(2)}, u32[]{:S(2)}) async-start(bf16[16,8,3,4,128]{4,3,2,1,0:T(4,128)(2,1)} %reshape.62), calls=%async_computation | async-start | bytes 786432 | tf_op jit(solution)/shard_map/all_to_all | solution.py:31
  19.7 4.9 %collective-permute-start = (f32[3,128,256]{2,1,0:T(8,128)S(1)}, f32[3,128,256]{2,1,0:T(8,128)S(1)}, u32[]{:S(2)}, u32[]{:S(2)}) collective-permute-start(f32[3,128,256]{2,1,0:T(8,128)S(1)} %get-tuple-element.29), channel_id=1, source_target_pairs={{0,3},{1,0},{2,1},{3,2},{4,7},{5,4},{6,5},{7,6},{8,11},{9,8},{10,9... | collective-permute-start | bytes 1179656 | tf_op jit(solution)/shard_map/ppermute | solution.py:298
  24.6 2.5 %collective-permute-start.1 = (f32[3,128,256]{2,1,0:T(8,128)S(1)}, f32[3,128,256]{2,1,0:T(8,128)S(1)}, u32[]{:S(2)}, u32[]{:S(2)}) collective-permute-start(f32[3,128,256]{2,1,0:T(8,128)S(1)} %get-tuple-element.28), channel_id=1, source_target_pairs={{0,2},{1,3},{2,0},{3,1},{4,6},{5,7},{6,4},{7,5},{8,10},{9,11},{10,... | collective-permute-start | bytes 1179656 | tf_op jit(solution)/shard_map/ppermute | solution.py:298
  27.1 2.9 %collective-permute-start.2 = (f32[3,128,256]{2,1,0:T(8,128)S(1)}, f32[3,128,256]{2,1,0:T(8,128)S(1)}, u32[]{:S(2)}, u32[]{:S(2)}) collective-permute-start(f32[3,128,256]{2,1,0:T(8,128)S(1)} %get-tuple-element.28), channel_id=1, source_target_pairs={{0,1},{1,2},{2,3},{3,0},{4,5},{5,6},{6,7},{7,4},{8,9},{9,10},{10,1... | collective-permute-start | bytes 1179656 | tf_op jit(solution)/shard_map/ppermute | solution.py:298
  30.0 11.1 %collective-permute-done.one_ref = f32[3,128,256]{2,1,0:T(8,128)S(1)} collective-permute-done((f32[3,128,256]{2,1,0:T(8,128)S(1)}, f32[3,128,256]{2,1,0:T(8,128)S(1)}, u32[]{:S(2)}, u32[]{:S(2)}) %collective-permute-start) | collective-permute-done | bytes 393248 | tf_op jit(solution)/shard_map/ppermute | solution.py:298
  41.1 5.6 %collective-permute-done.2.three_ref = f32[3,128,256]{2,1,0:T(8,128)S(1)} collective-permute-done((f32[3,128,256]{2,1,0:T(8,128)S(1)}, f32[3,128,256]{2,1,0:T(8,128)S(1)}, u32[]{:S(2)}, u32[]{:S(2)}) %collective-permute-start.2) | collective-permute-done | bytes 393248 | tf_op jit(solution)/shard_map/ppermute | solution.py:298
  46.9 2.0 %broadcast_in_dim.31 = bf16[8,4,3,16,4,128]{5,4,3,2,1,0:T(4,128)(2,1)} broadcast(bf16[8,3,16,4,128]{4,3,2,1,0:T(4,128)(2,1)S(1)} %copy.14), dimensions={0,2,3,4,5} | broadcast | bytes 1966080 | tf_op jit(solution)/shard_map/broadcast_in_dim | solution.py:304
  48.9 5.2 %all-to-all-start.1 = ((bf16[32,192,128]{2,1,0:T(8,128)(2,1)}), bf16[32,192,128]{2,1,0:T(8,128)(2,1)S(1)}, u32[]{:S(2)}, u32[]{:S(2)}) async-start(bf16[32,192,128]{2,1,0:T(8,128)(2,1)} %bitcast.30), calls=%async_computation.1 | async-start | bytes 3145728 | tf_op jit(solution)/shard_map/all_to_all | solution.py:31
  56.4 1.1 shard_map.85
  57.4 1.1 copy-done.1
  58.6 1.2 copy-done.3
  60.1 14.9 %all-to-all-done.1 = bf16[32,192,128]{2,1,0:T(8,128)(2,1)S(1)} async-done(((bf16[32,192,128]{2,1,0:T(8,128)(2,1)}), bf16[32,192,128]{2,1,0:T(8,128)(2,1)S(1)}, u32[]{:S(2)}, u32[]{:S(2)}) %all-to-all-start.1) | async-done | bytes 1572896 | tf_op jit(solution)/shard_map/all_to_all | solution.py:31
  75.1 1.4 %copy-done.2 = bf16[3,512,512]{2,1,0:T(8,128)(2,1)S(1)} copy-done((bf16[3,512,512]{2,1,0:T(8,128)(2,1)S(1)}, bf16[3,512,512]{2,1,0:T(8,128)(2,1)}, u32[]{:S(2)}) %copy-start.2) | copy-done | bytes 1572888
  76.5 1.4 %copy-done.4 = bf16[3,512,512]{2,1,0:T(8,128)(2,1)S(1)} copy-done((bf16[3,512,512]{2,1,0:T(8,128)(2,1)S(1)}, bf16[3,512,512]{2,1,0:T(8,128)(2,1)}, u32[]{:S(2)}) %copy-start.4) | copy-done | bytes 1572888
  77.9 3.8 %shard_map.86 = s16[32,13,4,128]{3,2,1,0:T(4,128)(2,1)S(1)} custom-call(s32[2]{0:T(128)S(1)} %pad_add_fusion.place_ref, s32[3]{0:T(128)S(1)} %select_reduce_fusion.taken_ref, bf16[8,4,192,128]{3,2,1,0:T(8,128)(2,1)S(1)} %bitcast.23, bf16[3,512,128]{2,1,0:T(8,128)(2,1)S(1)} %bitcast.25, bf16[3,512,128]{2,1,0:T(8,128)(2,1)S(1)} %bitcast.26, ...), custom_call_target="tpu_custom_call" | custom-call | flops 1006632960 | bytes 6291456 | tf_op jit(solution)/shard_map/pallas_call | solution.py:179
  81.7 14.1 %all_to_all.20.back_ref = s16[32,13,4,128]{3,2,1,0:T(4,128)(2,1)S(1)} all-to-all(s16[32,13,4,128]{3,2,1,0:T(4,128)(2,1)S(1)} %shard_map.86), channel_id=1, replica_groups={{0,1,2,3,4,5,6,7,8,9,10,11,12,13,14,15,16,17,18,19,20,21,22,23,24,25,26..., dimensions={0} | all-to-all | bytes 851968 | tf_op jit(solution)/shard_map/all_to_all | solution.py:31
  96.7 11.7 %all-to-all-start.3 = ((s16[16,25,4,128]{3,2,1,0:T(4,128)(2,1)}), s16[16,25,4,128]{3,2,1,0:T(4,128)(2,1)S(1)}, u32[]{:S(2)}, u32[]{:S(2)}) async-start(s16[16,25,4,128]{3,2,1,0:T(4,128)(2,1)} %shard_map.87), calls=%async_computation.3 | async-start | bytes 819200 | tf_op jit(solution)/shard_map/all_to_all | solution.py:31
  108.4 3.2 %copy.26 = bf16[8,4,3,16,4,128]{5,1,4,0,3,2:T(4,128)(2,1)} copy(bf16[8,4,3,16,4,128]{5,4,3,2,1,0:T(4,128)(2,1)S(1)} %bitcast.24) | data formatting | bytes 3145728 | tf_op jit(solution)/shard_map/reshape | solution.py:328
  111.6 2.6 %reshape.70 = bf16[3,512,512]{2,1,0:T(8,128)(2,1)S(1)} reshape(bf16[3,16,8,4,4,128]{5,4,3,2,1,0:T(4,128)(2,1)} %bitcast.29) | data formatting | bytes 3145728 | tf_op jit(solution)/shard_map/reshape | solution.py:329
  114.2 1.5 %fusion.2 = f32[3,128,512]{2,1,0:T(8,128)} fusion(f32[3,128,512]{2,1,0:T(8,128)S(1)} %copy-done.10, bf16[3,512,512]{2,1,0:T(8,128)(2,1)S(1)} %reshape.70, s32[]{:T(128)S(6)} %select_n.82, pred[3]{0:T(512)(128)(4,1)S(1)} %broadcast_compare_fusion), kind=kOutput, calls=%fused_computation.5 | convolution fusion | flops 202113024 | bytes 3539460 | tf_op jit(solution)/shard_map/skc,sjc->skj/dot_general | solution.py:37
  115.8 1.3 fusion.3
  117.1 16.4 %all-to-all-done.3.arrived_ref = s16[16,25,4,128]{3,2,1,0:T(4,128)(2,1)S(1)} async-done(((s16[16,25,4,128]{3,2,1,0:T(4,128)(2,1)}), s16[16,25,4,128]{3,2,1,0:T(4,128)(2,1)S(1)}, u32[]{:S(2)}, u32[]{:S(2)}) %all-to-all-start.3) | async-done | bytes 409632 | tf_op jit(solution)/shard_map/all_to_all | solution.py:31
  133.6 2.2 %shard_map.88 = bf16[128,4,128]{2,1,0:T(4,128)(2,1)} custom-call(s32[128]{0:T(128)S(1)} %get-tuple-element.24.at_ref, s32[128,128]{1,0:T(8,128)S(1)} %broadcast_in_dim.29.spot_ref, s32[128,128]{1,0:T(8,128)S(1)} %broadcast_in_dim.30.up_ref, s16[16,25,4,128]{3,2,1,0:T(4,128)(2,1)S(1)} %all-to-all-done.3.arrived_ref), custom_call_target="tpu_custom_call" | custom-call | bytes 1048576 | tf_op jit(solution)/shard_map/pallas_call | solution.py:260
  (39 shorter events, 6.5 us)
Async XLA Ops:
  0.6 18.9 %copy-start = (f32[3,128,512]{2,1,0:T(8,128)S(1)}, f32[3,128,512]{2,1,0:T(8,128)}, u32[]{:S(2)}) copy-start(f32[3,128,512]{2,1,0:T(8,128)} %own_ref.1) | copy-start | bytes 2359300
  4.3 42.5 %all-to-all-start = ((bf16[16,8,3,4,128]{4,3,2,1,0:T(4,128)(2,1)}), bf16[16,8,3,4,128]{4,3,2,1,0:T(4,128)(2,1)S(1)}, u32[]{:S(2)}, u32[]{:S(2)}) async-start(bf16[16,8,3,4,128]{4,3,2,1,0:T(4,128)(2,1)} %reshape.62), calls=%async_computation | async-start | bytes 786432 | tf_op jit(solution)/shard_map/all_to_all | solution.py:31
  19.7 21.4 %collective-permute-start = (f32[3,128,256]{2,1,0:T(8,128)S(1)}, f32[3,128,256]{2,1,0:T(8,128)S(1)}, u32[]{:S(2)}, u32[]{:S(2)}) collective-permute-start(f32[3,128,256]{2,1,0:T(8,128)S(1)} %get-tuple-element.29), channel_id=1, source_target_pairs={{0,3},{1,0},{2,1},{3,2},{4,7},{5,4},{6,5},{7,6},{8,11},{9,8},{10,9... | collective-permute-start | bytes 1179656 | tf_op jit(solution)/shard_map/ppermute | solution.py:298
  24.6 16.5 %collective-permute-start.1 = (f32[3,128,256]{2,1,0:T(8,128)S(1)}, f32[3,128,256]{2,1,0:T(8,128)S(1)}, u32[]{:S(2)}, u32[]{:S(2)}) collective-permute-start(f32[3,128,256]{2,1,0:T(8,128)S(1)} %get-tuple-element.28), channel_id=1, source_target_pairs={{0,2},{1,3},{2,0},{3,1},{4,6},{5,7},{6,4},{7,5},{8,10},{9,11},{10,... | collective-permute-start | bytes 1179656 | tf_op jit(solution)/shard_map/ppermute | solution.py:298
  27.1 19.6 %collective-permute-start.2 = (f32[3,128,256]{2,1,0:T(8,128)S(1)}, f32[3,128,256]{2,1,0:T(8,128)S(1)}, u32[]{:S(2)}, u32[]{:S(2)}) collective-permute-start(f32[3,128,256]{2,1,0:T(8,128)S(1)} %get-tuple-element.28), channel_id=1, source_target_pairs={{0,1},{1,2},{2,3},{3,0},{4,5},{5,6},{6,7},{7,4},{8,9},{9,10},{10,1... | collective-permute-start | bytes 1179656 | tf_op jit(solution)/shard_map/ppermute | solution.py:298
  41.1 7.8 %copy-start.6 = (f32[3,128,256]{2,1,0:T(8,128)}, f32[3,128,256]{2,1,0:T(8,128)S(1)}, u32[]{:S(2)}) copy-start(f32[3,128,256]{2,1,0:T(8,128)S(1)} %collective-permute-done.1.two_ref) | copy-start | bytes 1179652
  46.7 2.2 %copy-start.8 = (f32[3,128,256]{2,1,0:T(8,128)}, f32[3,128,256]{2,1,0:T(8,128)S(1)}, u32[]{:S(2)}) copy-start(f32[3,128,256]{2,1,0:T(8,128)S(1)} %collective-permute-done.2.three_ref) | copy-start | bytes 1179652
  48.9 5.5 %copy-start.5 = (f32[3,128,512]{2,1,0:T(8,128)S(1)}, f32[3,128,512]{2,1,0:T(8,128)}, u32[]{:S(2)}) copy-start(f32[3,128,512]{2,1,0:T(8,128)} %left_ref.1) | copy-start | bytes 2359300
  48.9 26.2 %all-to-all-start.1 = ((bf16[32,192,128]{2,1,0:T(8,128)(2,1)}), bf16[32,192,128]{2,1,0:T(8,128)(2,1)S(1)}, u32[]{:S(2)}, u32[]{:S(2)}) async-start(bf16[32,192,128]{2,1,0:T(8,128)(2,1)} %bitcast.30), calls=%async_computation.1 | async-start | bytes 3145728 | tf_op jit(solution)/shard_map/all_to_all | solution.py:31
  54.4 1.0 copy-start.7
  55.4 1.0 copy-start.9
  57.4 1.1 copy-start.1
  58.6 1.2 copy-start.3
  75.1 1.4 %copy-start.2 = (bf16[3,512,512]{2,1,0:T(8,128)(2,1)S(1)}, bf16[3,512,512]{2,1,0:T(8,128)(2,1)}, u32[]{:S(2)}) copy-start(bf16[3,512,512]{2,1,0:T(8,128)(2,1)} %copy-done.1) | copy-start | bytes 4718596
  76.5 1.4 %copy-start.4 = (bf16[3,512,512]{2,1,0:T(8,128)(2,1)S(1)}, bf16[3,512,512]{2,1,0:T(8,128)(2,1)}, u32[]{:S(2)}) copy-start(bf16[3,512,512]{2,1,0:T(8,128)(2,1)} %copy-done.3) | copy-start | bytes 4718596
  96.7 36.7 %all-to-all-start.3 = ((s16[16,25,4,128]{3,2,1,0:T(4,128)(2,1)}), s16[16,25,4,128]{3,2,1,0:T(4,128)(2,1)S(1)}, u32[]{:S(2)}, u32[]{:S(2)}) async-start(s16[16,25,4,128]{3,2,1,0:T(4,128)(2,1)} %shard_map.87), calls=%async_computation.3 | async-start | bytes 819200 | tf_op jit(solution)/shard_map/all_to_all | solution.py:31
  111.6 2.6 %copy-start.10 = (f32[3,128,512]{2,1,0:T(8,128)S(1)}, f32[3,128,512]{2,1,0:T(8,128)}, u32[]{:S(2)}) copy-start(f32[3,128,512]{2,1,0:T(8,128)} %param.8) | copy-start | bytes 2359300
  114.2 1.6 %copy-start.11 = (f32[3,128,512]{2,1,0:T(8,128)S(1)}, f32[3,128,512]{2,1,0:T(8,128)}, u32[]{:S(2)}) copy-start(f32[3,128,512]{2,1,0:T(8,128)} %param.9) | copy-start | bytes 2359300

commit v3 on v2

--- a/solution.py
+++ b/solution.py
@@ -42,6 +42,58 @@
     return high, (array - high.astype(jnp.float32)).astype(jnp.bfloat16)
 
 
+def pack_kernel(owner_ref, grad_ref, packed_ref, count_ref):
+    blocks = grad_ref.shape[0]
+    slots = packed_ref.shape[0] // blocks
+    packed_ref[...] = jnp.zeros_like(packed_ref)
+    for owner in range(blocks):
+        count_ref[owner] = 0
+    for b in range(blocks):
+        owner = owner_ref[b]
+        rank = count_ref[owner]
+        count_ref[owner] = rank + 1
+        packed_ref[owner * slots + rank] = grad_ref[b]
+
+
+def pack(owner_map, gradient, slots):
+    blocks = gradient.shape[0]
+    whole = lambda shape: pl.BlockSpec(shape, lambda i, *_: (0,) * len(shape))
+    packed = (blocks * slots,) + gradient.shape[1:]
+    return pl.pallas_call(
+        pack_kernel,
+        grid_spec=pltpu.PrefetchScalarGridSpec(
+            num_scalar_prefetch=1,
+            grid=(1,),
+            in_specs=[whole(gradient.shape)],
+            out_specs=whole(packed),
+            scratch_shapes=[pltpu.SMEM((blocks,), jnp.int32)],
+        ),
+        out_shape=jax.ShapeDtypeStruct(packed, gradient.dtype),
+        compiler_params=pltpu.CompilerParams(vmem_limit_bytes=16 * 1024 * 1024),
+        cost_estimate=pl.CostEstimate(flops=0, bytes_accessed=1 << 20, transcendentals=0),
+    )(owner_map, gradient)
+
+
+def fan_kernel(plane_ref, fan_ref):
+    for n in range(near):
+        for s in range(plane_ref.shape[2]):
+            rows = plane_ref[:, n, s]
+            for m in range(parts):
+                fan_ref[n, m, s] = rows
+
+
+def fan(in_plane):
+    _, _, slots, rows, width = in_plane.shape
+    return pl.pallas_call(
+        fan_kernel,
+        out_shape=jax.ShapeDtypeStruct((near, parts, slots, far, rows, width), in_plane.dtype),
+        in_specs=[pl.BlockSpec(memory_space=pltpu.VMEM)],
+        out_specs=pl.BlockSpec(memory_space=pltpu.VMEM),
+        compiler_params=pltpu.CompilerParams(vmem_limit_bytes=16 * 1024 * 1024),
+        cost_estimate=pl.CostEstimate(flops=0, bytes_accessed=1 << 21, transcendentals=0),
+    )(in_plane)
+
+
 def roots_kernel(
     part_ref, left_ref, own_ref, one_ref, two_ref, three_ref,
     left_high_ref, left_low_ref, right_high_ref, right_low_ref,
@@ -66,9 +118,9 @@
     for step in range(1, parts):
         put_pair(0, step, own_ref[0, :, span(step)])
     put(1, 1, one_ref[0, :, :width])
-    put_pair(1, 3, one_ref[0, :, width:])
-    put(2, 2, two_ref[0, :, :width])
-    put_pair(2, 1, two_ref[0, :, width:])
+    put_pair(1, 3, one_ref[0, :, width : 2 * width])
+    put_pair(1, 2, one_ref[0, :, 2 * width :])
+    put(2, 2, two_ref[0])
     put(3, 3, three_ref[0, :, :width])
     put_pair(3, 2, three_ref[0, :, width:])
     left_high_ref[0], left_low_ref[0] = split_two(left_ref[0].T)
@@ -83,7 +135,7 @@
         grid_spec=pltpu.PrefetchScalarGridSpec(
             num_scalar_prefetch=1,
             grid=(slots,),
-            in_specs=[by_slot(width, order)] * 2 + [by_slot(width, 2 * width)] * 3,
+            in_specs=[by_slot(width, order)] * 2 + [by_slot(width, other.shape[2]) for other in others],
             out_specs=[by_slot(order, width)] * 2 + [by_slot(order, order)] * 2,
         ),
         out_shape=[of(order, width)] * 2 + [of(order, order)] * 2,
@@ -116,6 +168,7 @@
     message_ref, line_ref,
 ):
     slot = pl.program_id(0)
+    slots = taken_ref.shape[0]
     tn = (((0,), (0,)), ((), ()))
     nn = (((1,), (0,)), ((), ()))
     dot = functools.partial(lax.dot_general, preferred_element_type=jnp.float32)
@@ -136,7 +189,7 @@
         for device in range(near):
             for m in range(parts):
                 row = (step * near + device) * deep
-                message_ref[device * parts + m, step * 3 + slot] = code[
+                message_ref[device * parts + m, step * slots + slot] = code[
                     row : row + deep, m * wide_rows : (m + 1) * wide_rows
                 ].astype(jnp.int16)
 
@@ -167,14 +220,14 @@
         tops = jnp.where(in_tops, jnp.where(step == 0, exponent, jnp.where(step == 1, high, low)), 0.0)
         facts = jnp.where(row < 3, sums, tops)[:deep].astype(jnp.int32).astype(jnp.int16)
         for device in range(near * parts):
-            message_ref[device, message_ref.shape[1] - 1] = facts
+            message_ref[device, slots * far // parts] = facts
 
 
 def precondition(place, taken, landed, roots):
     slots, width = taken.shape[0], landed.shape[2]
     rows = landed.shape[1] // slots
     order = near * rows
-    message = (near * parts, slots * far // parts + 1, rows // far, width)
+    message = (near * parts, slots * far // parts + 4, rows // far, width)
     by_slot = lambda *shape: pl.BlockSpec((1,) + shape, lambda s, *_: (s, 0, 0))
     return pl.pallas_call(
         precondition_kernel,
@@ -196,9 +249,9 @@
 
 
 def repack_kernel(back_ref, ahead_ref):
-    cells = ahead_ref.shape[1] - 1
+    cells = ahead_ref.shape[1] - 4
     slots = cells // near
-    last = back_ref.shape[1] - 1
+    last = back_ref.shape[1] - 4
     for m in range(parts):
         for step in range(far // parts):
             for device in range(near):
@@ -216,10 +269,10 @@
 
 
 def repack(back):
-    slots = (back.shape[1] - 1) // (far // parts)
+    slots = (back.shape[1] - 4) // (far // parts)
     return pl.pallas_call(
         repack_kernel,
-        out_shape=jax.ShapeDtypeStruct((far, near * slots + 1) + back.shape[2:], back.dtype),
+        out_shape=jax.ShapeDtypeStruct((far, near * slots + 4) + back.shape[2:], back.dtype),
         in_specs=[pl.BlockSpec(memory_space=pltpu.VMEM)],
         out_specs=pl.BlockSpec(memory_space=pltpu.VMEM),
         compiler_params=pltpu.CompilerParams(vmem_limit_bytes=16 * 1024 * 1024),
@@ -228,7 +281,7 @@
 
 
 def finish_kernel(at_ref, spot_ref, up_ref, arrived_ref, update_ref, factor_ref):
-    cells = arrived_ref.shape[1] - 1
+    cells = arrived_ref.shape[1] - 4
     facts = [arrived_ref[z, cells].astype(jnp.int32).astype(jnp.float32) for z in range(far)]
     row = lambda r: jnp.concatenate([fact[r : r + 1] for fact in facts], axis=0)
     sums = jnp.sum(decoded(row(0), row(1), row(2)), axis=0, keepdims=True)
@@ -273,51 +326,43 @@
 
 
 def on_device(gradient, owner_map, left_stats, right_stats, left_root, right_root):
-    fsdp_size = lax.axis_size("fsdp")
     block_count, row_share, col_share = gradient.shape
     capacity, part_rows, block_size = left_stats.shape
     my_owner = lax.axis_index("fsdp")
     my_part = lax.axis_index("mp")
     row_start = my_part * part_rows
-    cell_count = fsdp_size * capacity
-
-    cell_ids = cell_index(owner_map, capacity)
-    one_hot = cell_ids[None, :] == jnp.arange(cell_count, dtype=jnp.int32)[:, None]
-    flat_grad = gradient.reshape(block_count, row_share * col_share)
-    packed = jnp.dot(
-        one_hot.astype(jnp.bfloat16), flat_grad, preferred_element_type=jnp.float32
-    ).astype(jnp.bfloat16)
-    packed = packed.reshape(far, near, capacity, row_share, col_share)
+
+    packed = pack(owner_map, gradient, capacity).reshape(far, near, capacity, row_share, col_share)
     in_plane = exchange(packed, "fsdp", far_groups)
 
     def column(step):
         start = (my_part + step) % parts * part_rows
         return lax.dynamic_slice_in_dim(right_root, start, part_rows, 2)
 
-    pair = lambda step: jnp.concatenate([column(0), column(step)], axis=2)
+    some = lambda *steps: jnp.concatenate([column(step) for step in steps], axis=2)
     send = lambda array, k: lax.ppermute(array, "mp", [(i, (i + k) % parts) for i in range(parts)])
-    three = send(pair(3), 1)
-    two = send(pair(3), 2)
-    one = send(pair(2), 3)
-    in_plane, one, two, three = lax.optimization_barrier((in_plane, one, two, three))
-
-    fanned = jnp.broadcast_to(
-        in_plane.transpose(1, 2, 0, 3, 4)[:, None], (near, parts, capacity, far, row_share, col_share)
-    ).reshape(near * parts, capacity * far * row_share, col_share)
+    three = send(some(0, 3), 1)
+    two = send(column(0), 2)
+    one = send(some(0, 2, 1), 3)
+    in_plane, one, two, three, owner_map = lax.optimization_barrier((in_plane, one, two, three, owner_map))
+
+    fanned = fan(in_plane).reshape(near * parts, capacity * far * row_share, col_share)
     landed = exchange(fanned, ("fsdp", "mp"), plane_groups)
 
+    cell_ids = cell_index(owner_map, capacity)
     up_block = jnp.arange(block_count, dtype=jnp.int32) >= block_count // 2
     my_cells = my_owner * capacity + jnp.arange(capacity, dtype=jnp.int32)
     holding = cell_ids[None, :] == my_cells[:, None]
     taken = jnp.max(jnp.where(holding, 1 + up_block.astype(jnp.int32)[None, :], 0), axis=1)
 
-    left_high, left_low, right_high, right_low = spread_roots(my_part, left_root, right_root, (one, two, three))
+    left_high, left_low, *right_pair = spread_roots(my_part, left_root, right_root, (one, two, three))
 
     def landed_order(array):
         split = array.reshape(capacity, far, near, row_share, part_rows)
         return jnp.swapaxes(split, 1, 2).reshape(capacity, block_size, part_rows)
 
     place = jnp.stack([my_owner % near, my_part])
+    right_high, right_low = (pltpu.with_memory_space_constraint(x, pltpu.HBM) for x in right_pair)
     message = precondition(
         place, taken, landed, (landed_order(left_high), landed_order(left_low), right_high, right_low)
     )

time: 137 us -> 135 us (0.985)
  Pallas kernels: 7.89 us -> 12.7 us
  local copies, waits for them, and re-layouts: 16.5 us -> 11.7 us
  waiting for transfers between devices: 48 us -> 46.1 us
  starting transfers between devices: 42.4 us -> 44 us
  other arithmetic: 1.94 us -> 0.55 us
    ppermute x3, waiting for transfers between devices: 16.7 us -> 11.6 us  [on_device(): lax.ppermute(array, 'mp', [(i, (i + k) % parts) for i in range(parts)])]
    pallas_call x0 -> x2, Pallas kernels: none -> 3.48 us  [the longest x1 1.89 us: pack(): pl.pallas_call(pack_kernel, grid_spec=pltpu.PrefetchScalarGridSpec(num_sc...]
    all_to_all x3, waiting for transfers between devices: 31.3 us -> 34.5 us  [exchange(): lax.all_to_all(array, axis_name, split_axis=0, concat_axis=0, axis_index_...]
    broadcast_in_dim x1 -> x0, local copies, waits for them, and re-layouts: 1.96 us -> none  [on_device(): jnp.broadcast_to(in_plane.transpose(1, 2, 0, 3, 4)[:, None], (near, parts...]
    unnamed x24 -> x26, local copies, waits for them, and re-layouts: 7.11 us -> 5.3 us
  transfers between devices with their start and end apart: 6 -> 6, of which waited for: 4 -> 5; matrix products, arithmetic and copies ran while one was open for 7% -> 7% of each run, Pallas kernels for 1% -> 1%
where the time goes in v3:
time: 135 us; the launch traced here: 134 us
  waiting for transfers between devices  46.1 us (34%)
  starting transfers between devices  44 us (33%)
  blocking collectives  15 us (11%)
  Pallas kernels  12.7 us (9%)
  local copies, waits for them, and re-layouts  11.7 us (9%)
  matrix products  2.86 us (2%)
    all_to_all x3, waiting for transfers between devices, exchange(): lax.all_to_all(array, axis_name, split_axis=0, concat_axis=0, axis_index_...  34.5 us
    all_to_all x3, starting transfers between devices, exchange(): lax.all_to_all(array, axis_name, split_axis=0, concat_axis=0, axis_index_...  33 us
    all_to_all x1, blocking collectives, exchange(): lax.all_to_all(array, axis_name, split_axis=0, concat_axis=0, axis_index_...  15 us
    ppermute x3, waiting for transfers between devices, on_device(): lax.ppermute(array, 'mp', [(i, (i + k) % parts) for i in range(parts)])  11.6 us
    ppermute x3, starting transfers between devices, on_device(): lax.ppermute(array, 'mp', [(i, (i + k) % parts) for i in range(parts)])  10.9 us
    unnamed x26, local copies, waits for them, and re-layouts  5.3 us
    pallas_call x1, Pallas kernels, precondition(): pl.pallas_call(precondition_kernel, grid_spec=pltpu.PrefetchScalarGridSpe...  5.09 us
    reshape x1, local copies, waits for them, and re-layouts, on_device(): landed = landed.reshape(near, parts, capacity, far, row_share, col_share)  3.21 us
  transfers between devices with their start and end apart: 6, of which 5 were waited for; matrix products, arithmetic and copies ran while one was open for 7% of the time, Pallas kernels for 1%

profile of v3, /device:TPU:6, one launch (start us, length us, event | category | flops | bytes accessed | tf_op | source)
XLA Modules:
  0.0 133.8 jit_solution(10480276097205168327)
XLA Ops:
  0.6 1.0 copy-done.8
  2.3 1.9 %shard_map.85 = bf16[384,4,128]{2,1,0:T(4,128)(2,1)} custom-call(s32[128]{0:T(128)S(1)} %copy-done.9, bf16[128,4,128]{2,1,0:T(4,128)(2,1)S(1)} %copy-done.8), custom_call_target="tpu_custom_call" | custom-call | bytes 1048576 | tf_op jit(solution)/shard_map/pallas_call | solution.py:62
  4.2 15.2 %all-to-all-start = ((bf16[16,8,3,4,128]{4,3,2,1,0:T(4,128)(2,1)}), bf16[16,8,3,4,128]{4,3,2,1,0:T(4,128)(2,1)S(1)}, u32[]{:S(2)}, u32[]{:S(2)}) async-start(bf16[16,8,3,4,128]{4,3,2,1,0:T(4,128)(2,1)} %bitcast), calls=%async_computation | async-start | bytes 786432 | tf_op jit(solution)/shard_map/all_to_all | solution.py:31
  19.6 4.9 %collective-permute-start = (f32[3,128,384]{2,1,0:T(8,128)S(1)}, f32[3,128,384]{2,1,0:T(8,128)S(1)}, u32[]{:S(2)}, u32[]{:S(2)}) collective-permute-start(f32[3,128,384]{2,1,0:T(8,128)S(1)} %pad_maximum_fusion), channel_id=1, source_target_pairs={{0,3},{1,0},{2,1},{3,2},{4,7},{5,4},{6,5},{7,6},{8,11},{9,8},{10,9... | collective-permute-start | bytes 1769480 | tf_op jit(solution)/shard_map/ppermute | solution.py:343
  24.6 1.9 %collective-permute-start.2 = (f32[3,128,256]{2,1,0:T(8,128)S(1)}, f32[3,128,256]{2,1,0:T(8,128)S(1)}, u32[]{:S(2)}, u32[]{:S(2)}) collective-permute-start(f32[3,128,256]{2,1,0:T(8,128)S(1)} %pad_maximum_fusion.1), channel_id=1, source_target_pairs={{0,1},{1,2},{2,3},{3,0},{4,5},{5,6},{6,7},{7,4},{8,9},{9,10},{10,1... | collective-permute-start | bytes 1179656 | tf_op jit(solution)/shard_map/ppermute | solution.py:343
  26.5 4.1 %collective-permute-start.1 = (f32[3,128,128]{2,1,0:T(8,128)S(1)}, f32[3,128,128]{2,1,0:T(8,128)S(1)}, u32[]{:S(2)}, u32[]{:S(2)}) collective-permute-start(f32[3,128,128]{2,1,0:T(8,128)S(1)} %get-tuple-element.30), channel_id=1, source_target_pairs={{0,2},{1,3},{2,0},{3,1},{4,6},{5,7},{6,4},{7,5},{8,10},{9,11},{10,... | collective-permute-start | bytes 589832 | tf_op jit(solution)/shard_map/ppermute | solution.py:343
  30.6 10.7 %collective-permute-done.1.two_ref = f32[3,128,128]{2,1,0:T(8,128)S(1)} collective-permute-done((f32[3,128,128]{2,1,0:T(8,128)S(1)}, f32[3,128,128]{2,1,0:T(8,128)S(1)}, u32[]{:S(2)}, u32[]{:S(2)}) %collective-permute-start.1) | collective-permute-done | bytes 196640 | tf_op jit(solution)/shard_map/ppermute | solution.py:343
  42.2 0.9 all-to-all-done.plane_ref
  43.1 1.6 %shard_map.86 = bf16[8,4,3,16,4,128]{5,4,3,2,1,0:T(4,128)(2,1)} custom-call(bf16[16,8,3,4,128]{4,3,2,1,0:T(4,128)(2,1)S(1)} %all-to-all-done.plane_ref), custom_call_target="tpu_custom_call" | custom-call | bytes 2097152 | tf_op jit(solution)/shard_map/pallas_call | solution.py:87
  44.7 7.7 %all-to-all-start.1 = ((bf16[32,192,128]{2,1,0:T(8,128)(2,1)}), bf16[32,192,128]{2,1,0:T(8,128)(2,1)S(1)}, u32[]{:S(2)}, u32[]{:S(2)}) async-start(bf16[32,192,128]{2,1,0:T(8,128)(2,1)} %bitcast.1), calls=%async_computation.1 | async-start | bytes 3145728 | tf_op jit(solution)/shard_map/all_to_all | solution.py:31
  52.6 1.1 copy-done.5
  53.7 0.9 copy-done.7
  54.6 1.0 shard_map.87
  55.6 1.1 copy-done.2
  58.1 15.4 %all-to-all-done.1 = bf16[32,192,128]{2,1,0:T(8,128)(2,1)S(1)} async-done(((bf16[32,192,128]{2,1,0:T(8,128)(2,1)}), bf16[32,192,128]{2,1,0:T(8,128)(2,1)S(1)}, u32[]{:S(2)}, u32[]{:S(2)}) %all-to-all-start.1) | async-done | bytes 1572896 | tf_op jit(solution)/shard_map/all_to_all | solution.py:31
  73.5 5.1 %shard_map.88 = s16[32,16,4,128]{3,2,1,0:T(4,128)(2,1)S(1)} custom-call(s32[2]{0:T(128)S(1)} %pad_add_fusion.place_ref, s32[3]{0:T(128)S(1)} %select_reduce_fusion.taken_ref, bf16[8,4,192,128]{3,2,1,0:T(8,128)(2,1)S(1)} %bitcast.19, bf16[3,512,128]{2,1,0:T(8,128)(2,1)S(1)} %bitcast.21, bf16[3,512,128]{2,1,0:T(8,128)(2,1)S(1)} %bitcast.22, ...), custom_call_target="tpu_custom_call" | custom-call | flops 1006632960 | bytes 6291456 | tf_op jit(solution)/shard_map/pallas_call | solution.py:232
  78.6 15.0 %all_to_all.20.back_ref = s16[32,16,4,128]{3,2,1,0:T(4,128)(2,1)S(1)} all-to-all(s16[32,16,4,128]{3,2,1,0:T(4,128)(2,1)S(1)} %shard_map.88), channel_id=1, replica_groups={{0,1,2,3,4,5,6,7,8,9,10,11,12,13,14,15,16,17,18,19,20,21,22,23,24,25,26..., dimensions={0} | all-to-all | bytes 1048576 | tf_op jit(solution)/shard_map/all_to_all | solution.py:31
  94.5 10.1 %all-to-all-start.3 = ((s16[16,28,4,128]{3,2,1,0:T(4,128)(2,1)}), s16[16,28,4,128]{3,2,1,0:T(4,128)(2,1)S(1)}, u32[]{:S(2)}, u32[]{:S(2)}) async-start(s16[16,28,4,128]{3,2,1,0:T(4,128)(2,1)} %shard_map.89), calls=%async_computation.3 | async-start | bytes 917504 | tf_op jit(solution)/shard_map/all_to_all | solution.py:31
  104.6 3.2 %copy.19 = bf16[8,4,3,16,4,128]{5,1,4,0,3,2:T(4,128)(2,1)} copy(bf16[8,4,3,16,4,128]{5,4,3,2,1,0:T(4,128)(2,1)S(1)} %bitcast.20) | data formatting | bytes 3145728 | tf_op jit(solution)/shard_map/reshape | solution.py:373
  107.8 2.6 %reshape.65 = bf16[3,512,512]{2,1,0:T(8,128)(2,1)S(1)} reshape(bf16[3,16,8,4,4,128]{5,4,3,2,1,0:T(4,128)(2,1)} %bitcast.25) | data formatting | bytes 3145728 | tf_op jit(solution)/shard_map/reshape | solution.py:374
  110.4 1.5 %fusion.2 = f32[3,128,512]{2,1,0:T(8,128)} fusion(f32[3,128,512]{2,1,0:T(8,128)S(1)} %copy-done.11, bf16[3,512,512]{2,1,0:T(8,128)(2,1)S(1)} %reshape.65, s32[]{:T(128)S(6)} %select_n.88, pred[3]{0:T(512)(128)(4,1)S(1)} %broadcast_compare_fusion), kind=kOutput, calls=%fused_computation.5 | convolution fusion | flops 202113024 | bytes 3539460 | tf_op jit(solution)/shard_map/skc,sjc->skj/dot_general | solution.py:37
  112.0 1.3 fusion.3
  113.3 18.2 %all-to-all-done.3.arrived_ref = s16[16,28,4,128]{3,2,1,0:T(4,128)(2,1)S(1)} async-done(((s16[16,28,4,128]{3,2,1,0:T(4,128)(2,1)}), s16[16,28,4,128]{3,2,1,0:T(4,128)(2,1)S(1)}, u32[]{:S(2)}, u32[]{:S(2)}) %all-to-all-start.3) | async-done | bytes 458784 | tf_op jit(solution)/shard_map/all_to_all | solution.py:31
  131.7 2.2 %shard_map.90 = bf16[128,4,128]{2,1,0:T(4,128)(2,1)} custom-call(s32[128]{0:T(128)S(1)} %get-tuple-element.26.at_ref, s32[128,128]{1,0:T(8,128)S(1)} %broadcast_in_dim.27.spot_ref, s32[128,128]{1,0:T(8,128)S(1)} %broadcast_in_dim.28.up_ref, s16[16,28,4,128]{3,2,1,0:T(4,128)(2,1)S(1)} %all-to-all-done.3.arrived_ref), custom_call_target="tpu_custom_call" | custom-call | bytes 1048576 | tf_op jit(solution)/shard_map/pallas_call | solution.py:313
  (39 shorter events, 4.2 us)
Async XLA Ops:
  0.6 18.8 %copy-start = (f32[3,128,512]{2,1,0:T(8,128)S(1)}, f32[3,128,512]{2,1,0:T(8,128)}, u32[]{:S(2)}) copy-start(f32[3,128,512]{2,1,0:T(8,128)} %own_ref.1) | copy-start | bytes 2359300
  0.6 1.0 copy-start.8
  1.6 0.7 copy-start.9
  4.2 39.0 %all-to-all-start = ((bf16[16,8,3,4,128]{4,3,2,1,0:T(4,128)(2,1)}), bf16[16,8,3,4,128]{4,3,2,1,0:T(4,128)(2,1)S(1)}, u32[]{:S(2)}, u32[]{:S(2)}) async-start(bf16[16,8,3,4,128]{4,3,2,1,0:T(4,128)(2,1)} %bitcast), calls=%async_computation | async-start | bytes 786432 | tf_op jit(solution)/shard_map/all_to_all | solution.py:31
  19.6 22.6 %collective-permute-start = (f32[3,128,384]{2,1,0:T(8,128)S(1)}, f32[3,128,384]{2,1,0:T(8,128)S(1)}, u32[]{:S(2)}, u32[]{:S(2)}) collective-permute-start(f32[3,128,384]{2,1,0:T(8,128)S(1)} %pad_maximum_fusion), channel_id=1, source_target_pairs={{0,3},{1,0},{2,1},{3,2},{4,7},{5,4},{6,5},{7,6},{8,11},{9,8},{10,9... | collective-permute-start | bytes 1769480 | tf_op jit(solution)/shard_map/ppermute | solution.py:343
  24.6 17.6 %collective-permute-start.2 = (f32[3,128,256]{2,1,0:T(8,128)S(1)}, f32[3,128,256]{2,1,0:T(8,128)S(1)}, u32[]{:S(2)}, u32[]{:S(2)}) collective-permute-start(f32[3,128,256]{2,1,0:T(8,128)S(1)} %pad_maximum_fusion.1), channel_id=1, source_target_pairs={{0,1},{1,2},{2,3},{3,0},{4,5},{5,6},{6,7},{7,4},{8,9},{9,10},{10,1... | collective-permute-start | bytes 1179656 | tf_op jit(solution)/shard_map/ppermute | solution.py:343
  26.5 14.8 %collective-permute-start.1 = (f32[3,128,128]{2,1,0:T(8,128)S(1)}, f32[3,128,128]{2,1,0:T(8,128)S(1)}, u32[]{:S(2)}, u32[]{:S(2)}) collective-permute-start(f32[3,128,128]{2,1,0:T(8,128)S(1)} %get-tuple-element.30), channel_id=1, source_target_pairs={{0,2},{1,3},{2,0},{3,1},{4,6},{5,7},{6,4},{7,5},{8,10},{9,11},{10,... | collective-permute-start | bytes 589832 | tf_op jit(solution)/shard_map/ppermute | solution.py:343
  41.3 3.5 %copy-start.6 = (f32[3,128,128]{2,1,0:T(8,128)}, f32[3,128,128]{2,1,0:T(8,128)S(1)}, u32[]{:S(2)}) copy-start(f32[3,128,128]{2,1,0:T(8,128)S(1)} %collective-permute-done.1.two_ref) | copy-start | bytes 589828
  42.2 2.5 %copy-start.4 = (f32[3,128,384]{2,1,0:T(8,128)}, f32[3,128,384]{2,1,0:T(8,128)S(1)}, u32[]{:S(2)}) copy-start(f32[3,128,384]{2,1,0:T(8,128)S(1)} %collective-permute-done.one_ref) | copy-start | bytes 1769476
  44.7 7.9 %copy-start.3 = (f32[3,128,512]{2,1,0:T(8,128)S(1)}, f32[3,128,512]{2,1,0:T(8,128)}, u32[]{:S(2)}) copy-start(f32[3,128,512]{2,1,0:T(8,128)} %left_ref.1) | copy-start | bytes 2359300
  44.7 28.8 %all-to-all-start.1 = ((bf16[32,192,128]{2,1,0:T(8,128)(2,1)}), bf16[32,192,128]{2,1,0:T(8,128)(2,1)S(1)}, u32[]{:S(2)}, u32[]{:S(2)}) async-start(bf16[32,192,128]{2,1,0:T(8,128)(2,1)} %bitcast.1), calls=%async_computation.1 | async-start | bytes 3145728 | tf_op jit(solution)/shard_map/all_to_all | solution.py:31
  52.6 1.1 copy-start.5
  53.6 0.9 copy-start.7
  54.6 2.6 %copy-start.10 = (s32[128]{0:T(128)S(1)}, s32[128]{0:T(128)}, u32[]{:S(2)}) copy-start(s32[128]{0:T(128)} %owner_ref.1) | copy-start | bytes 1540
  55.6 1.2 copy-start.2
  56.8 1.1 copy-start.1
  94.5 37.0 %all-to-all-start.3 = ((s16[16,28,4,128]{3,2,1,0:T(4,128)(2,1)}), s16[16,28,4,128]{3,2,1,0:T(4,128)(2,1)S(1)}, u32[]{:S(2)}, u32[]{:S(2)}) async-start(s16[16,28,4,128]{3,2,1,0:T(4,128)(2,1)} %shard_map.89), calls=%async_computation.3 | async-start | bytes 917504 | tf_op jit(solution)/shard_map/all_to_all | solution.py:31
  107.8 2.6 %copy-start.11 = (f32[3,128,512]{2,1,0:T(8,128)S(1)}, f32[3,128,512]{2,1,0:T(8,128)}, u32[]{:S(2)}) copy-start(f32[3,128,512]{2,1,0:T(8,128)} %param.8) | copy-start | bytes 2359300
  110.4 1.6 %copy-start.12 = (f32[3,128,512]{2,1,0:T(8,128)S(1)}, f32[3,128,512]{2,1,0:T(8,128)}, u32[]{:S(2)}) copy-start(f32[3,128,512]{2,1,0:T(8,128)} %param.9) | copy-start | bytes 2359300

commit v4 on v3

v4 whole, which is shorter than its diff:
```python
import functools

import jax
import jax.numpy as jnp
from jax import lax
from jax.experimental import pallas as pl
from jax.experimental.pallas import tpu as pltpu
from jax.sharding import PartitionSpec as P

decay_rate = 0.95
code_top = 32767.0
parts = 4
near = 8
far = 16


def cell_index(owner_map, capacity):
    total_rows = owner_map.shape[0]
    positions = jnp.arange(total_rows, dtype=jnp.int32)
    same_owner = owner_map[None, :] == owner_map[:, None]
    earlier = positions[None, :] < positions[:, None]
    ranks = jnp.sum((same_owner & earlier).astype(jnp.int32), axis=1)
    return owner_map * capacity + ranks


far_groups = [[z * near + n for z in range(far)] for n in range(near)]
plane_groups = [[(z * near + n) * parts + m for n in range(near) for m in range(parts)] for z in range(far)]


def exchange(array, axis_name, groups):
    return lax.all_to_all(
        array, axis_name, split_axis=0, concat_axis=0, axis_index_groups=groups, tiled=True
    )


def split_two(array):
    high = array.astype(jnp.bfloat16)
    return high, (array - high.astype(jnp.float32)).astype(jnp.bfloat16)


def pack_kernel(owner_ref, grad_ref, packed_ref, count_ref):
    blocks = grad_ref.shape[0]
    slots = packed_ref.shape[0] // blocks
    packed_ref[...] = jnp.zeros_like(packed_ref)
    for owner in range(blocks):
        count_ref[owner] = 0
    for b in range(blocks):
        owner = owner_ref[b]
        rank = count_ref[owner]
        count_ref[owner] = rank + 1
        packed_ref[owner * slots + rank] = grad_ref[b]


def pack(owner_map, gradient, slots):
    blocks = gradient.shape[0]
    packed = (blocks * slots,) + gradient.shape[1:]
    return pl.pallas_call(
        pack_kernel,
        grid_spec=pltpu.PrefetchScalarGridSpec(
            num_scalar_prefetch=1,
            grid=(1,),
            in_specs=[whole(gradient.shape)],
            out_specs=whole(packed),
            scratch_shapes=[pltpu.SMEM((blocks,), jnp.int32)],
        ),
        out_shape=jax.ShapeDtypeStruct(packed, gradient.dtype),
        compiler_params=pltpu.CompilerParams(vmem_limit_bytes=16 * 1024 * 1024),
        cost_estimate=pl.CostEstimate(flops=0, bytes_accessed=1 << 20, transcendentals=0),
    )(owner_map, gradient)


def fan_kernel(plane_ref, fan_ref):
    for n in range(near):
        for slot in range(parts):
            if slot < plane_ref.shape[2]:
                fan_ref[n, slot] = plane_ref[:, n, slot]
            else:
                fan_ref[n, slot] = jnp.zeros(fan_ref.shape[2:], fan_ref.dtype)


def fan(in_plane):
    _, _, slots, rows, width = in_plane.shape
    return pl.pallas_call(
        fan_kernel,
        out_shape=jax.ShapeDtypeStruct((near, parts, far, rows, width), in_plane.dtype),
        in_specs=[pl.BlockSpec(memory_space=pltpu.VMEM)],
        out_specs=pl.BlockSpec(memory_space=pltpu.VMEM),
        compiler_params=pltpu.CompilerParams(vmem_limit_bytes=16 * 1024 * 1024),
        cost_estimate=pl.CostEstimate(flops=0, bytes_accessed=1 << 20, transcendentals=0),
    )(in_plane)


def roots_kernel(
    place_ref, left_ref, right_ref, one_ref, two_ref, three_ref,
    left_high_ref, left_low_ref, right_high_ref, right_low_ref,
):
    part = place_ref[1]
    width = left_ref.shape[1]

    def span(step):
        at = lax.rem(part + step, parts)
        return pl.ds(pl.multiple_of(at * width, width), width)

    def spread(root, own_ref, high_ref, low_ref):
        def put(row, col, block):
            high, low = split_two(block)
            high_ref[span(row), span(col)] = high
            low_ref[span(row), span(col)] = low

        def put_pair(row, col, block):
            put(row, col, block)
            put(col, row, block.T)

        put(0, 0, own_ref[0, :, span(0)])
        for step in range(1, parts):
            put_pair(0, step, own_ref[0, :, span(step)])
        put(1, 1, one_ref[root, :, :width])
        put_pair(1, 3, one_ref[root, :, width : 2 * width])
        put_pair(1, 2, one_ref[root, :, 2 * width :])
        put(2, 2, two_ref[root])
        put(3, 3, three_ref[root, :, :width])
        put_pair(3, 2, three_ref[root, :, width:])

    spread(0, left_ref, left_high_ref, left_low_ref)
    spread(1, right_ref, right_high_ref, right_low_ref)


def whole(shape):
    return pl.BlockSpec(shape, lambda i, *_: (0,) * len(shape))


def spread_roots(place, left_root, right_root, others):
    _, width, order = right_root.shape
    mine = pl.BlockSpec((1, width, order), lambda i, place: (place[2], 0, 0))
    out = jax.ShapeDtypeStruct((order, order), jnp.bfloat16)
    return pl.pallas_call(
        roots_kernel,
        grid_spec=pltpu.PrefetchScalarGridSpec(
            num_scalar_prefetch=1,
            grid=(1,),
            in_specs=[mine, mine] + [whole(other.shape) for other in others],
            out_specs=[whole(out.shape)] * 4,
        ),
        out_shape=[out] * 4,
        compiler_params=pltpu.CompilerParams(vmem_limit_bytes=32 * 1024 * 1024),
        cost_estimate=pl.CostEstimate(flops=0, bytes_accessed=5 << 20, transcendentals=0),
    )(place, left_root, right_root, *others)


def power(exponent):
    half = jnp.floor(exponent * 0.5)
    return jnp.exp2(half), jnp.exp2(exponent - half)


def coded(value):
    value = jnp.maximum(value, 1e-37)
    exponent = jnp.floor(jnp.log2(value)) + 1.0
    one, two = power(-exponent)
    share = value * one * two * 16384.0
    high = jnp.floor(share)
    return exponent, high, jnp.floor((share - high) * 16384.0)


def decoded(exponent, high, low):
    one, two = power(exponent - 14.0)
    return jnp.where(high > 0, (high + low * (1.0 / 16384.0)) * one * two, 0.0)


def square_root_code(value, top):
    root = jnp.sqrt(jnp.abs(value) * (code_top * code_top / top))
    return jnp.round(jnp.where(value < 0, -root, root)).astype(jnp.int32)


tn = (((0,), (0,)), ((), ()))
nn = (((1,), (0,)), ((), ()))
nt = (((1,), (1,)), ((), ()))
dot = functools.partial(lax.dot_general, preferred_element_type=jnp.float32)


def precondition_kernel(
    place_ref, grad_ref, left_high_ref, left_low_ref, right_high_ref, right_low_ref, message_ref
):
    order = left_high_ref.shape[0]
    grad = jnp.concatenate([grad_ref[:, m].reshape(order, -1) for m in range(parts)], axis=1)
    half = dot(left_high_ref[...], grad, tn) + dot(left_low_ref[...], grad, tn)
    half_high, half_low = split_two(half)
    right_high = right_high_ref[...]
    result = dot(half_high, right_high, nn) + dot(half_low, right_high, nn) + dot(half_high, right_low_ref[...], nn)
    taken = place_ref[3]
    result = jnp.where(taken > 0, result, 0.0)
    top = jnp.maximum(jnp.max(jnp.abs(result)), 1e-30)
    code = square_root_code(result, top)
    deep, width = message_ref.shape[2:]
    for z in range(far):
        for device in range(near):
            for m in range(parts):
                row = (z * near + device) * deep
                message_ref[device * parts + m, z] = code[row : row + deep, m * width : (m + 1) * width].astype(
                    jnp.int16
                )

    wide = grad.astype(jnp.float32)
    grad_sum = jnp.where(taken > 0, jnp.sum(wide * wide), 0.0)
    upd_sum = jnp.sum(result * result)
    row = lax.broadcasted_iota(jnp.int32, (8, 128), 0)
    at = lax.broadcasted_iota(jnp.int32, (8, 128), 1) - place_ref[0] * 16
    sum_at = at - place_ref[1] * 4
    top_at = at - place_ref[1] * 3
    is_up = jnp.where(taken > 1, 1, 0)
    exponent, high, low = coded(
        jnp.where(sum_at == is_up, grad_sum, jnp.where(sum_at == 2 + is_up, upd_sum, 0.0))
    )
    in_sums = (sum_at >= 0) & (sum_at < 4)
    sums = jnp.where(in_sums, jnp.where(row == 0, exponent, jnp.where(row == 1, high, low)), 0.0)
    exponent, high, low = coded(jnp.full((8, 128), top))
    in_tops = (top_at >= 0) & (top_at < 3) & (place_ref[1] < parts - 1)
    tops = jnp.where(in_tops, jnp.where(top_at == 0, exponent, jnp.where(top_at == 1, high, low)), 0.0)
    facts = jnp.where(row < 3, sums, tops)[:deep].astype(jnp.int32).astype(jnp.int16)
    for device in range(near * parts):
        message_ref[device, far] = facts


def precondition(place, landed, roots):
    _, rows, width = landed.shape
    order = near * rows
    landed = landed.reshape(near, parts, rows, width)
    message = (near * parts, far + 1, rows // far, width)
    return pl.pallas_call(
        precondition_kernel,
        grid_spec=pltpu.PrefetchScalarGridSpec(
            num_scalar_prefetch=1,
            grid=(1,),
            in_specs=[whole(landed.shape)] + [whole((order, order))] * 4,
            out_specs=whole(message),
        ),
        out_shape=jax.ShapeDtypeStruct(message, jnp.int16),
        compiler_params=pltpu.CompilerParams(vmem_limit_bytes=32 * 1024 * 1024),
        cost_estimate=pl.CostEstimate(flops=10 * order**3, bytes_accessed=4 << 20, transcendentals=0),
    )(place, landed, *roots)


def terms_kernel(place_ref, block_ref, own_ref, one_ref, two_ref, three_ref, term_ref):
    block = block_ref[...]
    out_refs = (own_ref, one_ref, two_ref, three_ref)
    width = own_ref.shape[1] - 16
    row = lax.broadcasted_iota(jnp.int32, (16, block.shape[1]), 0)
    for side in range(2):
        term = dot(block, block, nt if side == 0 else tn)
        top = jnp.maximum(jnp.max(jnp.abs(term)), 1e-30)
        term_ref[...] = square_root_code(term, top)
        exponent, high, low = coded(jnp.full(row.shape, top))
        scale = jnp.where(row == 0, exponent, jnp.where(row == 1, high, low)).astype(jnp.int32).astype(jnp.int16)
        for step in range(parts):
            at = lax.rem(place_ref[1] + step, parts)
            out_refs[step][side, :width] = term_ref[pl.ds(pl.multiple_of(at * width, width), width), :].astype(
                jnp.int16
            )
            out_refs[step][side, width:] = scale


def terms(place, block):
    order = block.shape[0]
    out = jax.ShapeDtypeStruct((2, order // parts + 16, order), jnp.int16)
    return pl.pallas_call(
        terms_kernel,
        grid_spec=pltpu.PrefetchScalarGridSpec(
            num_scalar_prefetch=1,
            grid=(1,),
            in_specs=[whole(block.shape)],
            out_specs=[whole(out.shape)] * parts,
            scratch_shapes=[pltpu.VMEM((order, order), jnp.int32)],
        ),
        out_shape=[out] * parts,
        compiler_params=pltpu.CompilerParams(vmem_limit_bytes=32 * 1024 * 1024),
        cost_estimate=pl.CostEstimate(flops=4 * order**3, bytes_accessed=2 << 20, transcendentals=0),
    )(place, block)


def stats_kernel(place_ref, own_ref, one_ref, two_ref, three_ref, left_ref, right_ref, left_new_ref, right_new_ref):
    slots, width, order = left_ref.shape
    sides = ((left_ref, left_new_ref), (right_ref, right_new_ref))
    for slot in range(slots):
        steps = lax.rem(place_ref[1] + parts - slot, parts)
        taken = place_ref[4 + slot]
        for step, terms_ref in enumerate((own_ref, one_ref, two_ref, three_ref)):

            @pl.when((steps == step) & (taken > 0))
            def _(terms_ref=terms_ref):
                for side, (old_ref, new_ref) in enumerate(sides):
                    code = terms_ref[side, :width].astype(jnp.int32).astype(jnp.float32)
                    scale = terms_ref[side, width:].astype(jnp.int32).astype(jnp.float32)
                    top = decoded(scale[0:1], scale[1:2], scale[2:3])
                    gain = top * ((1.0 - decay_rate) / order / (code_top * code_top))
                    new_ref[slot] = decay_rate * old_ref[slot] + code * jnp.abs(code) * gain

        @pl.when(taken == 0)
        def _():
            for old_ref, new_ref in sides:
                new_ref[slot] = old_ref[slot]


def new_stats(place, coded_terms, left_stats, right_stats):
    out = jax.ShapeDtypeStruct(left_stats.shape, jnp.float32)
    return pl.pallas_call(
        stats_kernel,
        grid_spec=pltpu.PrefetchScalarGridSpec(
            num_scalar_prefetch=1,
            grid=(1,),
            in_specs=[whole(coded_terms[0].shape)] * parts + [whole(out.shape)] * 2,
            out_specs=[whole(out.shape)] * 2,
        ),
        out_shape=[out] * 2,
        compiler_params=pltpu.CompilerParams(vmem_limit_bytes=32 * 1024 * 1024),
        cost_estimate=pl.CostEstimate(flops=0, bytes_accessed=5 << 20, transcendentals=0),
    )(place, *coded_terms, left_stats, right_stats)


def repack_kernel(back_ref, ahead_ref):
    cells = ahead_ref.shape[1] - 1
    slots = cells // near
    for device in range(near):
        for slot in range(slots):
            ahead_ref[:, device * slots + slot] = back_ref[device * parts + slot, :far]
    wide = [back_ref[device, far].astype(jnp.int32) for device in range(near * parts)]
    facts = functools.reduce(jnp.add, wide).astype(jnp.int16)
    for z in range(far):
        ahead_ref[z, cells] = facts


def repack(back, slots):
    return pl.pallas_call(
        repack_kernel,
        out_shape=jax.ShapeDtypeStruct((far, near * slots + 1) + back.shape[2:], back.dtype),
        in_specs=[pl.BlockSpec(memory_space=pltpu.VMEM)],
        out_specs=pl.BlockSpec(memory_space=pltpu.VMEM),
        compiler_params=pltpu.CompilerParams(vmem_limit_bytes=16 * 1024 * 1024),
        cost_estimate=pl.CostEstimate(flops=0, bytes_accessed=1 << 20, transcendentals=0),
    )(back)


def finish_kernel(at_ref, spot_ref, up_ref, arrived_ref, update_ref, factor_ref):
    cells = arrived_ref.shape[1] - 1
    facts = [arrived_ref[z, cells].astype(jnp.int32).astype(jnp.float32) for z in range(far)]
    row = lambda r: jnp.concatenate([fact[r : r + 1] for fact in facts], axis=0)
    sums = jnp.sum(decoded(row(0), row(1), row(2)), axis=0, keepdims=True)
    kind = lax.rem(lax.broadcasted_iota(jnp.int32, sums.shape, 1), 4)
    total = lambda k: jnp.sum(jnp.where(kind == k, sums, 0.0), axis=1, keepdims=True)
    gate_scale = jnp.sqrt(total(0) / total(2))
    up_scale = jnp.sqrt(total(1) / total(3))
    tops = row(3)
    lanes = tops.shape[1]
    steps = decoded(tops, pltpu.roll(tops, lanes - 1, 1), pltpu.roll(tops, lanes - 2, 1))
    steps = steps * (1.0 / (code_top * code_top))
    spot = spot_ref[...]
    lane = lax.broadcasted_iota(jnp.int32, spot.shape, 1)
    mine = jnp.zeros(spot.shape, jnp.float32)
    for z in range(far):
        mine += jnp.where(spot == lane + z * lanes, steps[z : z + 1], 0.0)
    step = jnp.sum(mine, axis=1, keepdims=True)
    factor_ref[...] = jnp.where(up_ref[...] > 0, up_scale, gate_scale) * step

    for b in range(update_ref.shape[0]):
        at = at_ref[b]
        code = arrived_ref[at // cells, lax.rem(at, cells)].astype(jnp.int32).astype(jnp.float32)
        update_ref[b] = (code * jnp.abs(code) * factor_ref[b : b + 1, :]).astype(jnp.bfloat16)


def finish(cell_ids, spot, up, arrived):
    blocks = cell_ids.shape[0]
    return pl.pallas_call(
        finish_kernel,
        grid_spec=pltpu.PrefetchScalarGridSpec(
            num_scalar_prefetch=1,
            grid=(1,),
            in_specs=[whole(spot.shape), whole(up.shape), whole(arrived.shape)],
            out_specs=whole((blocks,) + arrived.shape[2:]),
            scratch_shapes=[pltpu.VMEM((blocks, arrived.shape[3]), jnp.float32)],
        ),
        out_shape=jax.ShapeDtypeStruct((blocks,) + arrived.shape[2:], jnp.bfloat16),
        compiler_params=pltpu.CompilerParams(vmem_limit_bytes=16 * 1024 * 1024),
        cost_estimate=pl.CostEstimate(flops=0, bytes_accessed=1 << 20, transcendentals=0),
    )(cell_ids, spot, up, arrived)


def on_device(gradient, owner_map, left_stats, right_stats, left_root, right_root):
    block_count, row_share, col_share = gradient.shape
    capacity, part_rows, block_size = left_stats.shape
    my_owner = lax.axis_index("fsdp")
    my_part = lax.axis_index("mp")

    packed = pack(owner_map, gradient, capacity).reshape(far, near, capacity, row_share, col_share)
    in_plane = exchange(packed, "fsdp", far_groups)

    def send(steps, k):
        slot = jnp.minimum((my_part + k) % parts, capacity - 1)

        def column(root, step):
            start = (my_part + step) % parts * part_rows
            return lax.dynamic_slice(root, (slot, 0, start), (1, part_rows, part_rows))

        rows = [jnp.concatenate([column(root, step) for step in steps], axis=2) for root in (left_root, right_root)]
        pairs = [(i, (i + k) % parts) for i in range(parts)]
        return lax.ppermute(jnp.concatenate(rows, axis=0), "mp", pairs)

    three = send((0, 3), 1)
    two = send((0,), 2)
    one = send((0, 2, 1), 3)
    in_plane, one, two, three, owner_map = lax.optimization_barrier((in_plane, one, two, three, owner_map))

    fanned = fan(in_plane).reshape(near * parts, far * row_share, col_share)
    landed = exchange(fanned, ("fsdp", "mp"), plane_groups)

    cell_ids = cell_index(owner_map, capacity)
    up_block = jnp.arange(block_count, dtype=jnp.int32) >= block_count // 2
    my_cells = my_owner * capacity + jnp.arange(capacity, dtype=jnp.int32)
    holding = cell_ids[None, :] == my_cells[:, None]
    taken = jnp.max(jnp.where(holding, 1 + up_block.astype(jnp.int32)[None, :], 0), axis=1)
    my_slot = jnp.minimum(my_part, capacity - 1)
    my_taken = jnp.where(my_part < capacity, taken[my_slot], 0)
    place = jnp.concatenate([jnp.stack([my_owner % near, my_part, my_slot, my_taken]), taken])

    roots = spread_roots(place, left_root, right_root, (one, two, three))

    def landed_order(array):
        split = array.reshape(far, near, row_share, block_size)
        return jnp.swapaxes(split, 0, 1).reshape(block_size, block_size)

    roots = (landed_order(roots[0]), landed_order(roots[1]), roots[2], roots[3])
    message = precondition(place, landed, roots)
    landed, message = lax.optimization_barrier((landed, message))
    back = exchange(message, ("fsdp", "mp"), plane_groups)
    arrived = exchange(repack(back, capacity), "fsdp", far_groups)

    block = landed.reshape(near, parts, far, row_share, col_share).transpose(2, 0, 3, 1, 4)
    own_terms, *other_terms = terms(place, block.reshape(block_size, block_size))
    coded_terms = [own_terms]
    for k, other in enumerate(other_terms, 1):
        coded_terms.append(lax.ppermute(other, "mp", [(i, (i + k) % parts) for i in range(parts)]))
    left_new, right_new = new_stats(place, coded_terms, left_stats, right_stats)

    cells = near * capacity
    spot = cell_ids // cells * 128 + cell_ids % cells // capacity * 16 + cell_ids % capacity * 3
    across = lambda array: jnp.broadcast_to(array.astype(jnp.int32)[:, None], (block_count, 128))
    update = finish(cell_ids, across(spot), across(up_block), arrived)
    return (update, left_new, right_new)


def solution(mesh):
    placed = (
        P(None, "fsdp", "mp"),
        P(),
        P("fsdp", "mp", None),
        P("fsdp", "mp", None),
        P("fsdp", "mp", None),
        P("fsdp", "mp", None),
    )
    return jax.shard_map(
        on_device,
        mesh=mesh,
        in_specs=placed,
        out_specs=(P(None, "fsdp", "mp"), P("fsdp", "mp", None), P("fsdp", "mp", None)),
        check_vma=False,
    )
```

time: 135 us -> 119 us (0.88)
  waiting for transfers between devices: 46.1 us -> 21.7 us
  starting transfers between devices: 44 us -> 49.6 us
  matrix products: 2.86 us -> 0 us
  blocking collectives: 15 us -> 17.1 us
  Pallas kernels: 12.7 us -> 14.7 us
    all_to_all x3, waiting for transfers between devices: 34.5 us -> 4.19 us  [exchange(): lax.all_to_all(array, axis_name, split_axis=0, concat_axis=0, axis_index_...]
    ppermute x3 -> x6, starting transfers between devices: 10.9 us -> 20.8 us  [the longest x3 10.9 us: send(): return lax.ppermute(jnp.concatenate(rows, axis=0), 'mp', pairs)]
    ppermute x3 -> x6, waiting for transfers between devices: 11.6 us -> 17.5 us  [the longest x3 10.8 us: on_device(): lax.ppermute(other, 'mp', [(i, (i + k) % parts) for i in range(parts)])]
    all_to_all x3, starting transfers between devices: 33 us -> 28.8 us  [exchange(): lax.all_to_all(array, axis_name, split_axis=0, concat_axis=0, axis_index_...]
    pallas_call x1 -> x3, Pallas kernels: 1.58 us -> 5.6 us  [the longest x1 2.57 us: terms(): pl.pallas_call(terms_kernel, grid_spec=pltpu.PrefetchScalarGridSpec(num_s...]
    reshape x4 -> x6, local copies, waits for them, and re-layouts: 6.17 us -> 2.81 us  [the longest x4 1.43 us: landed_order(): split = array.reshape(far, near, row_share, block_size)]
    dot_general x2 -> x0, matrix products: 2.86 us -> none  [dot32(): return jnp.einsum(spec, a, b, preferred_element_type=jnp.float32)]
    all_to_all x1, blocking collectives: 15 us -> 17.1 us  [exchange(): lax.all_to_all(array, axis_name, split_axis=0, concat_axis=0, axis_index_...]
  transfers between devices with their start and end apart: 6 -> 9, of which waited for: 5 -> 5; matrix products, arithmetic and copies ran while one was open for 7% -> 6% of each run, Pallas kernels for 1% -> 5%
where the time goes in v4:
time: 119 us; the launch traced here: 117 us
  starting transfers between devices  49.6 us (42%)
  waiting for transfers between devices  21.7 us (18%)
  blocking collectives  17.1 us (14%)
  Pallas kernels  14.7 us (12%)
  local copies, waits for them, and re-layouts  11.3 us (9%)
  between operations  1.63 us (1%)
    all_to_all x3, starting transfers between devices, exchange(): lax.all_to_all(array, axis_name, split_axis=0, concat_axis=0, axis_index_...  28.8 us
    all_to_all x1, blocking collectives, exchange(): lax.all_to_all(array, axis_name, split_axis=0, concat_axis=0, axis_index_...  17.1 us
    ppermute x3, starting transfers between devices, send(): return lax.ppermute(jnp.concatenate(rows, axis=0), 'mp', pairs)  10.9 us
    ppermute x3, waiting for transfers between devices, on_device(): lax.ppermute(other, 'mp', [(i, (i + k) % parts) for i in range(parts)])  10.8 us
    ppermute x3, starting transfers between devices, on_device(): lax.ppermute(other, 'mp', [(i, (i + k) % parts) for i in range(parts)])  9.88 us
    ppermute x3, waiting for transfers between devices, send(): return lax.ppermute(jnp.concatenate(rows, axis=0), 'mp', pairs)  6.68 us
    unnamed x31, local copies, waits for them, and re-layouts  5.91 us
    all_to_all x3, waiting for transfers between devices, exchange(): lax.all_to_all(array, axis_name, split_axis=0, concat_axis=0, axis_index_...  4.19 us
  transfers between devices with their start and end apart: 9, of which 5 were waited for; matrix products, arithmetic and copies ran while one was open for 6% of the time, Pallas kernels for 5%

profile of v4, /device:TPU:6, one launch (start us, length us, event | category | flops | bytes accessed | tf_op | source)
XLA Modules:
  0.0 117.2 jit_solution(1750327492975170708)
XLA Ops:
  0.6 1.0 copy-done.6
  2.3 1.9 %shard_map.85 = bf16[384,4,128]{2,1,0:T(4,128)(2,1)} custom-call(s32[128]{0:T(128)S(1)} %copy-done.9, bf16[128,4,128]{2,1,0:T(4,128)(2,1)S(1)} %copy-done.6), custom_call_target="tpu_custom_call" | custom-call | bytes 1048576 | tf_op jit(solution)/shard_map/pallas_call | solution.py:57
  4.2 15.2 %all-to-all-start = ((bf16[16,8,3,4,128]{4,3,2,1,0:T(4,128)(2,1)}), bf16[16,8,3,4,128]{4,3,2,1,0:T(4,128)(2,1)S(1)}, u32[]{:S(2)}, u32[]{:S(2)}) async-start(bf16[16,8,3,4,128]{4,3,2,1,0:T(4,128)(2,1)} %bitcast), calls=%async_computation | async-start | bytes 786432 | tf_op jit(solution)/shard_map/all_to_all | solution.py:31
  19.5 1.1 constant_dynamic-slice_fusion.1
  20.6 4.9 %collective-permute-start = (f32[2,128,384]{2,1,0:T(8,128)S(1)}, f32[2,128,384]{2,1,0:T(8,128)S(1)}, u32[]{:S(2)}, u32[]{:S(2)}) collective-permute-start(f32[2,128,384]{2,1,0:T(8,128)S(1)} %maximum_maximum_fusion), channel_id=1, source_target_pairs={{0,3},{1,0},{2,1},{3,2},{4,7},{5,4},{6,5},{7,6},{8,11},{9,8},{10,9... | collective-permute-start | bytes 1179656 | tf_op jit(solution)/shard_map/ppermute | solution.py:403
  25.6 1.9 %collective-permute-start.2 = (f32[2,128,256]{2,1,0:T(8,128)S(1)}, f32[2,128,256]{2,1,0:T(8,128)S(1)}, u32[]{:S(2)}, u32[]{:S(2)}) collective-permute-start(f32[2,128,256]{2,1,0:T(8,128)S(1)} %maximum_maximum_fusion.1), channel_id=1, source_target_pairs={{0,1},{1,2},{2,3},{3,0},{4,5},{5,6},{6,7},{7,4},{8,9},{9,10},{10,1... | collective-permute-start | bytes 786440 | tf_op jit(solution)/shard_map/ppermute | solution.py:403
  28.1 4.1 %collective-permute-start.1 = (f32[2,128,128]{2,1,0:T(8,128)}, f32[2,128,128]{2,1,0:T(8,128)S(1)}, u32[]{:S(2)}, u32[]{:S(2)}) collective-permute-start(f32[2,128,128]{2,1,0:T(8,128)} %pad_maximum_fusion), channel_id=1, source_target_pairs={{0,2},{1,3},{2,0},{3,1},{4,6},{5,7},{6,4},{7,5},{8,10},{9,11},{10,... | collective-permute-start | bytes 393224 | tf_op jit(solution)/shard_map/ppermute | solution.py:403
  32.3 5.8 %collective-permute-done.1.two_ref = f32[2,128,128]{2,1,0:T(8,128)S(1)} collective-permute-done((f32[2,128,128]{2,1,0:T(8,128)}, f32[2,128,128]{2,1,0:T(8,128)S(1)}, u32[]{:S(2)}, u32[]{:S(2)}) %collective-permute-start.1) | collective-permute-done | bytes 131104 | tf_op jit(solution)/shard_map/ppermute | solution.py:403
  39.0 4.2 %all-to-all-done.plane_ref = bf16[16,8,3,4,128]{4,3,2,1,0:T(4,128)(2,1)S(1)} async-done(((bf16[16,8,3,4,128]{4,3,2,1,0:T(4,128)(2,1)}), bf16[16,8,3,4,128]{4,3,2,1,0:T(4,128)(2,1)S(1)}, u32[]{:S(2)}, u32[]{:S(2)}) %all-to-all-start) | async-done | bytes 393248 | tf_op jit(solution)/shard_map/all_to_all | solution.py:31
  44.1 7.6 %all-to-all-start.1 = ((bf16[32,64,128]{2,1,0:T(8,128)(2,1)}), bf16[32,64,128]{2,1,0:T(8,128)(2,1)S(1)}, u32[]{:S(2)}, u32[]{:S(2)}) async-start(bf16[32,64,128]{2,1,0:T(8,128)(2,1)} %bitcast.1), calls=%async_computation.1 | async-start | bytes 1048576 | tf_op jit(solution)/shard_map/all_to_all | solution.py:31
  56.0 1.0 shard_map.87
  59.2 1.0 copy.22
  60.2 1.3 %reshape.59.left_low_ref = bf16[512,512]{1,0:T(8,128)(2,1)S(1)} reshape(bf16[8,16,4,512]{3,2,1,0:T(4,128)(2,1)} %bitcast.26) | data formatting | bytes 1048576 | tf_op jit(solution)/shard_map/reshape | solution.py:426
  61.5 3.1 %shard_map.88 = s16[32,17,4,128]{3,2,1,0:T(4,128)(2,1)S(1)} custom-call(s32[7]{0:T(128)S(1)} %concatenate.31.place_ref, bf16[8,4,64,128]{3,2,1,0:T(8,128)(2,1)S(1)} %bitcast.22, bf16[512,512]{1,0:T(8,128)(2,1)S(1)} %reshape.57.left_high_ref, bf16[512,512]{1,0:T(8,128)(2,1)S(1)} %reshape.59.left_low_ref, bf16[512,512]{1,0:T(8,128)(2,1)S(1)} %copy-done.12, ...), custom_call_target="tpu_custom_call" | custom-call | flops 1342177280 | bytes 4194304 | tf_op jit(solution)/shard_map/pallas_call | solution.py:228
  64.6 17.1 %all_to_all.20.back_ref = s16[32,17,4,128]{3,2,1,0:T(4,128)(2,1)S(1)} all-to-all(s16[32,17,4,128]{3,2,1,0:T(4,128)(2,1)S(1)} %shard_map.88), channel_id=1, replica_groups={{0,1,2,3,4,5,6,7,8,9,10,11,12,13,14,15,16,17,18,19,20,21,22,23,24,25,26..., dimensions={0} | all-to-all | bytes 1114112 | tf_op jit(solution)/shard_map/all_to_all | solution.py:31
  82.7 6.0 %all-to-all-start.3 = ((s16[16,25,4,128]{3,2,1,0:T(4,128)(2,1)}), s16[16,25,4,128]{3,2,1,0:T(4,128)(2,1)S(1)}, u32[]{:S(2)}, u32[]{:S(2)}) async-start(s16[16,25,4,128]{3,2,1,0:T(4,128)(2,1)} %shard_map.89), calls=%async_computation.3 | async-start | bytes 819200 | tf_op jit(solution)/shard_map/all_to_all | solution.py:31
  89.5 2.6 %shard_map.91 = (s16[2,144,512]{2,1,0:T(8,128)(2,1)S(1)}, s16[2,144,512]{2,1,0:T(8,128)(2,1)S(1)}, s16[2,144,512]{2,1,0:T(8,128)(2,1)S(1)}, s16[2,144,512]{2,1,0:T(8,128)(2,1)S(1)}) custom-call(s32[7]{0:T(128)S(1)} %concatenate.31.place_ref, bf16[512,512]{1,0:T(8,128)(2,1)S(1)} %bitcast.24), custom_call_target="tpu_custom_call" | custom-call | flops 536870912 | bytes 2097152 | tf_op jit(solution)/shard_map/pallas_call | solution.py:264
  92.0 2.3 %collective-permute-start.3 = (s16[2,144,512]{2,1,0:T(8,128)(2,1)S(1)}, s16[2,144,512]{2,1,0:T(8,128)(2,1)S(1)}, u32[]{:S(2)}, u32[]{:S(2)}) collective-permute-start(s16[2,144,512]{2,1,0:T(8,128)(2,1)S(1)} %get-tuple-element.32), channel_id=1, source_target_pairs={{0,1},{1,2},{2,3},{3,0},{4,5},{5,6},{6,7},{7,4},{8,9},{9,10},{10,1... | collective-permute-start | bytes 884744 | tf_op jit(solution)/shard_map/ppermute | solution.py:438
  94.4 4.4 %collective-permute-start.4 = (s16[2,144,512]{2,1,0:T(8,128)(2,1)S(1)}, s16[2,144,512]{2,1,0:T(8,128)(2,1)S(1)}, u32[]{:S(2)}, u32[]{:S(2)}) collective-permute-start(s16[2,144,512]{2,1,0:T(8,128)(2,1)S(1)} %get-tuple-element.33), channel_id=1, source_target_pairs={{0,2},{1,3},{2,0},{3,1},{4,6},{5,7},{6,4},{7,5},{8,10},{9,11},{10,... | collective-permute-start | bytes 884744 | tf_op jit(solution)/shard_map/ppermute | solution.py:438
  98.8 3.1 %collective-permute-start.5 = (s16[2,144,512]{2,1,0:T(8,128)(2,1)S(1)}, s16[2,144,512]{2,1,0:T(8,128)(2,1)S(1)}, u32[]{:S(2)}, u32[]{:S(2)}) collective-permute-start(s16[2,144,512]{2,1,0:T(8,128)(2,1)S(1)} %get-tuple-element.34), channel_id=1, source_target_pairs={{0,3},{1,0},{2,1},{3,2},{4,7},{5,4},{6,5},{7,6},{8,11},{9,8},{10,9... | collective-permute-start | bytes 884744 | tf_op jit(solution)/shard_map/ppermute | solution.py:438
  102.0 8.3 %collective-permute-done.3.one_ref = s16[2,144,512]{2,1,0:T(8,128)(2,1)S(1)} collective-permute-done((s16[2,144,512]{2,1,0:T(8,128)(2,1)S(1)}, s16[2,144,512]{2,1,0:T(8,128)(2,1)S(1)}, u32[]{:S(2)}, u32[]{:S(2)}) %collective-permute-start.3) | collective-permute-done | bytes 294944 | tf_op jit(solution)/shard_map/ppermute | solution.py:438
  110.2 2.5 %collective-permute-done.5.three_ref = s16[2,144,512]{2,1,0:T(8,128)(2,1)S(1)} collective-permute-done((s16[2,144,512]{2,1,0:T(8,128)(2,1)S(1)}, s16[2,144,512]{2,1,0:T(8,128)(2,1)S(1)}, u32[]{:S(2)}, u32[]{:S(2)}) %collective-permute-start.5) | collective-permute-done | bytes 294944 | tf_op jit(solution)/shard_map/ppermute | solution.py:438
  112.8 2.1 %shard_map.92 = (f32[3,128,512]{2,1,0:T(8,128)}, f32[3,128,512]{2,1,0:T(8,128)}) custom-call(s32[7]{0:T(128)S(1)} %concatenate.31.place_ref, s16[2,144,512]{2,1,0:T(8,128)(2,1)S(1)} %get-tuple-element.31.own_ref, s16[2,144,512]{2,1,0:T(8,128)(2,1)S(1)} %collective-permute-done.3.one_ref, s16[2,144,512]{2,1,0:T(8,128)(2,1)S(1)} %collective-permute-done.4.two_ref, ...), custom_call_target="tpu_custom_call" | custom-call | bytes 5242880 | tf_op jit(solution)/shard_map/pallas_call | solution.py:304
  115.0 2.2 %shard_map.90 = bf16[128,4,128]{2,1,0:T(4,128)(2,1)} custom-call(s32[128]{0:T(128)S(1)} %get-tuple-element.38.at_ref, s32[128,128]{1,0:T(8,128)S(1)} %broadcast_in_dim.16.spot_ref, s32[128,128]{1,0:T(8,128)S(1)} %broadcast_in_dim.17.up_ref, s16[16,25,4,128]{3,2,1,0:T(4,128)(2,1)S(1)} %all-to-all-done.3.arrived_ref), custom_call_target="tpu_custom_call" | custom-call | bytes 1048576 | tf_op jit(solution)/shard_map/pallas_call | solution.py:370
  (55 shorter events, 11.0 us)
Async XLA Ops:
  0.6 18.8 %copy-start = (f32[3,128,512]{2,1,0:T(8,128)S(1)}, f32[3,128,512]{2,1,0:T(8,128)}, u32[]{:S(2)}) copy-start(f32[3,128,512]{2,1,0:T(8,128)} %left_ref.2) | copy-start | bytes 2359300
  0.6 1.0 copy-start.6
  1.6 0.7 copy-start.9
  4.2 39.0 %all-to-all-start = ((bf16[16,8,3,4,128]{4,3,2,1,0:T(4,128)(2,1)}), bf16[16,8,3,4,128]{4,3,2,1,0:T(4,128)(2,1)S(1)}, u32[]{:S(2)}, u32[]{:S(2)}) async-start(bf16[16,8,3,4,128]{4,3,2,1,0:T(4,128)(2,1)} %bitcast), calls=%async_computation | async-start | bytes 786432 | tf_op jit(solution)/shard_map/all_to_all | solution.py:31
  20.6 18.4 %collective-permute-start = (f32[2,128,384]{2,1,0:T(8,128)S(1)}, f32[2,128,384]{2,1,0:T(8,128)S(1)}, u32[]{:S(2)}, u32[]{:S(2)}) collective-permute-start(f32[2,128,384]{2,1,0:T(8,128)S(1)} %maximum_maximum_fusion), channel_id=1, source_target_pairs={{0,3},{1,0},{2,1},{3,2},{4,7},{5,4},{6,5},{7,6},{8,11},{9,8},{10,9... | collective-permute-start | bytes 1179656 | tf_op jit(solution)/shard_map/ppermute | solution.py:403
  25.6 13.4 %collective-permute-start.2 = (f32[2,128,256]{2,1,0:T(8,128)S(1)}, f32[2,128,256]{2,1,0:T(8,128)S(1)}, u32[]{:S(2)}, u32[]{:S(2)}) collective-permute-start(f32[2,128,256]{2,1,0:T(8,128)S(1)} %maximum_maximum_fusion.1), channel_id=1, source_target_pairs={{0,1},{1,2},{2,3},{3,0},{4,5},{5,6},{6,7},{7,4},{8,9},{9,10},{10,1... | collective-permute-start | bytes 786440 | tf_op jit(solution)/shard_map/ppermute | solution.py:403
  28.1 9.9 %collective-permute-start.1 = (f32[2,128,128]{2,1,0:T(8,128)}, f32[2,128,128]{2,1,0:T(8,128)S(1)}, u32[]{:S(2)}, u32[]{:S(2)}) collective-permute-start(f32[2,128,128]{2,1,0:T(8,128)} %pad_maximum_fusion), channel_id=1, source_target_pairs={{0,2},{1,3},{2,0},{3,1},{4,6},{5,7},{6,4},{7,5},{8,10},{9,11},{10,... | collective-permute-start | bytes 393224 | tf_op jit(solution)/shard_map/ppermute | solution.py:403
  32.3 21.9 %copy-start.1 = (f32[3,128,512]{2,1,0:T(8,128)S(1)}, f32[3,128,512]{2,1,0:T(8,128)}, u32[]{:S(2)}) copy-start(f32[3,128,512]{2,1,0:T(8,128)} %right_ref.2) | copy-start | bytes 2359300
  38.0 6.1 %copy-start.7 = (f32[2,128,128]{2,1,0:T(8,128)}, f32[2,128,128]{2,1,0:T(8,128)S(1)}, u32[]{:S(2)}) copy-start(f32[2,128,128]{2,1,0:T(8,128)S(1)} %collective-permute-done.1.two_ref) | copy-start | bytes 393220
  39.0 5.1 %copy-start.4 = (f32[2,128,256]{2,1,0:T(8,128)}, f32[2,128,256]{2,1,0:T(8,128)S(1)}, u32[]{:S(2)}) copy-start(f32[2,128,256]{2,1,0:T(8,128)S(1)} %collective-permute-done.2.three_ref) | copy-start | bytes 786436
  44.1 17.4 %all-to-all-start.1 = ((bf16[32,64,128]{2,1,0:T(8,128)(2,1)}), bf16[32,64,128]{2,1,0:T(8,128)(2,1)S(1)}, u32[]{:S(2)}, u32[]{:S(2)}) async-start(bf16[32,64,128]{2,1,0:T(8,128)(2,1)} %bitcast.1), calls=%async_computation.1 | async-start | bytes 1048576 | tf_op jit(solution)/shard_map/all_to_all | solution.py:31
  51.7 0.7 copy-start.10
  54.1 1.0 copy-start.5
  55.1 0.9 copy-start.8
  57.0 0.8 copy-start.11
  57.8 0.8 copy-start.13
  60.2 1.3 %copy-start.12 = (bf16[512,512]{1,0:T(8,128)(2,1)S(1)}, bf16[512,512]{1,0:T(8,128)(2,1)}, u32[]{:S(2)}) copy-start(bf16[512,512]{1,0:T(8,128)(2,1)} %copy-done.11) | copy-start | bytes 1572868
  60.2 1.4 %copy-start.14 = (bf16[512,512]{1,0:T(8,128)(2,1)S(1)}, bf16[512,512]{1,0:T(8,128)(2,1)}, u32[]{:S(2)}) copy-start(bf16[512,512]{1,0:T(8,128)(2,1)} %copy-done.13) | copy-start | bytes 1572868
  82.7 32.2 %all-to-all-start.3 = ((s16[16,25,4,128]{3,2,1,0:T(4,128)(2,1)}), s16[16,25,4,128]{3,2,1,0:T(4,128)(2,1)S(1)}, u32[]{:S(2)}, u32[]{:S(2)}) async-start(s16[16,25,4,128]{3,2,1,0:T(4,128)(2,1)} %shard_map.89), calls=%async_computation.3 | async-start | bytes 819200 | tf_op jit(solution)/shard_map/all_to_all | solution.py:31
  89.4 23.3 %copy-start.2 = (f32[3,128,512]{2,1,0:T(8,128)S(1)}, f32[3,128,512]{2,1,0:T(8,128)}, u32[]{:S(2)}) copy-start(f32[3,128,512]{2,1,0:T(8,128)} %left_ref.3) | copy-start | bytes 2359300
  89.5 23.3 %copy-start.3 = (f32[3,128,512]{2,1,0:T(8,128)S(1)}, f32[3,128,512]{2,1,0:T(8,128)}, u32[]{:S(2)}) copy-start(f32[3,128,512]{2,1,0:T(8,128)} %right_ref.3) | copy-start | bytes 2359300
  92.0 18.2 %collective-permute-start.3 = (s16[2,144,512]{2,1,0:T(8,128)(2,1)S(1)}, s16[2,144,512]{2,1,0:T(8,128)(2,1)S(1)}, u32[]{:S(2)}, u32[]{:S(2)}) collective-permute-start(s16[2,144,512]{2,1,0:T(8,128)(2,1)S(1)} %get-tuple-element.32), channel_id=1, source_target_pairs={{0,1},{1,2},{2,3},{3,0},{4,5},{5,6},{6,7},{7,4},{8,9},{9,10},{10,1... | collective-permute-start | bytes 884744 | tf_op jit(solution)/shard_map/ppermute | solution.py:438
  94.4 15.8 %collective-permute-start.4 = (s16[2,144,512]{2,1,0:T(8,128)(2,1)S(1)}, s16[2,144,512]{2,1,0:T(8,128)(2,1)S(1)}, u32[]{:S(2)}, u32[]{:S(2)}) collective-permute-start(s16[2,144,512]{2,1,0:T(8,128)(2,1)S(1)} %get-tuple-element.33), channel_id=1, source_target_pairs={{0,2},{1,3},{2,0},{3,1},{4,6},{5,7},{6,4},{7,5},{8,10},{9,11},{10,... | collective-permute-start | bytes 884744 | tf_op jit(solution)/shard_map/ppermute | solution.py:438
  98.8 14.0 %collective-permute-start.5 = (s16[2,144,512]{2,1,0:T(8,128)(2,1)S(1)}, s16[2,144,512]{2,1,0:T(8,128)(2,1)S(1)}, u32[]{:S(2)}, u32[]{:S(2)}) collective-permute-start(s16[2,144,512]{2,1,0:T(8,128)(2,1)S(1)} %get-tuple-element.34), channel_id=1, source_target_pairs={{0,3},{1,0},{2,1},{3,2},{4,7},{5,4},{6,5},{7,6},{8,11},{9,8},{10,9... | collective-permute-start | bytes 884744 | tf_op jit(solution)/shard_map/ppermute | solution.py:438

commit v5 on v4

--- a/solution.py
+++ b/solution.py
@@ -36,6 +36,12 @@
 def split_two(array):
     high = array.astype(jnp.bfloat16)
     return high, (array - high.astype(jnp.float32)).astype(jnp.bfloat16)
+
+
+tn = (((0,), (0,)), ((), ()))
+nn = (((1,), (0,)), ((), ()))
+nt = (((1,), (1,)), ((), ()))
+dot = functools.partial(lax.dot_general, preferred_element_type=jnp.float32)
 
 
 def pack_kernel(owner_ref, grad_ref, packed_ref, count_ref):
@@ -92,7 +98,7 @@
 
 def roots_kernel(
     place_ref, left_ref, right_ref, one_ref, two_ref, three_ref,
-    left_high_ref, left_low_ref, right_high_ref, right_low_ref,
+    left_high_ref, left_low_ref, right_high_ref, right_low_ref, high_ref, low_ref,
 ):
     part = place_ref[1]
     width = left_ref.shape[1]
@@ -121,8 +127,17 @@
         put(3, 3, three_ref[root, :, :width])
         put_pair(3, 2, three_ref[root, :, width:])
 
-    spread(0, left_ref, left_high_ref, left_low_ref)
+    spread(0, left_ref, high_ref, low_ref)
     spread(1, right_ref, right_high_ref, right_low_ref)
+    row = lax.broadcasted_iota(jnp.int32, (width, width), 0)
+    col = lax.broadcasted_iota(jnp.int32, (width, width), 1)
+    z = lax.shift_right_logical(row, 2) & (parts - 1)
+    source = z * (width // parts) + lax.shift_right_logical(row, 4) * 4 + (row & 3)
+    order = jnp.where(col == source, 1.0, 0.0).astype(jnp.bfloat16)
+    for m in range(parts):
+        cols = slice(m * width, (m + 1) * width)
+        left_high_ref[:, cols] = dot(high_ref[:, cols], order, nt).astype(jnp.bfloat16)
+        left_low_ref[:, cols] = dot(low_ref[:, cols], order, nt).astype(jnp.bfloat16)
 
 
 def whole(shape):
@@ -140,6 +155,7 @@
             grid=(1,),
             in_specs=[mine, mine] + [whole(other.shape) for other in others],
             out_specs=[whole(out.shape)] * 4,
+            scratch_shapes=[pltpu.VMEM(out.shape, out.dtype)] * 2,
         ),
         out_shape=[out] * 4,
         compiler_params=pltpu.CompilerParams(vmem_limit_bytes=32 * 1024 * 1024),
@@ -171,18 +187,16 @@
     return jnp.round(jnp.where(value < 0, -root, root)).astype(jnp.int32)
 
 
-tn = (((0,), (0,)), ((), ()))
-nn = (((1,), (0,)), ((), ()))
-nt = (((1,), (1,)), ((), ()))
-dot = functools.partial(lax.dot_general, preferred_element_type=jnp.float32)
-
-
 def precondition_kernel(
     place_ref, grad_ref, left_high_ref, left_low_ref, right_high_ref, right_low_ref, message_ref
 ):
     order = left_high_ref.shape[0]
-    grad = jnp.concatenate([grad_ref[:, m].reshape(order, -1) for m in range(parts)], axis=1)
-    half = dot(left_high_ref[...], grad, tn) + dot(left_low_ref[...], grad, tn)
+    deep = grad_ref.shape[2] // parts
+    rows = [(device, slice(m * deep, (m + 1) * deep)) for m in range(parts) for device in range(near)]
+    grad = jnp.concatenate(
+        [jnp.concatenate([grad_ref[device, m, at] for device, at in rows], axis=0) for m in range(parts)], axis=1
+    )
+    half = dot(left_high_ref[...], grad, nn) + dot(left_low_ref[...], grad, nn)
     half_high, half_low = split_two(half)
     right_high = right_high_ref[...]
     result = dot(half_high, right_high, nn) + dot(half_low, right_high, nn) + dot(half_high, right_low_ref[...], nn)
@@ -405,7 +419,10 @@
     three = send((0, 3), 1)
     two = send((0,), 2)
     one = send((0, 2, 1), 3)
-    in_plane, one, two, three, owner_map = lax.optimization_barrier((in_plane, one, two, three, owner_map))
+    my_slot = jnp.minimum(my_part, capacity - 1)
+    place = jnp.stack([my_owner % near, my_part, my_slot])
+    roots = spread_roots(place, left_root, right_root, (one, two, three))
+    in_plane, owner_map, *roots = lax.optimization_barrier((in_plane, owner_map, *roots))
 
     fanned = fan(in_plane).reshape(near * parts, far * row_share, col_share)
     landed = exchange(fanned, ("fsdp", "mp"), plane_groups)
@@ -415,27 +432,19 @@
     my_cells = my_owner * capacity + jnp.arange(capacity, dtype=jnp.int32)
     holding = cell_ids[None, :] == my_cells[:, None]
     taken = jnp.max(jnp.where(holding, 1 + up_block.astype(jnp.int32)[None, :], 0), axis=1)
-    my_slot = jnp.minimum(my_part, capacity - 1)
     my_taken = jnp.where(my_part < capacity, taken[my_slot], 0)
-    place = jnp.concatenate([jnp.stack([my_owner % near, my_part, my_slot, my_taken]), taken])
-
-    roots = spread_roots(place, left_root, right_root, (one, two, three))
-
-    def landed_order(array):
-        split = array.reshape(far, near, row_share, block_size)
-        return jnp.swapaxes(split, 0, 1).reshape(block_size, block_size)
-
-    roots = (landed_order(roots[0]), landed_order(roots[1]), roots[2], roots[3])
+    place = jnp.concatenate([place, my_taken[None], taken])
     message = precondition(place, landed, roots)
     landed, message = lax.optimization_barrier((landed, message))
     back = exchange(message, ("fsdp", "mp"), plane_groups)
-    arrived = exchange(repack(back, capacity), "fsdp", far_groups)
 
     block = landed.reshape(near, parts, far, row_share, col_share).transpose(2, 0, 3, 1, 4)
-    own_terms, *other_terms = terms(place, block.reshape(block_size, block_size))
+    made = terms(place, block.reshape(block_size, block_size))
+    back, own_terms, *other_terms = lax.optimization_barrier((back, *made))
     coded_terms = [own_terms]
     for k, other in enumerate(other_terms, 1):
         coded_terms.append(lax.ppermute(other, "mp", [(i, (i + k) % parts) for i in range(parts)]))
+    arrived = exchange(repack(back, capacity), "fsdp", far_groups)
     left_new, right_new = new_stats(place, coded_terms, left_stats, right_stats)
 
     cells = near * capacity

time: 119 us -> 122 us (1.025)
  blocking collectives: 17.1 us -> 0 us
  waiting for transfers between devices: 21.7 us -> 34.7 us
  starting transfers between devices: 49.6 us -> 59.2 us
  local copies, waits for them, and re-layouts: 11.3 us -> 8.4 us
    all_to_all x1 -> x0, blocking collectives: 17.1 us -> none  [exchange(): lax.all_to_all(array, axis_name, split_axis=0, concat_axis=0, axis_index_...]
    all_to_all x3 -> x4, waiting for transfers between devices: 4.19 us -> 16.6 us  [exchange(): lax.all_to_all(array, axis_name, split_axis=0, concat_axis=0, axis_index_...]
    all_to_all x3 -> x4, starting transfers between devices: 28.8 us -> 38.2 us  [exchange(): lax.all_to_all(array, axis_name, split_axis=0, concat_axis=0, axis_index_...]
    reshape x6 -> x0, local copies, waits for them, and re-layouts: 2.81 us -> none  [the longest x4 1.43 us: landed_order(): split = array.reshape(far, near, row_share, block_size)]
    unnamed x31 -> x27, local copies, waits for them, and re-layouts: 5.91 us -> 5.81 us
  transfers between devices with their start and end apart: 9 -> 10, of which waited for: 5 -> 8; matrix products, arithmetic and copies ran while one was open for 6% -> 3% of each run, Pallas kernels for 5% -> 5%
where the time goes in v5:
time: 122 us; the launch traced here: 120 us
  starting transfers between devices  59.2 us (49%)
  waiting for transfers between devices  34.7 us (28%)
  Pallas kernels  15.7 us (13%)
  local copies, waits for them, and re-layouts  8.4 us (7%)
  between operations  1.54 us (1%)
    all_to_all x4, starting transfers between devices, exchange(): lax.all_to_all(array, axis_name, split_axis=0, concat_axis=0, axis_index_...  38.2 us
    all_to_all x4, waiting for transfers between devices, exchange(): lax.all_to_all(array, axis_name, split_axis=0, concat_axis=0, axis_index_...  16.6 us
    ppermute x3, starting transfers between devices, send(): return lax.ppermute(jnp.concatenate(rows, axis=0), 'mp', pairs)  11.1 us
    ppermute x3, waiting for transfers between devices, on_device(): lax.ppermute(other, 'mp', [(i, (i + k) % parts) for i in range(parts)])  10.8 us
    ppermute x3, starting transfers between devices, on_device(): lax.ppermute(other, 'mp', [(i, (i + k) % parts) for i in range(parts)])  9.86 us
    ppermute x3, waiting for transfers between devices, send(): return lax.ppermute(jnp.concatenate(rows, axis=0), 'mp', pairs)  7.24 us
    unnamed x27, local copies, waits for them, and re-layouts  5.81 us
    pallas_call x1, Pallas kernels, precondition(): pl.pallas_call(precondition_kernel, grid_spec=pltpu.PrefetchScalarGridSpe...  3.93 us
  transfers between devices with their start and end apart: 10, of which 8 were waited for; matrix products, arithmetic and copies ran while one was open for 3% of the time, Pallas kernels for 5%

profile of v5, /device:TPU:6, one launch (start us, length us, event | category | flops | bytes accessed | tf_op | source)
XLA Modules:
  0.0 120.0 jit_solution(385029944097952823)
XLA Ops:
  2.3 1.9 %shard_map.85 = bf16[384,4,128]{2,1,0:T(4,128)(2,1)} custom-call(s32[128]{0:T(128)S(1)} %copy-done.5, bf16[128,4,128]{2,1,0:T(4,128)(2,1)S(1)} %copy-done.4), custom_call_target="tpu_custom_call" | custom-call | bytes 1048576 | tf_op jit(solution)/shard_map/pallas_call | solution.py:63
  4.2 15.2 %all-to-all-start = ((bf16[16,8,3,4,128]{4,3,2,1,0:T(4,128)(2,1)}), bf16[16,8,3,4,128]{4,3,2,1,0:T(4,128)(2,1)S(1)}, u32[]{:S(2)}, u32[]{:S(2)}) async-start(bf16[16,8,3,4,128]{4,3,2,1,0:T(4,128)(2,1)} %bitcast), calls=%async_computation | async-start | bytes 786432 | tf_op jit(solution)/shard_map/all_to_all | solution.py:31
  19.5 1.1 constant_dynamic-slice_fusion.1
  20.6 5.1 %collective-permute-start = (f32[2,128,384]{2,1,0:T(8,128)S(1)}, f32[2,128,384]{2,1,0:T(8,128)S(1)}, u32[]{:S(2)}, u32[]{:S(2)}) collective-permute-start(f32[2,128,384]{2,1,0:T(8,128)S(1)} %maximum_maximum_fusion), channel_id=1, source_target_pairs={{0,3},{1,0},{2,1},{3,2},{4,7},{5,4},{6,5},{7,6},{8,11},{9,8},{10,9... | collective-permute-start | bytes 1179656 | tf_op jit(solution)/shard_map/ppermute | solution.py:417
  25.7 1.9 %collective-permute-start.2 = (f32[2,128,256]{2,1,0:T(8,128)S(1)}, f32[2,128,256]{2,1,0:T(8,128)S(1)}, u32[]{:S(2)}, u32[]{:S(2)}) collective-permute-start(f32[2,128,256]{2,1,0:T(8,128)S(1)} %maximum_maximum_fusion.1), channel_id=1, source_target_pairs={{0,1},{1,2},{2,3},{3,0},{4,5},{5,6},{6,7},{7,4},{8,9},{9,10},{10,1... | collective-permute-start | bytes 786440 | tf_op jit(solution)/shard_map/ppermute | solution.py:417
  27.6 4.1 %collective-permute-start.1 = (f32[2,128,128]{2,1,0:T(8,128)S(1)}, f32[2,128,128]{2,1,0:T(8,128)S(1)}, u32[]{:S(2)}, u32[]{:S(2)}) collective-permute-start(f32[2,128,128]{2,1,0:T(8,128)S(1)} %pad_maximum_fusion), channel_id=1, source_target_pairs={{0,2},{1,3},{2,0},{3,1},{4,6},{5,7},{6,4},{7,5},{8,10},{9,11},{10,... | collective-permute-start | bytes 393224 | tf_op jit(solution)/shard_map/ppermute | solution.py:417
  31.9 6.3 %collective-permute-done.1.two_ref = f32[2,128,128]{2,1,0:T(8,128)S(1)} collective-permute-done((f32[2,128,128]{2,1,0:T(8,128)S(1)}, f32[2,128,128]{2,1,0:T(8,128)S(1)}, u32[]{:S(2)}, u32[]{:S(2)}) %collective-permute-start.1) | collective-permute-done | bytes 131104 | tf_op jit(solution)/shard_map/ppermute | solution.py:417
  39.1 1.3 %shard_map.86 = (bf16[512,512]{1,0:T(8,128)(2,1)S(1)}, bf16[512,512]{1,0:T(8,128)(2,1)S(1)}, bf16[512,512]{1,0:T(8,128)(2,1)S(1)}, bf16[512,512]{1,0:T(8,128)(2,1)S(1)}) custom-call(s32[3]{0:T(128)S(1)} %pad_add_fusion.place_ref, f32[3,128,512]{2,1,0:T(8,128)S(1)} %copy-done, f32[3,128,512]{2,1,0:T(8,128)S(1)} %copy-done.1, ...), custom_call_target="tpu_custom_call" | custom-call | bytes 5242880 | tf_op jit(solution)/shard_map/pallas_call | solution.py:151
  44.1 7.7 %all-to-all-start.1 = ((bf16[32,64,128]{2,1,0:T(8,128)(2,1)}), bf16[32,64,128]{2,1,0:T(8,128)(2,1)S(1)}, u32[]{:S(2)}, u32[]{:S(2)}) async-start(bf16[32,64,128]{2,1,0:T(8,128)(2,1)} %bitcast.4), calls=%async_computation.1 | async-start | bytes 1048576 | tf_op jit(solution)/shard_map/all_to_all | solution.py:31
  54.2 7.3 %all-to-all-done.1 = bf16[32,64,128]{2,1,0:T(8,128)(2,1)S(1)} async-done(((bf16[32,64,128]{2,1,0:T(8,128)(2,1)}), bf16[32,64,128]{2,1,0:T(8,128)(2,1)S(1)}, u32[]{:S(2)}, u32[]{:S(2)}) %all-to-all-start.1) | async-done | bytes 524320 | tf_op jit(solution)/shard_map/all_to_all | solution.py:31
  61.5 1.0 copy-done.12
  62.6 3.9 %shard_map.88 = s16[32,17,4,128]{3,2,1,0:T(4,128)(2,1)} custom-call(s32[7]{0:T(128)S(1)} %concatenate.32.place_ref, bf16[8,4,64,128]{3,2,1,0:T(8,128)(2,1)S(1)} %bitcast.16, bf16[512,512]{1,0:T(8,128)(2,1)S(1)} %get-tuple-element.32.left_high_ref, bf16[512,512]{1,0:T(8,128)(2,1)S(1)} %copy-done.8, bf16[512,512]{1,0:T(8,128)(2,1)S(1)} %copy-done.10, ...), custom_call_target="tpu_custom_call" | custom-call | flops 1342177280 | bytes 4194304 | tf_op jit(solution)/shard_map/pallas_call | solution.py:242
  66.5 6.0 %all-to-all-start.2 = ((s16[32,17,4,128]{3,2,1,0:T(4,128)(2,1)}), s16[32,17,4,128]{3,2,1,0:T(4,128)(2,1)S(1)}, u32[]{:S(2)}, u32[]{:S(2)}) async-start(s16[32,17,4,128]{3,2,1,0:T(4,128)(2,1)} %shard_map.88), calls=%async_computation.2 | async-start | bytes 1114112 | tf_op jit(solution)/shard_map/all_to_all | solution.py:31
  73.3 2.6 %shard_map.89 = (s16[2,144,512]{2,1,0:T(8,128)(2,1)S(1)}, s16[2,144,512]{2,1,0:T(8,128)(2,1)S(1)}, s16[2,144,512]{2,1,0:T(8,128)(2,1)S(1)}, s16[2,144,512]{2,1,0:T(8,128)(2,1)S(1)}) custom-call(s32[7]{0:T(128)S(1)} %concatenate.32.place_ref, bf16[512,512]{1,0:T(8,128)(2,1)S(1)} %bitcast.18), custom_call_target="tpu_custom_call" | custom-call | flops 536870912 | bytes 2097152 | tf_op jit(solution)/shard_map/pallas_call | solution.py:278
  75.9 6.5 %all-to-all-done.2.back_ref = s16[32,17,4,128]{3,2,1,0:T(4,128)(2,1)S(1)} async-done(((s16[32,17,4,128]{3,2,1,0:T(4,128)(2,1)}), s16[32,17,4,128]{3,2,1,0:T(4,128)(2,1)S(1)}, u32[]{:S(2)}, u32[]{:S(2)}) %all-to-all-start.2) | async-done | bytes 557088 | tf_op jit(solution)/shard_map/all_to_all | solution.py:31
  83.3 9.3 %all-to-all-start.3 = ((s16[16,25,4,128]{3,2,1,0:T(4,128)(2,1)}), s16[16,25,4,128]{3,2,1,0:T(4,128)(2,1)S(1)}, u32[]{:S(2)}, u32[]{:S(2)}) async-start(s16[16,25,4,128]{3,2,1,0:T(4,128)(2,1)} %shard_map.90), calls=%async_computation.3 | async-start | bytes 819200 | tf_op jit(solution)/shard_map/all_to_all | solution.py:31
  92.6 2.5 %collective-permute-start.3 = (s16[2,144,512]{2,1,0:T(8,128)(2,1)S(1)}, s16[2,144,512]{2,1,0:T(8,128)(2,1)S(1)}, u32[]{:S(2)}, u32[]{:S(2)}) collective-permute-start(s16[2,144,512]{2,1,0:T(8,128)(2,1)S(1)} %get-tuple-element.44), channel_id=1, source_target_pairs={{0,1},{1,2},{2,3},{3,0},{4,5},{5,6},{6,7},{7,4},{8,9},{9,10},{10,1... | collective-permute-start | bytes 884744 | tf_op jit(solution)/shard_map/ppermute | solution.py:446
  95.1 4.2 %collective-permute-start.4 = (s16[2,144,512]{2,1,0:T(8,128)(2,1)S(1)}, s16[2,144,512]{2,1,0:T(8,128)(2,1)S(1)}, u32[]{:S(2)}, u32[]{:S(2)}) collective-permute-start(s16[2,144,512]{2,1,0:T(8,128)(2,1)S(1)} %get-tuple-element.45), channel_id=1, source_target_pairs={{0,2},{1,3},{2,0},{3,1},{4,6},{5,7},{6,4},{7,5},{8,10},{9,11},{10,... | collective-permute-start | bytes 884744 | tf_op jit(solution)/shard_map/ppermute | solution.py:446
  99.4 3.1 %collective-permute-start.5 = (s16[2,144,512]{2,1,0:T(8,128)(2,1)S(1)}, s16[2,144,512]{2,1,0:T(8,128)(2,1)S(1)}, u32[]{:S(2)}, u32[]{:S(2)}) collective-permute-start(s16[2,144,512]{2,1,0:T(8,128)(2,1)S(1)} %get-tuple-element.46), channel_id=1, source_target_pairs={{0,3},{1,0},{2,1},{3,2},{4,7},{5,4},{6,5},{7,6},{8,11},{9,8},{10,9... | collective-permute-start | bytes 884744 | tf_op jit(solution)/shard_map/ppermute | solution.py:446
  102.5 8.3 %collective-permute-done.3.one_ref = s16[2,144,512]{2,1,0:T(8,128)(2,1)S(1)} collective-permute-done((s16[2,144,512]{2,1,0:T(8,128)(2,1)S(1)}, s16[2,144,512]{2,1,0:T(8,128)(2,1)S(1)}, u32[]{:S(2)}, u32[]{:S(2)}) %collective-permute-start.3) | collective-permute-done | bytes 294944 | tf_op jit(solution)/shard_map/ppermute | solution.py:446
  110.8 2.5 %collective-permute-done.5.three_ref = s16[2,144,512]{2,1,0:T(8,128)(2,1)S(1)} collective-permute-done((s16[2,144,512]{2,1,0:T(8,128)(2,1)S(1)}, s16[2,144,512]{2,1,0:T(8,128)(2,1)S(1)}, u32[]{:S(2)}, u32[]{:S(2)}) %collective-permute-start.5) | collective-permute-done | bytes 294944 | tf_op jit(solution)/shard_map/ppermute | solution.py:446
  113.3 2.0 %shard_map.92 = (f32[3,128,512]{2,1,0:T(8,128)}, f32[3,128,512]{2,1,0:T(8,128)}) custom-call(s32[7]{0:T(128)S(1)} %concatenate.32.place_ref, s16[2,144,512]{2,1,0:T(8,128)(2,1)S(1)} %get-tuple-element.43.own_ref, s16[2,144,512]{2,1,0:T(8,128)(2,1)S(1)} %collective-permute-done.3.one_ref, s16[2,144,512]{2,1,0:T(8,128)(2,1)S(1)} %collective-permute-done.4.two_ref, ...), custom_call_target="tpu_custom_call" | custom-call | bytes 5242880 | tf_op jit(solution)/shard_map/pallas_call | solution.py:318
  115.3 2.4 %all-to-all-done.3.arrived_ref = s16[16,25,4,128]{3,2,1,0:T(4,128)(2,1)S(1)} async-done(((s16[16,25,4,128]{3,2,1,0:T(4,128)(2,1)}), s16[16,25,4,128]{3,2,1,0:T(4,128)(2,1)S(1)}, u32[]{:S(2)}, u32[]{:S(2)}) %all-to-all-start.3) | async-done | bytes 409632 | tf_op jit(solution)/shard_map/all_to_all | solution.py:31
  117.8 2.2 %shard_map.91 = bf16[128,4,128]{2,1,0:T(4,128)(2,1)} custom-call(s32[128]{0:T(128)S(1)} %get-tuple-element.50.at_ref, s32[128,128]{1,0:T(8,128)S(1)} %broadcast_in_dim.18.spot_ref, s32[128,128]{1,0:T(8,128)S(1)} %broadcast_in_dim.19.up_ref, s16[16,25,4,128]{3,2,1,0:T(4,128)(2,1)S(1)} %all-to-all-done.3.arrived_ref), custom_call_target="tpu_custom_call" | custom-call | bytes 1048576 | tf_op jit(solution)/shard_map/pallas_call | solution.py:384
  (47 shorter events, 10.0 us)
Async XLA Ops:
  0.6 18.8 %copy-start = (f32[3,128,512]{2,1,0:T(8,128)S(1)}, f32[3,128,512]{2,1,0:T(8,128)}, u32[]{:S(2)}) copy-start(f32[3,128,512]{2,1,0:T(8,128)} %left_ref.2) | copy-start | bytes 2359300
  0.6 1.0 copy-start.4
  1.6 0.7 copy-start.5
  4.2 39.0 %all-to-all-start = ((bf16[16,8,3,4,128]{4,3,2,1,0:T(4,128)(2,1)}), bf16[16,8,3,4,128]{4,3,2,1,0:T(4,128)(2,1)S(1)}, u32[]{:S(2)}, u32[]{:S(2)}) async-start(bf16[16,8,3,4,128]{4,3,2,1,0:T(4,128)(2,1)} %bitcast), calls=%async_computation | async-start | bytes 786432 | tf_op jit(solution)/shard_map/all_to_all | solution.py:31
  20.6 18.5 %copy-start.1 = (f32[3,128,512]{2,1,0:T(8,128)S(1)}, f32[3,128,512]{2,1,0:T(8,128)}, u32[]{:S(2)}) copy-start(f32[3,128,512]{2,1,0:T(8,128)} %right_ref.2) | copy-start | bytes 2359300
  20.6 18.5 %collective-permute-start = (f32[2,128,384]{2,1,0:T(8,128)S(1)}, f32[2,128,384]{2,1,0:T(8,128)S(1)}, u32[]{:S(2)}, u32[]{:S(2)}) collective-permute-start(f32[2,128,384]{2,1,0:T(8,128)S(1)} %maximum_maximum_fusion), channel_id=1, source_target_pairs={{0,3},{1,0},{2,1},{3,2},{4,7},{5,4},{6,5},{7,6},{8,11},{9,8},{10,9... | collective-permute-start | bytes 1179656 | tf_op jit(solution)/shard_map/ppermute | solution.py:417
  25.7 13.4 %collective-permute-start.2 = (f32[2,128,256]{2,1,0:T(8,128)S(1)}, f32[2,128,256]{2,1,0:T(8,128)S(1)}, u32[]{:S(2)}, u32[]{:S(2)}) collective-permute-start(f32[2,128,256]{2,1,0:T(8,128)S(1)} %maximum_maximum_fusion.1), channel_id=1, source_target_pairs={{0,1},{1,2},{2,3},{3,0},{4,5},{5,6},{6,7},{7,4},{8,9},{9,10},{10,1... | collective-permute-start | bytes 786440 | tf_op jit(solution)/shard_map/ppermute | solution.py:417
  27.6 10.5 %collective-permute-start.1 = (f32[2,128,128]{2,1,0:T(8,128)S(1)}, f32[2,128,128]{2,1,0:T(8,128)S(1)}, u32[]{:S(2)}, u32[]{:S(2)}) collective-permute-start(f32[2,128,128]{2,1,0:T(8,128)S(1)} %pad_maximum_fusion), channel_id=1, source_target_pairs={{0,2},{1,3},{2,0},{3,1},{4,6},{5,7},{6,4},{7,5},{8,10},{9,11},{10,... | collective-permute-start | bytes 393224 | tf_op jit(solution)/shard_map/ppermute | solution.py:417
  40.4 0.8 copy-start.7
  41.2 0.8 copy-start.9
  42.0 0.8 copy-start.11
  44.1 17.4 %copy-start.8 = (bf16[512,512]{1,0:T(8,128)(2,1)S(1)}, bf16[512,512]{1,0:T(8,128)(2,1)}, u32[]{:S(2)}) copy-start(bf16[512,512]{1,0:T(8,128)(2,1)} %copy-done.7) | copy-start | bytes 1572868
  44.1 17.4 %copy-start.10 = (bf16[512,512]{1,0:T(8,128)(2,1)S(1)}, bf16[512,512]{1,0:T(8,128)(2,1)}, u32[]{:S(2)}) copy-start(bf16[512,512]{1,0:T(8,128)(2,1)} %copy-done.9) | copy-start | bytes 1572868
  44.1 17.4 %all-to-all-start.1 = ((bf16[32,64,128]{2,1,0:T(8,128)(2,1)}), bf16[32,64,128]{2,1,0:T(8,128)(2,1)S(1)}, u32[]{:S(2)}, u32[]{:S(2)}) async-start(bf16[32,64,128]{2,1,0:T(8,128)(2,1)} %bitcast.4), calls=%async_computation.1 | async-start | bytes 1048576 | tf_op jit(solution)/shard_map/all_to_all | solution.py:31
  51.9 0.7 copy-start.6
  61.5 1.0 copy-start.12
  66.5 15.9 %all-to-all-start.2 = ((s16[32,17,4,128]{3,2,1,0:T(4,128)(2,1)}), s16[32,17,4,128]{3,2,1,0:T(4,128)(2,1)S(1)}, u32[]{:S(2)}, u32[]{:S(2)}) async-start(s16[32,17,4,128]{3,2,1,0:T(4,128)(2,1)} %shard_map.88), calls=%async_computation.2 | async-start | bytes 1114112 | tf_op jit(solution)/shard_map/all_to_all | solution.py:31
  82.4 30.9 %copy-start.2 = (f32[3,128,512]{2,1,0:T(8,128)S(1)}, f32[3,128,512]{2,1,0:T(8,128)}, u32[]{:S(2)}) copy-start(f32[3,128,512]{2,1,0:T(8,128)} %left_ref.3) | copy-start | bytes 2359300
  82.4 30.9 %copy-start.3 = (f32[3,128,512]{2,1,0:T(8,128)S(1)}, f32[3,128,512]{2,1,0:T(8,128)}, u32[]{:S(2)}) copy-start(f32[3,128,512]{2,1,0:T(8,128)} %right_ref.3) | copy-start | bytes 2359300
  83.3 34.3 %all-to-all-start.3 = ((s16[16,25,4,128]{3,2,1,0:T(4,128)(2,1)}), s16[16,25,4,128]{3,2,1,0:T(4,128)(2,1)S(1)}, u32[]{:S(2)}, u32[]{:S(2)}) async-start(s16[16,25,4,128]{3,2,1,0:T(4,128)(2,1)} %shard_map.90), calls=%async_computation.3 | async-start | bytes 819200 | tf_op jit(solution)/shard_map/all_to_all | solution.py:31
  92.6 18.2 %collective-permute-start.3 = (s16[2,144,512]{2,1,0:T(8,128)(2,1)S(1)}, s16[2,144,512]{2,1,0:T(8,128)(2,1)S(1)}, u32[]{:S(2)}, u32[]{:S(2)}) collective-permute-start(s16[2,144,512]{2,1,0:T(8,128)(2,1)S(1)} %get-tuple-element.44), channel_id=1, source_target_pairs={{0,1},{1,2},{2,3},{3,0},{4,5},{5,6},{6,7},{7,4},{8,9},{9,10},{10,1... | collective-permute-start | bytes 884744 | tf_op jit(solution)/shard_map/ppermute | solution.py:446
  95.1 15.6 %collective-permute-start.4 = (s16[2,144,512]{2,1,0:T(8,128)(2,1)S(1)}, s16[2,144,512]{2,1,0:T(8,128)(2,1)S(1)}, u32[]{:S(2)}, u32[]{:S(2)}) collective-permute-start(s16[2,144,512]{2,1,0:T(8,128)(2,1)S(1)} %get-tuple-element.45), channel_id=1, source_target_pairs={{0,2},{1,3},{2,0},{3,1},{4,6},{5,7},{6,4},{7,5},{8,10},{9,11},{10,... | collective-permute-start | bytes 884744 | tf_op jit(solution)/shard_map/ppermute | solution.py:446
  99.4 14.0 %collective-permute-start.5 = (s16[2,144,512]{2,1,0:T(8,128)(2,1)S(1)}, s16[2,144,512]{2,1,0:T(8,128)(2,1)S(1)}, u32[]{:S(2)}, u32[]{:S(2)}) collective-permute-start(s16[2,144,512]{2,1,0:T(8,128)(2,1)S(1)} %get-tuple-element.46), channel_id=1, source_target_pairs={{0,3},{1,0},{2,1},{3,2},{4,7},{5,4},{6,5},{7,6},{8,11},{9,8},{10,9... | collective-permute-start | bytes 884744 | tf_op jit(solution)/shard_map/ppermute | solution.py:446

commit v6 on v5

--- a/solution.py
+++ b/solution.py
@@ -14,13 +14,10 @@
 far = 16
 
 
-def cell_index(owner_map, capacity):
-    total_rows = owner_map.shape[0]
-    positions = jnp.arange(total_rows, dtype=jnp.int32)
-    same_owner = owner_map[None, :] == owner_map[:, None]
-    earlier = positions[None, :] < positions[:, None]
-    ranks = jnp.sum((same_owner & earlier).astype(jnp.int32), axis=1)
-    return owner_map * capacity + ranks
+def earlier_alike(kind):
+    positions = jnp.arange(kind.shape[0], dtype=jnp.int32)
+    alike = (kind[None, :] == kind[:, None]) & (positions[None, :] < positions[:, None])
+    return jnp.sum(alike.astype(jnp.int32), axis=1)
 
 
 far_groups = [[z * near + n for z in range(far)] for n in range(near)]
@@ -44,22 +41,23 @@
 dot = functools.partial(lax.dot_general, preferred_element_type=jnp.float32)
 
 
+def whole(shape):
+    return pl.BlockSpec(shape, lambda i, *_: (0,) * len(shape))
+
+
 def pack_kernel(owner_ref, grad_ref, packed_ref, count_ref):
-    blocks = grad_ref.shape[0]
-    slots = packed_ref.shape[0] // blocks
     packed_ref[...] = jnp.zeros_like(packed_ref)
-    for owner in range(blocks):
-        count_ref[owner] = 0
-    for b in range(blocks):
-        owner = owner_ref[b]
-        rank = count_ref[owner]
-        count_ref[owner] = rank + 1
-        packed_ref[owner * slots + rank] = grad_ref[b]
-
-
-def pack(owner_map, gradient, slots):
-    blocks = gradient.shape[0]
-    packed = (blocks * slots,) + gradient.shape[1:]
+    for z in range(far):
+        count_ref[z] = 0
+    for b in range(grad_ref.shape[0]):
+        z = lax.div(owner_ref[b], near)
+        rank = count_ref[z]
+        count_ref[z] = rank + 1
+        packed_ref[z, rank] = grad_ref[b]
+
+
+def pack(owner_map, gradient, room):
+    packed = (far, room) + gradient.shape[1:]
     return pl.pallas_call(
         pack_kernel,
         grid_spec=pltpu.PrefetchScalarGridSpec(
@@ -67,7 +65,7 @@
             grid=(1,),
             in_specs=[whole(gradient.shape)],
             out_specs=whole(packed),
-            scratch_shapes=[pltpu.SMEM((blocks,), jnp.int32)],
+            scratch_shapes=[pltpu.SMEM((far,), jnp.int32)],
         ),
         out_shape=jax.ShapeDtypeStruct(packed, gradient.dtype),
         compiler_params=pltpu.CompilerParams(vmem_limit_bytes=16 * 1024 * 1024),
@@ -75,25 +73,27 @@
     )(owner_map, gradient)
 
 
-def fan_kernel(plane_ref, fan_ref):
+def fan_kernel(rank_ref, plane_ref, fan_ref):
+    slots = rank_ref.shape[0] // near
     for n in range(near):
-        for slot in range(parts):
-            if slot < plane_ref.shape[2]:
-                fan_ref[n, slot] = plane_ref[:, n, slot]
-            else:
-                fan_ref[n, slot] = jnp.zeros(fan_ref.shape[2:], fan_ref.dtype)
-
-
-def fan(in_plane):
-    _, _, slots, rows, width = in_plane.shape
+        for slot in range(slots):
+            rank = jnp.maximum(rank_ref[n * slots + slot], 0)
+            fan_ref[n, slot] = plane_ref[:, rank]
+        for slot in range(slots, parts):
+            fan_ref[n, slot] = jnp.zeros(fan_ref.shape[2:], fan_ref.dtype)
+
+
+def fan(ranks, in_plane):
+    fanned = (near, parts, far) + in_plane.shape[2:]
     return pl.pallas_call(
         fan_kernel,
-        out_shape=jax.ShapeDtypeStruct((near, parts, far, rows, width), in_plane.dtype),
-        in_specs=[pl.BlockSpec(memory_space=pltpu.VMEM)],
-        out_specs=pl.BlockSpec(memory_space=pltpu.VMEM),
+        grid_spec=pltpu.PrefetchScalarGridSpec(
+            num_scalar_prefetch=1, grid=(1,), in_specs=[whole(in_plane.shape)], out_specs=whole(fanned)
+        ),
+        out_shape=jax.ShapeDtypeStruct(fanned, in_plane.dtype),
         compiler_params=pltpu.CompilerParams(vmem_limit_bytes=16 * 1024 * 1024),
         cost_estimate=pl.CostEstimate(flops=0, bytes_accessed=1 << 20, transcendentals=0),
-    )(in_plane)
+    )(ranks, in_plane)
 
 
 def roots_kernel(
@@ -138,10 +138,6 @@
         cols = slice(m * width, (m + 1) * width)
         left_high_ref[:, cols] = dot(high_ref[:, cols], order, nt).astype(jnp.bfloat16)
         left_low_ref[:, cols] = dot(low_ref[:, cols], order, nt).astype(jnp.bfloat16)
-
-
-def whole(shape):
-    return pl.BlockSpec(shape, lambda i, *_: (0,) * len(shape))
 
 
 def spread_roots(place, left_root, right_root, others):
@@ -329,32 +325,39 @@
     )(place, *coded_terms, left_stats, right_stats)
 
 
-def repack_kernel(back_ref, ahead_ref):
-    cells = ahead_ref.shape[1] - 1
-    slots = cells // near
+def repack_kernel(rank_ref, back_ref, ahead_ref):
+    room = ahead_ref.shape[1] - 1
+    slots = rank_ref.shape[0] // near
     for device in range(near):
         for slot in range(slots):
-            ahead_ref[:, device * slots + slot] = back_ref[device * parts + slot, :far]
+            rank = rank_ref[device * slots + slot]
+
+            @pl.when(rank >= 0)
+            def _():
+                ahead_ref[:, jnp.maximum(rank, 0)] = back_ref[device * parts + slot, :far]
+
     wide = [back_ref[device, far].astype(jnp.int32) for device in range(near * parts)]
     facts = functools.reduce(jnp.add, wide).astype(jnp.int16)
     for z in range(far):
-        ahead_ref[z, cells] = facts
-
-
-def repack(back, slots):
+        ahead_ref[z, room] = facts
+
+
+def repack(ranks, back, room):
+    ahead = (far, room + 1) + back.shape[2:]
     return pl.pallas_call(
         repack_kernel,
-        out_shape=jax.ShapeDtypeStruct((far, near * slots + 1) + back.shape[2:], back.dtype),
-        in_specs=[pl.BlockSpec(memory_space=pltpu.VMEM)],
-        out_specs=pl.BlockSpec(memory_space=pltpu.VMEM),
+        grid_spec=pltpu.PrefetchScalarGridSpec(
+            num_scalar_prefetch=1, grid=(1,), in_specs=[whole(back.shape)], out_specs=whole(ahead)
+        ),
+        out_shape=jax.ShapeDtypeStruct(ahead, back.dtype),
         compiler_params=pltpu.CompilerParams(vmem_limit_bytes=16 * 1024 * 1024),
         cost_estimate=pl.CostEstimate(flops=0, bytes_accessed=1 << 20, transcendentals=0),
-    )(back)
+    )(ranks, back)
 
 
 def finish_kernel(at_ref, spot_ref, up_ref, arrived_ref, update_ref, factor_ref):
-    cells = arrived_ref.shape[1] - 1
-    facts = [arrived_ref[z, cells].astype(jnp.int32).astype(jnp.float32) for z in range(far)]
+    room = arrived_ref.shape[1] - 1
+    facts = [arrived_ref[z, room].astype(jnp.int32).astype(jnp.float32) for z in range(far)]
     row = lambda r: jnp.concatenate([fact[r : r + 1] for fact in facts], axis=0)
     sums = jnp.sum(decoded(row(0), row(1), row(2)), axis=0, keepdims=True)
     kind = lax.rem(lax.broadcasted_iota(jnp.int32, sums.shape, 1), 4)
@@ -375,12 +378,12 @@
 
     for b in range(update_ref.shape[0]):
         at = at_ref[b]
-        code = arrived_ref[at // cells, lax.rem(at, cells)].astype(jnp.int32).astype(jnp.float32)
+        code = arrived_ref[lax.div(at, room), lax.rem(at, room)].astype(jnp.int32).astype(jnp.float32)
         update_ref[b] = (code * jnp.abs(code) * factor_ref[b : b + 1, :]).astype(jnp.bfloat16)
 
 
-def finish(cell_ids, spot, up, arrived):
-    blocks = cell_ids.shape[0]
+def finish(places, spot, up, arrived):
+    blocks = places.shape[0]
     return pl.pallas_call(
         finish_kernel,
         grid_spec=pltpu.PrefetchScalarGridSpec(
@@ -393,17 +396,16 @@
         out_shape=jax.ShapeDtypeStruct((blocks,) + arrived.shape[2:], jnp.bfloat16),
         compiler_params=pltpu.CompilerParams(vmem_limit_bytes=16 * 1024 * 1024),
         cost_estimate=pl.CostEstimate(flops=0, bytes_accessed=1 << 20, transcendentals=0),
-    )(cell_ids, spot, up, arrived)
-
-
-def on_device(gradient, owner_map, left_stats, right_stats, left_root, right_root):
+    )(places, spot, up, arrived)
+
+
+def run(room, gradient, owner_map, left_stats, right_stats, left_root, right_root):
     block_count, row_share, col_share = gradient.shape
     capacity, part_rows, block_size = left_stats.shape
     my_owner = lax.axis_index("fsdp")
     my_part = lax.axis_index("mp")
 
-    packed = pack(owner_map, gradient, capacity).reshape(far, near, capacity, row_share, col_share)
-    in_plane = exchange(packed, "fsdp", far_groups)
+    in_plane = exchange(pack(owner_map, gradient, room), "fsdp", far_groups)
 
     def send(steps, k):
         slot = jnp.minimum((my_part + k) % parts, capacity - 1)
@@ -419,15 +421,21 @@
     three = send((0, 3), 1)
     two = send((0,), 2)
     one = send((0, 2, 1), 3)
+
+    cell_ids = owner_map * capacity + earlier_alike(owner_map)
+    zone = owner_map // near
+    rank = earlier_alike(zone)
+    my_cells = my_owner // near * near * capacity + jnp.arange(near * capacity, dtype=jnp.int32)
+    my_ranks = jnp.max(jnp.where(cell_ids[None, :] == my_cells[:, None], rank[None, :], -1), axis=1)
+    in_plane, one, two, three, my_ranks = lax.optimization_barrier((in_plane, one, two, three, my_ranks))
+
     my_slot = jnp.minimum(my_part, capacity - 1)
     place = jnp.stack([my_owner % near, my_part, my_slot])
     roots = spread_roots(place, left_root, right_root, (one, two, three))
-    in_plane, owner_map, *roots = lax.optimization_barrier((in_plane, owner_map, *roots))
-
-    fanned = fan(in_plane).reshape(near * parts, far * row_share, col_share)
+
+    fanned = fan(my_ranks, in_plane).reshape(near * parts, far * row_share, col_share)
     landed = exchange(fanned, ("fsdp", "mp"), plane_groups)
 
-    cell_ids = cell_index(owner_map, capacity)
     up_block = jnp.arange(block_count, dtype=jnp.int32) >= block_count // 2
     my_cells = my_owner * capacity + jnp.arange(capacity, dtype=jnp.int32)
     holding = cell_ids[None, :] == my_cells[:, None]
@@ -444,14 +452,28 @@
     coded_terms = [own_terms]
     for k, other in enumerate(other_terms, 1):
         coded_terms.append(lax.ppermute(other, "mp", [(i, (i + k) % parts) for i in range(parts)]))
-    arrived = exchange(repack(back, capacity), "fsdp", far_groups)
+    arrived = exchange(repack(my_ranks, back, room), "fsdp", far_groups)
     left_new, right_new = new_stats(place, coded_terms, left_stats, right_stats)
 
-    cells = near * capacity
-    spot = cell_ids // cells * 128 + cell_ids % cells // capacity * 16 + cell_ids % capacity * 3
+    spot = zone * 128 + owner_map % near * 16 + cell_ids % capacity * 3
     across = lambda array: jnp.broadcast_to(array.astype(jnp.int32)[:, None], (block_count, 128))
-    update = finish(cell_ids, across(spot), across(up_block), arrived)
+    update = finish(zone * room + rank, across(spot), across(up_block), arrived)
     return (update, left_new, right_new)
+
+
+def on_device(gradient, owner_map, *rest):
+    slots = near * rest[0].shape[0]
+    room = slots * 2 // 3
+    zone = owner_map // near
+    held = jnp.sum((zone[None, :] == jnp.arange(far, dtype=jnp.int32)[:, None]).astype(jnp.int32), axis=1)
+    return lax.cond(
+        jnp.max(held) <= room,
+        functools.partial(run, room),
+        functools.partial(run, slots),
+        gradient,
+        owner_map,
+        *rest,
+    )
 
 
 def solution(mesh):

time: 122 us -> 122 us (level)
  the two profiles are of different devices: /device:TPU:6 before, /device:TPU:1 now
where the time goes in v6:
time: 122 us; the launch traced here: 121 us
  starting transfers between devices  60.1 us (49%)
  waiting for transfers between devices  31.4 us (26%)
  Pallas kernels  19.2 us (16%)
  local copies, waits for them, and re-layouts  5.82 us (5%)
  other arithmetic  2.31 us (2%)
  between operations  1.3 us (1%)
    all_to_all x4, starting transfers between devices, exchange(): lax.all_to_all(array, axis_name, split_axis=0, concat_axis=0, axis_index_...  40.5 us
    all_to_all x4, waiting for transfers between devices, exchange(): lax.all_to_all(array, axis_name, split_axis=0, concat_axis=0, axis_index_...  14.3 us
    ppermute x3, starting transfers between devices, send(): return lax.ppermute(jnp.concatenate(rows, axis=0), 'mp', pairs)  10.7 us
    ppermute x3, waiting for transfers between devices, run(): lax.ppermute(other, 'mp', [(i, (i + k) % parts) for i in range(parts)])  9.73 us
    ppermute x3, starting transfers between devices, run(): lax.ppermute(other, 'mp', [(i, (i + k) % parts) for i in range(parts)])  8.81 us
    ppermute x3, waiting for transfers between devices, send(): return lax.ppermute(jnp.concatenate(rows, axis=0), 'mp', pairs)  7.41 us
    pallas_call x1, Pallas kernels, precondition(): pl.pallas_call(precondition_kernel, grid_spec=pltpu.PrefetchScalarGridSpe...  3.93 us
    pallas_call x1, Pallas kernels, new_stats(): pl.pallas_call(stats_kernel, grid_spec=pltpu.PrefetchScalarGridSpec(num_s...  3.2 us
  transfers between devices with their start and end apart: 10, of which 7 were waited for; matrix products, arithmetic and copies ran while one was open for 3% of the time, Pallas kernels for 7%

profile of v6, /device:TPU:1, one launch (start us, length us, event | category | flops | bytes accessed | tf_op | source)
XLA Modules:
  0.0 121.0 jit_solution(8877813075843597485)
XLA Ops:
  3.4 117.0 %conditional.1 = (f32[3,128,512]{2,1,0:T(8,128)}, f32[3,128,512]{2,1,0:T(8,128)}, bf16[128,4,128]{2,1,0:T(4,128)(2,1)S(1)}) conditional(s32[]{:T(128)} %convert_element_type.47, (s32[128]{0:T(128)S(1)}, bf16[128,4,128]{2,1,0:T(4,128)(2,1)}, f32[3,128,512]{2,1,0:T(8,128)}, f32[3,128,512]{2,1,0:T(8,128)}, f32[3,128,512]{2,1,0:T(8,128)}, ...), branch_computations={%region_2.7_spmd, %region_7.12_spmd} | conditional | flops 1879948032 | bytes 52326428 | solution.py:469
  3.4 2.7 %branch_1_fun.8 = bf16[16,16,4,128]{3,2,1,0:T(4,128)(2,1)} custom-call(s32[128]{0:T(128)S(1)} %get-tuple-element.52.owner_ref, bf16[128,4,128]{2,1,0:T(4,128)(2,1)} %get-tuple-element.53.grad_ref), custom_call_target="tpu_custom_call" | custom-call | bytes 1048576 | tf_op jit(solution)/shard_map/cond/branch_1_fun/pallas_call | solution.py:61
  6.1 15.7 %all-to-all-start.4 = ((bf16[16,16,4,128]{3,2,1,0:T(4,128)(2,1)}), bf16[16,16,4,128]{3,2,1,0:T(4,128)(2,1)S(1)}, u32[]{:S(2)}, u32[]{:S(2)}) async-start(bf16[16,16,4,128]{3,2,1,0:T(4,128)(2,1)} %branch_1_fun.8), calls=%async_computation.4 | async-start | bytes 524288 | tf_op jit(solution)/shard_map/cond/branch_1_fun/all_to_all | solution.py:28
  23.1 3.2 %collective-permute-start.8 = (f32[2,128,256]{2,1,0:T(8,128)S(1)}, f32[2,128,256]{2,1,0:T(8,128)S(1)}, u32[]{:S(2)}, u32[]{:S(2)}) collective-permute-start(f32[2,128,256]{2,1,0:T(8,128)S(1)} %maximum_maximum_fusion.3), channel_id=1, source_target_pairs={{0,1},{1,2},{2,3},{3,0},{4,5},{5,6},{6,7},{7,4},{8,9},{9,10},{10,1... | collective-permute-start | bytes 786440 | tf_op jit(solution)/shard_map/cond/branch_1_fun/ppermute | solution.py:419
  26.3 4.5 %collective-permute-start.7 = (f32[2,128,128]{2,1,0:T(8,128)S(1)}, f32[2,128,128]{2,1,0:T(8,128)S(1)}, u32[]{:S(2)}, u32[]{:S(2)}) collective-permute-start(f32[2,128,128]{2,1,0:T(8,128)S(1)} %pad_maximum_fusion.1), channel_id=1, source_target_pairs={{0,2},{1,3},{2,0},{3,1},{4,6},{5,7},{6,4},{7,5},{8,10},{9,11},{10,... | collective-permute-start | bytes 393224 | tf_op jit(solution)/shard_map/cond/branch_1_fun/ppermute | solution.py:419
  30.9 3.0 %collective-permute-start.6 = (f32[2,128,384]{2,1,0:T(8,128)S(1)}, f32[2,128,384]{2,1,0:T(8,128)S(1)}, u32[]{:S(2)}, u32[]{:S(2)}) collective-permute-start(f32[2,128,384]{2,1,0:T(8,128)S(1)} %maximum_maximum_fusion.2), channel_id=1, source_target_pairs={{0,3},{1,0},{2,1},{3,2},{4,7},{5,4},{6,5},{7,6},{8,11},{9,8},{10,9... | collective-permute-start | bytes 1179656 | tf_op jit(solution)/shard_map/cond/branch_1_fun/ppermute | solution.py:419
  34.4 2.6 %collective-permute-done.7.two_ref = f32[2,128,128]{2,1,0:T(8,128)S(1)} collective-permute-done((f32[2,128,128]{2,1,0:T(8,128)S(1)}, f32[2,128,128]{2,1,0:T(8,128)S(1)}, u32[]{:S(2)}, u32[]{:S(2)}) %collective-permute-start.7) | collective-permute-done | bytes 131104 | tf_op jit(solution)/shard_map/cond/branch_1_fun/ppermute | solution.py:419
  37.1 4.8 %collective-permute-done.6.one_ref = f32[2,128,384]{2,1,0:T(8,128)S(1)} collective-permute-done((f32[2,128,384]{2,1,0:T(8,128)S(1)}, f32[2,128,384]{2,1,0:T(8,128)S(1)}, u32[]{:S(2)}, u32[]{:S(2)}) %collective-permute-start.6) | collective-permute-done | bytes 393248 | tf_op jit(solution)/shard_map/cond/branch_1_fun/ppermute | solution.py:419
  41.9 1.6 %branch_1_fun.9 = bf16[8,4,16,4,128]{4,3,2,1,0:T(4,128)(2,1)} custom-call(s32[24]{0:T(128)S(1)} %select_reduce_fusion.2.rank_ref, bf16[16,16,4,128]{3,2,1,0:T(4,128)(2,1)S(1)} %all-to-all-done.4.plane_ref), custom_call_target="tpu_custom_call" | custom-call | bytes 1048576 | tf_op jit(solution)/shard_map/cond/branch_1_fun/pallas_call | solution.py:88
  43.4 8.9 %all-to-all-start.5 = ((bf16[32,64,128]{2,1,0:T(8,128)(2,1)}), bf16[32,64,128]{2,1,0:T(8,128)(2,1)S(1)}, u32[]{:S(2)}, u32[]{:S(2)}) async-start(bf16[32,64,128]{2,1,0:T(8,128)(2,1)} %bitcast.15), calls=%async_computation.5 | async-start | bytes 1048576 | tf_op jit(solution)/shard_map/cond/branch_1_fun/all_to_all | solution.py:28
  53.9 2.3 %branch_1_fun.10 = (bf16[512,512]{1,0:T(8,128)(2,1)S(1)}, bf16[512,512]{1,0:T(8,128)(2,1)S(1)}, bf16[512,512]{1,0:T(8,128)(2,1)S(1)}, bf16[512,512]{1,0:T(8,128)(2,1)S(1)}) custom-call(s32[3]{0:T(128)S(1)} %pad_add_fusion.1.place_ref, f32[3,128,512]{2,1,0:T(8,128)} %get-tuple-element.54.left_ref, f32[3,128,512]{2,1,0:T(8,128)} %get-tuple-element.55.right_ref, ...), custom_call_target="tpu_custom_call" | custom-call | bytes 5242880 | tf_op jit(solution)/shard_map/cond/branch_1_fun/pallas_call | solution.py:147
  57.1 6.3 %all-to-all-done.5 = bf16[32,64,128]{2,1,0:T(8,128)(2,1)S(1)} async-done(((bf16[32,64,128]{2,1,0:T(8,128)(2,1)}), bf16[32,64,128]{2,1,0:T(8,128)(2,1)S(1)}, u32[]{:S(2)}, u32[]{:S(2)}) %all-to-all-start.5) | async-done | bytes 524320 | tf_op jit(solution)/shard_map/cond/branch_1_fun/all_to_all | solution.py:28
  64.4 3.9 %branch_1_fun.11 = s16[32,17,4,128]{3,2,1,0:T(4,128)(2,1)} custom-call(s32[7]{0:T(128)S(1)} %concatenate.49.place_ref, bf16[8,4,64,128]{3,2,1,0:T(8,128)(2,1)S(1)} %bitcast.32, bf16[512,512]{1,0:T(8,128)(2,1)S(1)} %get-tuple-element.61.left_high_ref, bf16[512,512]{1,0:T(8,128)(2,1)S(1)} %get-tuple-element.62.left_low_ref, ...), custom_call_target="tpu_custom_call" | custom-call | flops 1342177280 | bytes 4194304 | tf_op jit(solution)/shard_map/cond/branch_1_fun/pallas_call | solution.py:238
  68.3 4.5 %all-to-all-start.6 = ((s16[32,17,4,128]{3,2,1,0:T(4,128)(2,1)}), s16[32,17,4,128]{3,2,1,0:T(4,128)(2,1)S(1)}, u32[]{:S(2)}, u32[]{:S(2)}) async-start(s16[32,17,4,128]{3,2,1,0:T(4,128)(2,1)} %branch_1_fun.11), calls=%async_computation.6 | async-start | bytes 1114112 | tf_op jit(solution)/shard_map/cond/branch_1_fun/all_to_all | solution.py:28
  73.7 2.6 %branch_1_fun.12 = (s16[2,144,512]{2,1,0:T(8,128)(2,1)S(1)}, s16[2,144,512]{2,1,0:T(8,128)(2,1)S(1)}, s16[2,144,512]{2,1,0:T(8,128)(2,1)S(1)}, s16[2,144,512]{2,1,0:T(8,128)(2,1)S(1)}) custom-call(s32[7]{0:T(128)S(1)} %concatenate.49.place_ref, bf16[512,512]{1,0:T(8,128)(2,1)S(1)} %bitcast.35), custom_call_target="tpu_custom_call" | custom-call | flops 536870912 | bytes 2097152 | tf_op jit(solution)/shard_map/cond/branch_1_fun/pallas_call | solution.py:274
  76.3 8.0 %all-to-all-done.6.back_ref = s16[32,17,4,128]{3,2,1,0:T(4,128)(2,1)S(1)} async-done(((s16[32,17,4,128]{3,2,1,0:T(4,128)(2,1)}), s16[32,17,4,128]{3,2,1,0:T(4,128)(2,1)S(1)}, u32[]{:S(2)}, u32[]{:S(2)}) %all-to-all-start.6) | async-done | bytes 557088 | tf_op jit(solution)/shard_map/cond/branch_1_fun/all_to_all | solution.py:28
  85.8 11.4 %all-to-all-start.7 = ((s16[16,17,4,128]{3,2,1,0:T(4,128)(2,1)}), s16[16,17,4,128]{3,2,1,0:T(4,128)(2,1)S(1)}, u32[]{:S(2)}, u32[]{:S(2)}) async-start(s16[16,17,4,128]{3,2,1,0:T(4,128)(2,1)} %branch_1_fun.13), calls=%async_computation.7 | async-start | bytes 557056 | tf_op jit(solution)/shard_map/cond/branch_1_fun/all_to_all | solution.py:28
  97.2 3.0 %collective-permute-start.10 = (s16[2,144,512]{2,1,0:T(8,128)(2,1)S(1)}, s16[2,144,512]{2,1,0:T(8,128)(2,1)S(1)}, u32[]{:S(2)}, u32[]{:S(2)}) collective-permute-start(s16[2,144,512]{2,1,0:T(8,128)(2,1)S(1)} %get-tuple-element.74), channel_id=1, source_target_pairs={{0,2},{1,3},{2,0},{3,1},{4,6},{5,7},{6,4},{7,5},{8,10},{9,11},{10,... | collective-permute-start | bytes 884744 | tf_op jit(solution)/shard_map/cond/branch_1_fun/ppermute | solution.py:454
  100.2 3.9 %collective-permute-start.11 = (s16[2,144,512]{2,1,0:T(8,128)(2,1)S(1)}, s16[2,144,512]{2,1,0:T(8,128)(2,1)S(1)}, u32[]{:S(2)}, u32[]{:S(2)}) collective-permute-start(s16[2,144,512]{2,1,0:T(8,128)(2,1)S(1)} %get-tuple-element.75), channel_id=1, source_target_pairs={{0,3},{1,0},{2,1},{3,2},{4,7},{5,4},{6,5},{7,6},{8,11},{9,8},{10,9... | collective-permute-start | bytes 884744 | tf_op jit(solution)/shard_map/cond/branch_1_fun/ppermute | solution.py:454
  104.1 1.9 %collective-permute-start.9 = (s16[2,144,512]{2,1,0:T(8,128)(2,1)S(1)}, s16[2,144,512]{2,1,0:T(8,128)(2,1)S(1)}, u32[]{:S(2)}, u32[]{:S(2)}) collective-permute-start(s16[2,144,512]{2,1,0:T(8,128)(2,1)S(1)} %get-tuple-element.73), channel_id=1, source_target_pairs={{0,1},{1,2},{2,3},{3,0},{4,5},{5,6},{6,7},{7,4},{8,9},{9,10},{10,1... | collective-permute-start | bytes 884744 | tf_op jit(solution)/shard_map/cond/branch_1_fun/ppermute | solution.py:454
  106.0 1.7 %collective-permute-done.10.two_ref = s16[2,144,512]{2,1,0:T(8,128)(2,1)S(1)} collective-permute-done((s16[2,144,512]{2,1,0:T(8,128)(2,1)S(1)}, s16[2,144,512]{2,1,0:T(8,128)(2,1)S(1)}, u32[]{:S(2)}, u32[]{:S(2)}) %collective-permute-start.10) | collective-permute-done | bytes 294944 | tf_op jit(solution)/shard_map/cond/branch_1_fun/ppermute | solution.py:454
  107.7 5.9 %collective-permute-done.11.three_ref = s16[2,144,512]{2,1,0:T(8,128)(2,1)S(1)} collective-permute-done((s16[2,144,512]{2,1,0:T(8,128)(2,1)S(1)}, s16[2,144,512]{2,1,0:T(8,128)(2,1)S(1)}, u32[]{:S(2)}, u32[]{:S(2)}) %collective-permute-start.11) | collective-permute-done | bytes 294944 | tf_op jit(solution)/shard_map/cond/branch_1_fun/ppermute | solution.py:454
  113.6 2.2 %collective-permute-done.9.one_ref = s16[2,144,512]{2,1,0:T(8,128)(2,1)S(1)} collective-permute-done((s16[2,144,512]{2,1,0:T(8,128)(2,1)S(1)}, s16[2,144,512]{2,1,0:T(8,128)(2,1)S(1)}, u32[]{:S(2)}, u32[]{:S(2)}) %collective-permute-start.9) | collective-permute-done | bytes 294944 | tf_op jit(solution)/shard_map/cond/branch_1_fun/ppermute | solution.py:454
  115.8 3.2 %branch_1_fun.15 = (f32[3,128,512]{2,1,0:T(8,128)}, f32[3,128,512]{2,1,0:T(8,128)}) custom-call(s32[7]{0:T(128)S(1)} %concatenate.49.place_ref, s16[2,144,512]{2,1,0:T(8,128)(2,1)S(1)} %get-tuple-element.72.own_ref, s16[2,144,512]{2,1,0:T(8,128)(2,1)S(1)} %collective-permute-done.9.one_ref, s16[2,144,512]{2,1,0:T(8,128)(2,1)S(1)} %collective-permute-done.10.two_ref, ...), custom_call_target="tpu_custom_call" | custom-call | bytes 5242880 | tf_op jit(solution)/shard_map/cond/branch_1_fun/pallas_call | solution.py:314
  (41 shorter events, 10.9 us)
Async XLA Ops:
  2.7 0.7 copy-start.10
  3.4 18.6 %copy-start.5 = (f32[3,128,512]{2,1,0:T(8,128)S(1)}, f32[3,128,512]{2,1,0:T(8,128)}, u32[]{:S(2)}) copy-start(f32[3,128,512]{2,1,0:T(8,128)} %get-tuple-element.54.left_ref) | copy-start | bytes 2359300 | tf_op jit(solution)/shard_map/cond
  6.1 35.8 %all-to-all-start.4 = ((bf16[16,16,4,128]{3,2,1,0:T(4,128)(2,1)}), bf16[16,16,4,128]{3,2,1,0:T(4,128)(2,1)S(1)}, u32[]{:S(2)}, u32[]{:S(2)}) async-start(bf16[16,16,4,128]{3,2,1,0:T(4,128)(2,1)} %branch_1_fun.8), calls=%async_computation.4 | async-start | bytes 524288 | tf_op jit(solution)/shard_map/cond/branch_1_fun/all_to_all | solution.py:28
  23.1 14.0 %collective-permute-start.8 = (f32[2,128,256]{2,1,0:T(8,128)S(1)}, f32[2,128,256]{2,1,0:T(8,128)S(1)}, u32[]{:S(2)}, u32[]{:S(2)}) collective-permute-start(f32[2,128,256]{2,1,0:T(8,128)S(1)} %maximum_maximum_fusion.3), channel_id=1, source_target_pairs={{0,1},{1,2},{2,3},{3,0},{4,5},{5,6},{6,7},{7,4},{8,9},{9,10},{10,1... | collective-permute-start | bytes 786440 | tf_op jit(solution)/shard_map/cond/branch_1_fun/ppermute | solution.py:419
  26.3 10.8 %collective-permute-start.7 = (f32[2,128,128]{2,1,0:T(8,128)S(1)}, f32[2,128,128]{2,1,0:T(8,128)S(1)}, u32[]{:S(2)}, u32[]{:S(2)}) collective-permute-start(f32[2,128,128]{2,1,0:T(8,128)S(1)} %pad_maximum_fusion.1), channel_id=1, source_target_pairs={{0,2},{1,3},{2,0},{3,1},{4,6},{5,7},{6,4},{7,5},{8,10},{9,11},{10,... | collective-permute-start | bytes 393224 | tf_op jit(solution)/shard_map/cond/branch_1_fun/ppermute | solution.py:419
  30.9 11.0 %collective-permute-start.6 = (f32[2,128,384]{2,1,0:T(8,128)S(1)}, f32[2,128,384]{2,1,0:T(8,128)S(1)}, u32[]{:S(2)}, u32[]{:S(2)}) collective-permute-start(f32[2,128,384]{2,1,0:T(8,128)S(1)} %maximum_maximum_fusion.2), channel_id=1, source_target_pairs={{0,3},{1,0},{2,1},{3,2},{4,7},{5,4},{6,5},{7,6},{8,11},{9,8},{10,9... | collective-permute-start | bytes 1179656 | tf_op jit(solution)/shard_map/cond/branch_1_fun/ppermute | solution.py:419
  43.4 19.9 %all-to-all-start.5 = ((bf16[32,64,128]{2,1,0:T(8,128)(2,1)}), bf16[32,64,128]{2,1,0:T(8,128)(2,1)S(1)}, u32[]{:S(2)}, u32[]{:S(2)}) async-start(bf16[32,64,128]{2,1,0:T(8,128)(2,1)} %bitcast.15), calls=%async_computation.5 | async-start | bytes 1048576 | tf_op jit(solution)/shard_map/cond/branch_1_fun/all_to_all | solution.py:28
  56.3 0.8 copy-start.2
  63.4 1.0 copy-start.3
  68.3 15.9 %all-to-all-start.6 = ((s16[32,17,4,128]{3,2,1,0:T(4,128)(2,1)}), s16[32,17,4,128]{3,2,1,0:T(4,128)(2,1)S(1)}, u32[]{:S(2)}, u32[]{:S(2)}) async-start(s16[32,17,4,128]{3,2,1,0:T(4,128)(2,1)} %branch_1_fun.11), calls=%async_computation.6 | async-start | bytes 1114112 | tf_op jit(solution)/shard_map/cond/branch_1_fun/all_to_all | solution.py:28
  76.3 39.5 %copy-start.7 = (f32[3,128,512]{2,1,0:T(8,128)S(1)}, f32[3,128,512]{2,1,0:T(8,128)}, u32[]{:S(2)}) copy-start(f32[3,128,512]{2,1,0:T(8,128)} %get-tuple-element.76.left_ref) | copy-start | bytes 2359300 | tf_op jit(solution)/shard_map/cond
  85.8 33.2 %all-to-all-start.7 = ((s16[16,17,4,128]{3,2,1,0:T(4,128)(2,1)}), s16[16,17,4,128]{3,2,1,0:T(4,128)(2,1)S(1)}, u32[]{:S(2)}, u32[]{:S(2)}) async-start(s16[16,17,4,128]{3,2,1,0:T(4,128)(2,1)} %branch_1_fun.13), calls=%async_computation.7 | async-start | bytes 557056 | tf_op jit(solution)/shard_map/cond/branch_1_fun/all_to_all | solution.py:28
  97.2 10.6 %collective-permute-start.10 = (s16[2,144,512]{2,1,0:T(8,128)(2,1)S(1)}, s16[2,144,512]{2,1,0:T(8,128)(2,1)S(1)}, u32[]{:S(2)}, u32[]{:S(2)}) collective-permute-start(s16[2,144,512]{2,1,0:T(8,128)(2,1)S(1)} %get-tuple-element.74), channel_id=1, source_target_pairs={{0,2},{1,3},{2,0},{3,1},{4,6},{5,7},{6,4},{7,5},{8,10},{9,11},{10,... | collective-permute-start | bytes 884744 | tf_op jit(solution)/shard_map/cond/branch_1_fun/ppermute | solution.py:454
  100.2 13.4 %collective-permute-start.11 = (s16[2,144,512]{2,1,0:T(8,128)(2,1)S(1)}, s16[2,144,512]{2,1,0:T(8,128)(2,1)S(1)}, u32[]{:S(2)}, u32[]{:S(2)}) collective-permute-start(s16[2,144,512]{2,1,0:T(8,128)(2,1)S(1)} %get-tuple-element.75), channel_id=1, source_target_pairs={{0,3},{1,0},{2,1},{3,2},{4,7},{5,4},{6,5},{7,6},{8,11},{9,8},{10,9... | collective-permute-start | bytes 884744 | tf_op jit(solution)/shard_map/cond/branch_1_fun/ppermute | solution.py:454
  104.1 11.7 %collective-permute-start.9 = (s16[2,144,512]{2,1,0:T(8,128)(2,1)S(1)}, s16[2,144,512]{2,1,0:T(8,128)(2,1)S(1)}, u32[]{:S(2)}, u32[]{:S(2)}) collective-permute-start(s16[2,144,512]{2,1,0:T(8,128)(2,1)S(1)} %get-tuple-element.73), channel_id=1, source_target_pairs={{0,1},{1,2},{2,3},{3,0},{4,5},{5,6},{6,7},{7,4},{8,9},{9,10},{10,1... | collective-permute-start | bytes 884744 | tf_op jit(solution)/shard_map/cond/branch_1_fun/ppermute | solution.py:454
  120.4 0.7 copy-start.9

commit v7 on v5

--- a/solution.py
+++ b/solution.py
@@ -44,12 +44,15 @@
 dot = functools.partial(lax.dot_general, preferred_element_type=jnp.float32)
 
 
-def pack_kernel(owner_ref, grad_ref, packed_ref, count_ref):
+def pack_kernel(owner_ref, far_grad_ref, packed_ref, count_ref, grad_ref, sem):
     blocks = grad_ref.shape[0]
     slots = packed_ref.shape[0] // blocks
+    copy = pltpu.make_async_copy(far_grad_ref, grad_ref, sem)
+    copy.start()
     packed_ref[...] = jnp.zeros_like(packed_ref)
     for owner in range(blocks):
         count_ref[owner] = 0
+    copy.wait()
     for b in range(blocks):
         owner = owner_ref[b]
         rank = count_ref[owner]
@@ -65,14 +68,18 @@
         grid_spec=pltpu.PrefetchScalarGridSpec(
             num_scalar_prefetch=1,
             grid=(1,),
-            in_specs=[whole(gradient.shape)],
+            in_specs=[pl.BlockSpec(memory_space=pltpu.HBM)],
             out_specs=whole(packed),
-            scratch_shapes=[pltpu.SMEM((blocks,), jnp.int32)],
+            scratch_shapes=[
+                pltpu.SMEM((blocks,), jnp.int32),
+                pltpu.VMEM(gradient.shape, gradient.dtype),
+                pltpu.SemaphoreType.DMA,
+            ],
         ),
         out_shape=jax.ShapeDtypeStruct(packed, gradient.dtype),
         compiler_params=pltpu.CompilerParams(vmem_limit_bytes=16 * 1024 * 1024),
         cost_estimate=pl.CostEstimate(flops=0, bytes_accessed=1 << 20, transcendentals=0),
-    )(owner_map, gradient)
+    )(pltpu.with_memory_space_constraint(owner_map, pltpu.HBM), pltpu.with_memory_space_constraint(gradient, pltpu.HBM))
 
 
 def fan_kernel(plane_ref, fan_ref):
@@ -129,15 +136,14 @@
 
     spread(0, left_ref, high_ref, low_ref)
     spread(1, right_ref, right_high_ref, right_low_ref)
-    row = lax.broadcasted_iota(jnp.int32, (width, width), 0)
-    col = lax.broadcasted_iota(jnp.int32, (width, width), 1)
-    z = lax.shift_right_logical(row, 2) & (parts - 1)
-    source = z * (width // parts) + lax.shift_right_logical(row, 4) * 4 + (row & 3)
+    size = high_ref.shape[0]
+    row = lax.broadcasted_iota(jnp.int32, (size, size), 0)
+    col = lax.broadcasted_iota(jnp.int32, (size, size), 1)
+    z = lax.shift_right_logical(row, 2) & (far - 1)
+    source = z * (size // far) + lax.shift_right_logical(row, 6) * 4 + (row & 3)
     order = jnp.where(col == source, 1.0, 0.0).astype(jnp.bfloat16)
-    for m in range(parts):
-        cols = slice(m * width, (m + 1) * width)
-        left_high_ref[:, cols] = dot(high_ref[:, cols], order, nt).astype(jnp.bfloat16)
-        left_low_ref[:, cols] = dot(low_ref[:, cols], order, nt).astype(jnp.bfloat16)
+    left_high_ref[...] = dot(high_ref[...], order, nt).astype(jnp.bfloat16)
+    left_low_ref[...] = dot(low_ref[...], order, nt).astype(jnp.bfloat16)
 
 
 def whole(shape):
@@ -188,18 +194,18 @@
 
 
 def precondition_kernel(
-    place_ref, grad_ref, left_high_ref, left_low_ref, right_high_ref, right_low_ref, message_ref
+    place_ref, grad_ref, left_high_ref, left_low_ref, right_high_ref, right_low_ref, message_ref, late_ref, sem
 ):
     order = left_high_ref.shape[0]
-    deep = grad_ref.shape[2] // parts
-    rows = [(device, slice(m * deep, (m + 1) * deep)) for m in range(parts) for device in range(near)]
-    grad = jnp.concatenate(
-        [jnp.concatenate([grad_ref[device, m, at] for device, at in rows], axis=0) for m in range(parts)], axis=1
-    )
+    late = pltpu.make_async_copy(right_low_ref, late_ref, sem)
+    late.start()
+    grad = jnp.concatenate([grad_ref[:, m].reshape(order, -1) for m in range(parts)], axis=1)
     half = dot(left_high_ref[...], grad, nn) + dot(left_low_ref[...], grad, nn)
     half_high, half_low = split_two(half)
     right_high = right_high_ref[...]
-    result = dot(half_high, right_high, nn) + dot(half_low, right_high, nn) + dot(half_high, right_low_ref[...], nn)
+    result = dot(half_high, right_high, nn) + dot(half_low, right_high, nn)
+    late.wait()
+    result += dot(half_high, late_ref[...], nn)
     taken = place_ref[3]
     result = jnp.where(taken > 0, result, 0.0)
     top = jnp.maximum(jnp.max(jnp.abs(result)), 1e-30)
@@ -244,13 +250,14 @@
         grid_spec=pltpu.PrefetchScalarGridSpec(
             num_scalar_prefetch=1,
             grid=(1,),
-            in_specs=[whole(landed.shape)] + [whole((order, order))] * 4,
+            in_specs=[whole(landed.shape)] + [whole((order, order))] * 3 + [pl.BlockSpec(memory_space=pltpu.HBM)],
             out_specs=whole(message),
+            scratch_shapes=[pltpu.VMEM((order, order), jnp.bfloat16), pltpu.SemaphoreType.DMA],
         ),
         out_shape=jax.ShapeDtypeStruct(message, jnp.int16),
         compiler_params=pltpu.CompilerParams(vmem_limit_bytes=32 * 1024 * 1024),
         cost_estimate=pl.CostEstimate(flops=10 * order**3, bytes_accessed=4 << 20, transcendentals=0),
-    )(place, landed, *roots)
+    )(place, landed, *roots[:3], pltpu.with_memory_space_constraint(roots[3], pltpu.HBM))
 
 
 def terms_kernel(place_ref, block_ref, own_ref, one_ref, two_ref, three_ref, term_ref):
@@ -439,11 +446,10 @@
     back = exchange(message, ("fsdp", "mp"), plane_groups)
 
     block = landed.reshape(near, parts, far, row_share, col_share).transpose(2, 0, 3, 1, 4)
-    made = terms(place, block.reshape(block_size, block_size))
-    back, own_terms, *other_terms = lax.optimization_barrier((back, *made))
-    coded_terms = [own_terms]
-    for k, other in enumerate(other_terms, 1):
-        coded_terms.append(lax.ppermute(other, "mp", [(i, (i + k) % parts) for i in range(parts)]))
+    own_terms, *made = terms(place, block.reshape(block_size, block_size))
+    send_on = lambda k: lax.ppermute(made[k - 1], "mp", [(i, (i + k) % parts) for i in range(parts)])
+    back, *made[1:], own_terms, next_terms = lax.optimization_barrier((back, *made[1:], own_terms, send_on(1)))
+    coded_terms = [own_terms, next_terms] + [send_on(k) for k in range(2, parts)]
     arrived = exchange(repack(back, capacity), "fsdp", far_groups)
     left_new, right_new = new_stats(place, coded_terms, left_stats, right_stats)
 

time: 122 us -> 127 us (1.041)
  waiting for transfers between devices: 34.7 us -> 41.1 us
  local copies, waits for them, and re-layouts: 8.4 us -> 5.79 us
  Pallas kernels: 15.7 us -> 18.1 us
    ppermute x3, waiting for transfers between devices: 10.8 us -> 19.6 us  [on_device(): lax.ppermute(made[k - 1], 'mp', [(i, (i + k) % parts) for i in range(part...]
    unnamed x27 -> x21, local copies, waits for them, and re-layouts: 5.81 us -> 3.14 us
    all_to_all x4, waiting for transfers between devices: 16.6 us -> 14.3 us  [exchange(): lax.all_to_all(array, axis_name, split_axis=0, concat_axis=0, axis_index_...]
  transfers between devices with their start and end apart: 10 -> 10, of which waited for: 8 -> 7; matrix products, arithmetic and copies ran while one was open for 3% -> 2% of each run, Pallas kernels for 5% -> 5%
where the time goes in v7:
time: 127 us; the launch traced here: 126 us
  starting transfers between devices  59.1 us (47%)
  waiting for transfers between devices  41.1 us (32%)
  Pallas kernels  18.1 us (14%)
  local copies, waits for them, and re-layouts  5.79 us (5%)
  between operations  1.6 us (1%)
    all_to_all x4, starting transfers between devices, exchange(): lax.all_to_all(array, axis_name, split_axis=0, concat_axis=0, axis_index_...  38.6 us
    ppermute x3, waiting for transfers between devices, on_device(): lax.ppermute(made[k - 1], 'mp', [(i, (i + k) % parts) for i in range(part...  19.6 us
    all_to_all x4, waiting for transfers between devices, exchange(): lax.all_to_all(array, axis_name, split_axis=0, concat_axis=0, axis_index_...  14.3 us
    ppermute x3, starting transfers between devices, send(): return lax.ppermute(jnp.concatenate(rows, axis=0), 'mp', pairs)  11.1 us
    ppermute x3, starting transfers between devices, on_device(): lax.ppermute(made[k - 1], 'mp', [(i, (i + k) % parts) for i in range(part...  9.48 us
    ppermute x3, waiting for transfers between devices, send(): return lax.ppermute(jnp.concatenate(rows, axis=0), 'mp', pairs)  7.24 us
    pallas_call x1, Pallas kernels, precondition(): pl.pallas_call(precondition_kernel, grid_spec=pltpu.PrefetchScalarGridSpe...  4.92 us
    unnamed x21, local copies, waits for them, and re-layouts  3.14 us
  transfers between devices with their start and end apart: 10, of which 7 were waited for; matrix products, arithmetic and copies ran while one was open for 2% of the time, Pallas kernels for 5%

profile of v7, /device:TPU:6, one launch (start us, length us, event | category | flops | bytes accessed | tf_op | source)
XLA Modules:
  0.0 126.3 jit_solution(12255249281036415064)
XLA Ops:
  0.6 3.0 %shard_map.85 = bf16[384,4,128]{2,1,0:T(4,128)(2,1)} custom-call(s32[128]{0:T(128)} %owner_ref.1, bf16[128,4,128]{2,1,0:T(4,128)(2,1)} %far_grad_ref.1), custom_call_target="tpu_custom_call" | custom-call | bytes 1048576 | tf_op jit(solution)/shard_map/pallas_call | solution.py:66
  3.6 15.2 %all-to-all-start = ((bf16[16,8,3,4,128]{4,3,2,1,0:T(4,128)(2,1)}), bf16[16,8,3,4,128]{4,3,2,1,0:T(4,128)(2,1)S(1)}, u32[]{:S(2)}, u32[]{:S(2)}) async-start(bf16[16,8,3,4,128]{4,3,2,1,0:T(4,128)(2,1)} %bitcast), calls=%async_computation | async-start | bytes 786432 | tf_op jit(solution)/shard_map/all_to_all | solution.py:31
  18.9 1.1 constant_dynamic-slice_fusion.1
  20.1 5.1 %collective-permute-start = (f32[2,128,384]{2,1,0:T(8,128)S(1)}, f32[2,128,384]{2,1,0:T(8,128)S(1)}, u32[]{:S(2)}, u32[]{:S(2)}) collective-permute-start(f32[2,128,384]{2,1,0:T(8,128)S(1)} %maximum_maximum_fusion), channel_id=1, source_target_pairs={{0,3},{1,0},{2,1},{3,2},{4,7},{5,4},{6,5},{7,6},{8,11},{9,8},{10,9... | collective-permute-start | bytes 1179656 | tf_op jit(solution)/shard_map/ppermute | solution.py:424
  25.2 1.9 %collective-permute-start.2 = (f32[2,128,256]{2,1,0:T(8,128)S(1)}, f32[2,128,256]{2,1,0:T(8,128)S(1)}, u32[]{:S(2)}, u32[]{:S(2)}) collective-permute-start(f32[2,128,256]{2,1,0:T(8,128)S(1)} %maximum_maximum_fusion.1), channel_id=1, source_target_pairs={{0,1},{1,2},{2,3},{3,0},{4,5},{5,6},{6,7},{7,4},{8,9},{9,10},{10,1... | collective-permute-start | bytes 786440 | tf_op jit(solution)/shard_map/ppermute | solution.py:424
  27.1 4.1 %collective-permute-start.1 = (f32[2,128,128]{2,1,0:T(8,128)S(1)}, f32[2,128,128]{2,1,0:T(8,128)S(1)}, u32[]{:S(2)}, u32[]{:S(2)}) collective-permute-start(f32[2,128,128]{2,1,0:T(8,128)S(1)} %pad_maximum_fusion), channel_id=1, source_target_pairs={{0,2},{1,3},{2,0},{3,1},{4,6},{5,7},{6,4},{7,5},{8,10},{9,11},{10,... | collective-permute-start | bytes 393224 | tf_op jit(solution)/shard_map/ppermute | solution.py:424
  31.3 6.3 %collective-permute-done.1.two_ref = f32[2,128,128]{2,1,0:T(8,128)S(1)} collective-permute-done((f32[2,128,128]{2,1,0:T(8,128)S(1)}, f32[2,128,128]{2,1,0:T(8,128)S(1)}, u32[]{:S(2)}, u32[]{:S(2)}) %collective-permute-start.1) | collective-permute-done | bytes 131104 | tf_op jit(solution)/shard_map/ppermute | solution.py:424
  38.6 1.7 %shard_map.86 = (bf16[512,512]{1,0:T(8,128)(2,1)S(1)}, bf16[512,512]{1,0:T(8,128)(2,1)S(1)}, bf16[512,512]{1,0:T(8,128)(2,1)S(1)}, bf16[512,512]{1,0:T(8,128)(2,1)S(1)}) custom-call(s32[3]{0:T(128)S(1)} %pad_add_fusion.place_ref, f32[3,128,512]{2,1,0:T(8,128)S(1)} %copy-done, f32[3,128,512]{2,1,0:T(8,128)S(1)} %copy-done.1, ...), custom_call_target="tpu_custom_call" | custom-call | bytes 5242880 | tf_op jit(solution)/shard_map/pallas_call | solution.py:157
  42.7 1.0 shard_map.87
  43.6 7.7 %all-to-all-start.1 = ((bf16[32,64,128]{2,1,0:T(8,128)(2,1)}), bf16[32,64,128]{2,1,0:T(8,128)(2,1)S(1)}, u32[]{:S(2)}, u32[]{:S(2)}) async-start(bf16[32,64,128]{2,1,0:T(8,128)(2,1)} %bitcast.4), calls=%async_computation.1 | async-start | bytes 1048576 | tf_op jit(solution)/shard_map/all_to_all | solution.py:31
  53.8 7.2 %all-to-all-done.1 = bf16[32,64,128]{2,1,0:T(8,128)(2,1)S(1)} async-done(((bf16[32,64,128]{2,1,0:T(8,128)(2,1)}), bf16[32,64,128]{2,1,0:T(8,128)(2,1)S(1)}, u32[]{:S(2)}, u32[]{:S(2)}) %all-to-all-start.1) | async-done | bytes 524320 | tf_op jit(solution)/shard_map/all_to_all | solution.py:31
  61.0 4.9 %shard_map.88 = s16[32,17,4,128]{3,2,1,0:T(4,128)(2,1)} custom-call(s32[7]{0:T(128)S(1)} %concatenate.32.place_ref, bf16[8,4,64,128]{3,2,1,0:T(8,128)(2,1)S(1)} %bitcast.16, bf16[512,512]{1,0:T(8,128)(2,1)S(1)} %get-tuple-element.32.left_high_ref, bf16[512,512]{1,0:T(8,128)(2,1)S(1)} %copy-done.5, bf16[512,512]{1,0:T(8,128)(2,1)S(1)} %copy-done.7, ...), custom_call_target="tpu_custom_call" | custom-call | flops 1342177280 | bytes 4194304 | tf_op jit(solution)/shard_map/pallas_call | solution.py:248
  65.9 6.0 %all-to-all-start.2 = ((s16[32,17,4,128]{3,2,1,0:T(4,128)(2,1)}), s16[32,17,4,128]{3,2,1,0:T(4,128)(2,1)S(1)}, u32[]{:S(2)}, u32[]{:S(2)}) async-start(s16[32,17,4,128]{3,2,1,0:T(4,128)(2,1)} %shard_map.88), calls=%async_computation.2 | async-start | bytes 1114112 | tf_op jit(solution)/shard_map/all_to_all | solution.py:31
  72.7 2.6 %shard_map.89 = (s16[2,144,512]{2,1,0:T(8,128)(2,1)S(1)}, s16[2,144,512]{2,1,0:T(8,128)(2,1)S(1)}, s16[2,144,512]{2,1,0:T(8,128)(2,1)S(1)}, s16[2,144,512]{2,1,0:T(8,128)(2,1)S(1)}) custom-call(s32[7]{0:T(128)S(1)} %concatenate.32.place_ref, bf16[512,512]{1,0:T(8,128)(2,1)S(1)} %bitcast.18), custom_call_target="tpu_custom_call" | custom-call | flops 536870912 | bytes 2097152 | tf_op jit(solution)/shard_map/pallas_call | solution.py:285
  75.3 3.4 %collective-permute-start.3 = (s16[2,144,512]{2,1,0:T(8,128)(2,1)S(1)}, s16[2,144,512]{2,1,0:T(8,128)(2,1)S(1)}, u32[]{:S(2)}, u32[]{:S(2)}) collective-permute-start(s16[2,144,512]{2,1,0:T(8,128)(2,1)S(1)} %get-tuple-element.41), channel_id=1, source_target_pairs={{0,1},{1,2},{2,3},{3,0},{4,5},{5,6},{6,7},{7,4},{8,9},{9,10},{10,1... | collective-permute-start | bytes 884744 | tf_op jit(solution)/shard_map/ppermute | solution.py:450
  78.7 9.6 %collective-permute-done.3.one_ref = s16[2,144,512]{2,1,0:T(8,128)(2,1)S(1)} collective-permute-done((s16[2,144,512]{2,1,0:T(8,128)(2,1)S(1)}, s16[2,144,512]{2,1,0:T(8,128)(2,1)S(1)}, u32[]{:S(2)}, u32[]{:S(2)}) %collective-permute-start.3) | collective-permute-done | bytes 294944 | tf_op jit(solution)/shard_map/ppermute | solution.py:450
  89.3 9.7 %all-to-all-start.3 = ((s16[16,25,4,128]{3,2,1,0:T(4,128)(2,1)}), s16[16,25,4,128]{3,2,1,0:T(4,128)(2,1)S(1)}, u32[]{:S(2)}, u32[]{:S(2)}) async-start(s16[16,25,4,128]{3,2,1,0:T(4,128)(2,1)} %shard_map.90), calls=%async_computation.3 | async-start | bytes 819200 | tf_op jit(solution)/shard_map/all_to_all | solution.py:31
  98.9 3.0 %collective-permute-start.4 = (s16[2,144,512]{2,1,0:T(8,128)(2,1)S(1)}, s16[2,144,512]{2,1,0:T(8,128)(2,1)S(1)}, u32[]{:S(2)}, u32[]{:S(2)}) collective-permute-start(s16[2,144,512]{2,1,0:T(8,128)(2,1)S(1)} %get-tuple-element.45), channel_id=1, source_target_pairs={{0,2},{1,3},{2,0},{3,1},{4,6},{5,7},{6,4},{7,5},{8,10},{9,11},{10,... | collective-permute-start | bytes 884744 | tf_op jit(solution)/shard_map/ppermute | solution.py:450
  102.0 3.1 %collective-permute-start.5 = (s16[2,144,512]{2,1,0:T(8,128)(2,1)S(1)}, s16[2,144,512]{2,1,0:T(8,128)(2,1)S(1)}, u32[]{:S(2)}, u32[]{:S(2)}) collective-permute-start(s16[2,144,512]{2,1,0:T(8,128)(2,1)S(1)} %get-tuple-element.46), channel_id=1, source_target_pairs={{0,3},{1,0},{2,1},{3,2},{4,7},{5,4},{6,5},{7,6},{8,11},{9,8},{10,9... | collective-permute-start | bytes 884744 | tf_op jit(solution)/shard_map/ppermute | solution.py:450
  105.1 6.0 %collective-permute-done.4.two_ref = s16[2,144,512]{2,1,0:T(8,128)(2,1)S(1)} collective-permute-done((s16[2,144,512]{2,1,0:T(8,128)(2,1)S(1)}, s16[2,144,512]{2,1,0:T(8,128)(2,1)S(1)}, u32[]{:S(2)}, u32[]{:S(2)}) %collective-permute-start.4) | collective-permute-done | bytes 294944 | tf_op jit(solution)/shard_map/ppermute | solution.py:450
  111.0 4.0 %collective-permute-done.5.three_ref = s16[2,144,512]{2,1,0:T(8,128)(2,1)S(1)} collective-permute-done((s16[2,144,512]{2,1,0:T(8,128)(2,1)S(1)}, s16[2,144,512]{2,1,0:T(8,128)(2,1)S(1)}, u32[]{:S(2)}, u32[]{:S(2)}) %collective-permute-start.5) | collective-permute-done | bytes 294944 | tf_op jit(solution)/shard_map/ppermute | solution.py:450
  115.0 1.9 %shard_map.92 = (f32[3,128,512]{2,1,0:T(8,128)}, f32[3,128,512]{2,1,0:T(8,128)}) custom-call(s32[7]{0:T(128)S(1)} %concatenate.32.place_ref, s16[2,144,512]{2,1,0:T(8,128)(2,1)S(1)} %get-tuple-element.43.own_ref, s16[2,144,512]{2,1,0:T(8,128)(2,1)S(1)} %collective-permute-done.3.one_ref, s16[2,144,512]{2,1,0:T(8,128)(2,1)S(1)} %collective-permute-done.4.two_ref, ...), custom_call_target="tpu_custom_call" | custom-call | bytes 5242880 | tf_op jit(solution)/shard_map/pallas_call | solution.py:325
  116.9 7.0 %all-to-all-done.3.arrived_ref = s16[16,25,4,128]{3,2,1,0:T(4,128)(2,1)S(1)} async-done(((s16[16,25,4,128]{3,2,1,0:T(4,128)(2,1)}), s16[16,25,4,128]{3,2,1,0:T(4,128)(2,1)S(1)}, u32[]{:S(2)}, u32[]{:S(2)}) %all-to-all-start.3) | async-done | bytes 409632 | tf_op jit(solution)/shard_map/all_to_all | solution.py:31
  124.1 2.2 %shard_map.91 = bf16[128,4,128]{2,1,0:T(4,128)(2,1)} custom-call(s32[128]{0:T(128)S(1)} %get-tuple-element.50.at_ref, s32[128,128]{1,0:T(8,128)S(1)} %broadcast_in_dim.18.spot_ref, s32[128,128]{1,0:T(8,128)S(1)} %broadcast_in_dim.19.up_ref, s16[16,25,4,128]{3,2,1,0:T(4,128)(2,1)S(1)} %all-to-all-done.3.arrived_ref), custom_call_target="tpu_custom_call" | custom-call | bytes 1048576 | tf_op jit(solution)/shard_map/pallas_call | solution.py:391
  (41 shorter events, 7.1 us)
Async XLA Ops:
  0.6 18.3 %copy-start = (f32[3,128,512]{2,1,0:T(8,128)S(1)}, f32[3,128,512]{2,1,0:T(8,128)}, u32[]{:S(2)}) copy-start(f32[3,128,512]{2,1,0:T(8,128)} %left_ref.2) | copy-start | bytes 2359300
  3.6 39.1 %all-to-all-start = ((bf16[16,8,3,4,128]{4,3,2,1,0:T(4,128)(2,1)}), bf16[16,8,3,4,128]{4,3,2,1,0:T(4,128)(2,1)S(1)}, u32[]{:S(2)}, u32[]{:S(2)}) async-start(bf16[16,8,3,4,128]{4,3,2,1,0:T(4,128)(2,1)} %bitcast), calls=%async_computation | async-start | bytes 786432 | tf_op jit(solution)/shard_map/all_to_all | solution.py:31
  20.0 18.5 %copy-start.1 = (f32[3,128,512]{2,1,0:T(8,128)S(1)}, f32[3,128,512]{2,1,0:T(8,128)}, u32[]{:S(2)}) copy-start(f32[3,128,512]{2,1,0:T(8,128)} %right_ref.2) | copy-start | bytes 2359300
  20.1 18.5 %collective-permute-start = (f32[2,128,384]{2,1,0:T(8,128)S(1)}, f32[2,128,384]{2,1,0:T(8,128)S(1)}, u32[]{:S(2)}, u32[]{:S(2)}) collective-permute-start(f32[2,128,384]{2,1,0:T(8,128)S(1)} %maximum_maximum_fusion), channel_id=1, source_target_pairs={{0,3},{1,0},{2,1},{3,2},{4,7},{5,4},{6,5},{7,6},{8,11},{9,8},{10,9... | collective-permute-start | bytes 1179656 | tf_op jit(solution)/shard_map/ppermute | solution.py:424
  25.2 13.4 %collective-permute-start.2 = (f32[2,128,256]{2,1,0:T(8,128)S(1)}, f32[2,128,256]{2,1,0:T(8,128)S(1)}, u32[]{:S(2)}, u32[]{:S(2)}) collective-permute-start(f32[2,128,256]{2,1,0:T(8,128)S(1)} %maximum_maximum_fusion.1), channel_id=1, source_target_pairs={{0,1},{1,2},{2,3},{3,0},{4,5},{5,6},{6,7},{7,4},{8,9},{9,10},{10,1... | collective-permute-start | bytes 786440 | tf_op jit(solution)/shard_map/ppermute | solution.py:424
  27.1 10.5 %collective-permute-start.1 = (f32[2,128,128]{2,1,0:T(8,128)S(1)}, f32[2,128,128]{2,1,0:T(8,128)S(1)}, u32[]{:S(2)}, u32[]{:S(2)}) collective-permute-start(f32[2,128,128]{2,1,0:T(8,128)S(1)} %pad_maximum_fusion), channel_id=1, source_target_pairs={{0,2},{1,3},{2,0},{3,1},{4,6},{5,7},{6,4},{7,5},{8,10},{9,11},{10,... | collective-permute-start | bytes 393224 | tf_op jit(solution)/shard_map/ppermute | solution.py:424
  40.3 0.8 copy-start.4
  41.1 0.8 copy-start.6
  41.9 0.8 copy-start.8
  43.6 17.3 %copy-start.5 = (bf16[512,512]{1,0:T(8,128)(2,1)S(1)}, bf16[512,512]{1,0:T(8,128)(2,1)}, u32[]{:S(2)}) copy-start(bf16[512,512]{1,0:T(8,128)(2,1)} %copy-done.4) | copy-start | bytes 1572868
  43.6 17.3 %copy-start.7 = (bf16[512,512]{1,0:T(8,128)(2,1)S(1)}, bf16[512,512]{1,0:T(8,128)(2,1)}, u32[]{:S(2)}) copy-start(bf16[512,512]{1,0:T(8,128)(2,1)} %copy-done.6) | copy-start | bytes 1572868
  43.6 17.3 %all-to-all-start.1 = ((bf16[32,64,128]{2,1,0:T(8,128)(2,1)}), bf16[32,64,128]{2,1,0:T(8,128)(2,1)S(1)}, u32[]{:S(2)}, u32[]{:S(2)}) async-start(bf16[32,64,128]{2,1,0:T(8,128)(2,1)} %bitcast.4), calls=%async_computation.1 | async-start | bytes 1048576 | tf_op jit(solution)/shard_map/all_to_all | solution.py:31
  51.3 0.7 copy-start.9
  65.9 22.4 %all-to-all-start.2 = ((s16[32,17,4,128]{3,2,1,0:T(4,128)(2,1)}), s16[32,17,4,128]{3,2,1,0:T(4,128)(2,1)S(1)}, u32[]{:S(2)}, u32[]{:S(2)}) async-start(s16[32,17,4,128]{3,2,1,0:T(4,128)(2,1)} %shard_map.88), calls=%async_computation.2 | async-start | bytes 1114112 | tf_op jit(solution)/shard_map/all_to_all | solution.py:31
  75.3 13.0 %collective-permute-start.3 = (s16[2,144,512]{2,1,0:T(8,128)(2,1)S(1)}, s16[2,144,512]{2,1,0:T(8,128)(2,1)S(1)}, u32[]{:S(2)}, u32[]{:S(2)}) collective-permute-start(s16[2,144,512]{2,1,0:T(8,128)(2,1)S(1)} %get-tuple-element.41), channel_id=1, source_target_pairs={{0,1},{1,2},{2,3},{3,0},{4,5},{5,6},{6,7},{7,4},{8,9},{9,10},{10,1... | collective-permute-start | bytes 884744 | tf_op jit(solution)/shard_map/ppermute | solution.py:450
  88.3 26.7 %copy-start.2 = (f32[3,128,512]{2,1,0:T(8,128)S(1)}, f32[3,128,512]{2,1,0:T(8,128)}, u32[]{:S(2)}) copy-start(f32[3,128,512]{2,1,0:T(8,128)} %left_ref.3) | copy-start | bytes 2359300
  88.3 26.7 %copy-start.3 = (f32[3,128,512]{2,1,0:T(8,128)S(1)}, f32[3,128,512]{2,1,0:T(8,128)}, u32[]{:S(2)}) copy-start(f32[3,128,512]{2,1,0:T(8,128)} %right_ref.3) | copy-start | bytes 2359300
  89.3 34.7 %all-to-all-start.3 = ((s16[16,25,4,128]{3,2,1,0:T(4,128)(2,1)}), s16[16,25,4,128]{3,2,1,0:T(4,128)(2,1)S(1)}, u32[]{:S(2)}, u32[]{:S(2)}) async-start(s16[16,25,4,128]{3,2,1,0:T(4,128)(2,1)} %shard_map.90), calls=%async_computation.3 | async-start | bytes 819200 | tf_op jit(solution)/shard_map/all_to_all | solution.py:31
  98.9 12.1 %collective-permute-start.4 = (s16[2,144,512]{2,1,0:T(8,128)(2,1)S(1)}, s16[2,144,512]{2,1,0:T(8,128)(2,1)S(1)}, u32[]{:S(2)}, u32[]{:S(2)}) collective-permute-start(s16[2,144,512]{2,1,0:T(8,128)(2,1)S(1)} %get-tuple-element.45), channel_id=1, source_target_pairs={{0,2},{1,3},{2,0},{3,1},{4,6},{5,7},{6,4},{7,5},{8,10},{9,11},{10,... | collective-permute-start | bytes 884744 | tf_op jit(solution)/shard_map/ppermute | solution.py:450
  102.0 13.0 %collective-permute-start.5 = (s16[2,144,512]{2,1,0:T(8,128)(2,1)S(1)}, s16[2,144,512]{2,1,0:T(8,128)(2,1)S(1)}, u32[]{:S(2)}, u32[]{:S(2)}) collective-permute-start(s16[2,144,512]{2,1,0:T(8,128)(2,1)S(1)} %get-tuple-element.46), channel_id=1, source_target_pairs={{0,3},{1,0},{2,1},{3,2},{4,7},{5,4},{6,5},{7,6},{8,11},{9,8},{10,9... | collective-permute-start | bytes 884744 | tf_op jit(solution)/shard_map/ppermute | solution.py:450

commit v8 on v7

--- a/solution.py
+++ b/solution.py
@@ -144,6 +144,10 @@
     order = jnp.where(col == source, 1.0, 0.0).astype(jnp.bfloat16)
     left_high_ref[...] = dot(high_ref[...], order, nt).astype(jnp.bfloat16)
     left_low_ref[...] = dot(low_ref[...], order, nt).astype(jnp.bfloat16)
+
+
+in_vmem = pl.BlockSpec(memory_space=pltpu.VMEM)
+in_smem = pl.BlockSpec(memory_space=pltpu.SMEM)
 
 
 def whole(shape):
@@ -247,13 +251,9 @@
     message = (near * parts, far + 1, rows // far, width)
     return pl.pallas_call(
         precondition_kernel,
-        grid_spec=pltpu.PrefetchScalarGridSpec(
-            num_scalar_prefetch=1,
-            grid=(1,),
-            in_specs=[whole(landed.shape)] + [whole((order, order))] * 3 + [pl.BlockSpec(memory_space=pltpu.HBM)],
-            out_specs=whole(message),
-            scratch_shapes=[pltpu.VMEM((order, order), jnp.bfloat16), pltpu.SemaphoreType.DMA],
-        ),
+        in_specs=[in_smem] + [in_vmem] * 4 + [pl.BlockSpec(memory_space=pltpu.HBM)],
+        out_specs=in_vmem,
+        scratch_shapes=[pltpu.VMEM((order, order), jnp.bfloat16), pltpu.SemaphoreType.DMA],
         out_shape=jax.ShapeDtypeStruct(message, jnp.int16),
         compiler_params=pltpu.CompilerParams(vmem_limit_bytes=32 * 1024 * 1024),
         cost_estimate=pl.CostEstimate(flops=10 * order**3, bytes_accessed=4 << 20, transcendentals=0),
@@ -390,13 +390,9 @@
     blocks = cell_ids.shape[0]
     return pl.pallas_call(
         finish_kernel,
-        grid_spec=pltpu.PrefetchScalarGridSpec(
-            num_scalar_prefetch=1,
-            grid=(1,),
-            in_specs=[whole(spot.shape), whole(up.shape), whole(arrived.shape)],
-            out_specs=whole((blocks,) + arrived.shape[2:]),
-            scratch_shapes=[pltpu.VMEM((blocks, arrived.shape[3]), jnp.float32)],
-        ),
+        in_specs=[in_smem] + [in_vmem] * 3,
+        out_specs=in_vmem,
+        scratch_shapes=[pltpu.VMEM((blocks, arrived.shape[3]), jnp.float32)],
         out_shape=jax.ShapeDtypeStruct((blocks,) + arrived.shape[2:], jnp.bfloat16),
         compiler_params=pltpu.CompilerParams(vmem_limit_bytes=16 * 1024 * 1024),
         cost_estimate=pl.CostEstimate(flops=0, bytes_accessed=1 << 20, transcendentals=0),
@@ -446,10 +442,10 @@
     back = exchange(message, ("fsdp", "mp"), plane_groups)
 
     block = landed.reshape(near, parts, far, row_share, col_share).transpose(2, 0, 3, 1, 4)
-    own_terms, *made = terms(place, block.reshape(block_size, block_size))
-    send_on = lambda k: lax.ppermute(made[k - 1], "mp", [(i, (i + k) % parts) for i in range(parts)])
-    back, *made[1:], own_terms, next_terms = lax.optimization_barrier((back, *made[1:], own_terms, send_on(1)))
-    coded_terms = [own_terms, next_terms] + [send_on(k) for k in range(2, parts)]
+    own_terms, *other_terms = terms(place, block.reshape(block_size, block_size))
+    coded_terms = [own_terms]
+    for k, other in enumerate(other_terms, 1):
+        coded_terms.append(lax.ppermute(other, "mp", [(i, (i + k) % parts) for i in range(parts)]))
     arrived = exchange(repack(back, capacity), "fsdp", far_groups)
     left_new, right_new = new_stats(place, coded_terms, left_stats, right_stats)
 

time: 127 us -> 122 us (0.961); the launches traced: 126 us -> 120 us
  waiting for transfers between devices: 41.1 us -> 25.3 us
  blocking collectives: 0 us -> 15.7 us
  starting transfers between devices: 59.1 us -> 53.5 us
    all_to_all x0 -> x1, blocking collectives: none -> 15.7 us  [exchange(): lax.all_to_all(array, axis_name, split_axis=0, concat_axis=0, axis_index_...]
    ppermute x3, waiting for transfers between devices: 19.6 us -> 10.8 us  [on_device(): lax.ppermute(other, 'mp', [(i, (i + k) % parts) for i in range(parts)])]
    all_to_all x4 -> x3, waiting for transfers between devices: 14.3 us -> 7.21 us  [exchange(): lax.all_to_all(array, axis_name, split_axis=0, concat_axis=0, axis_index_...]
    all_to_all x4 -> x3, starting transfers between devices: 38.6 us -> 32.5 us  [exchange(): lax.all_to_all(array, axis_name, split_axis=0, concat_axis=0, axis_index_...]
  transfers between devices with their start and end apart: 10 -> 9, of which waited for: 7 -> 5; matrix products, arithmetic and copies ran while one was open for 2% -> 3% of each run, Pallas kernels for 5% -> 5%
where the time goes in v8:
time: 122 us; the launch traced here: 120 us
  starting transfers between devices  53.5 us (44%)
  waiting for transfers between devices  25.3 us (21%)
  Pallas kernels  17.3 us (14%)
  blocking collectives  15.7 us (13%)
  local copies, waits for them, and re-layouts  5.8 us (5%)
  between operations  1.62 us (1%)
    all_to_all x3, starting transfers between devices, exchange(): lax.all_to_all(array, axis_name, split_axis=0, concat_axis=0, axis_index_...  32.5 us
    all_to_all x1, blocking collectives, exchange(): lax.all_to_all(array, axis_name, split_axis=0, concat_axis=0, axis_index_...  15.7 us
    ppermute x3, starting transfers between devices, send(): return lax.ppermute(jnp.concatenate(rows, axis=0), 'mp', pairs)  11.1 us
    ppermute x3, waiting for transfers between devices, on_device(): lax.ppermute(other, 'mp', [(i, (i + k) % parts) for i in range(parts)])  10.8 us
    ppermute x3, starting transfers between devices, on_device(): lax.ppermute(other, 'mp', [(i, (i + k) % parts) for i in range(parts)])  9.85 us
    ppermute x3, waiting for transfers between devices, send(): return lax.ppermute(jnp.concatenate(rows, axis=0), 'mp', pairs)  7.24 us
    all_to_all x3, waiting for transfers between devices, exchange(): lax.all_to_all(array, axis_name, split_axis=0, concat_axis=0, axis_index_...  7.21 us
    pallas_call x1, Pallas kernels, precondition(): pl.pallas_call(precondition_kernel, in_specs=[in_smem] + [in_vmem] * 4 +...  4 us
  transfers between devices with their start and end apart: 9, of which 5 were waited for; matrix products, arithmetic and copies ran while one was open for 3% of the time, Pallas kernels for 5%

profile of v8, /device:TPU:6, one launch (start us, length us, event | category | flops | bytes accessed | tf_op | source)
XLA Modules:
  0.0 119.7 jit_solution(10853669686106481131)
XLA Ops:
  0.6 3.0 %shard_map.85 = bf16[384,4,128]{2,1,0:T(4,128)(2,1)} custom-call(s32[128]{0:T(128)} %owner_ref.1, bf16[128,4,128]{2,1,0:T(4,128)(2,1)} %far_grad_ref.1), custom_call_target="tpu_custom_call" | custom-call | bytes 1048576 | tf_op jit(solution)/shard_map/pallas_call | solution.py:66
  3.6 15.2 %all-to-all-start = ((bf16[16,8,3,4,128]{4,3,2,1,0:T(4,128)(2,1)}), bf16[16,8,3,4,128]{4,3,2,1,0:T(4,128)(2,1)S(1)}, u32[]{:S(2)}, u32[]{:S(2)}) async-start(bf16[16,8,3,4,128]{4,3,2,1,0:T(4,128)(2,1)} %bitcast), calls=%async_computation | async-start | bytes 786432 | tf_op jit(solution)/shard_map/all_to_all | solution.py:31
  18.9 1.1 constant_dynamic-slice_fusion.1
  20.1 5.1 %collective-permute-start = (f32[2,128,384]{2,1,0:T(8,128)S(1)}, f32[2,128,384]{2,1,0:T(8,128)S(1)}, u32[]{:S(2)}, u32[]{:S(2)}) collective-permute-start(f32[2,128,384]{2,1,0:T(8,128)S(1)} %maximum_maximum_fusion), channel_id=1, source_target_pairs={{0,3},{1,0},{2,1},{3,2},{4,7},{5,4},{6,5},{7,6},{8,11},{9,8},{10,9... | collective-permute-start | bytes 1179656 | tf_op jit(solution)/shard_map/ppermute | solution.py:420
  25.2 1.9 %collective-permute-start.2 = (f32[2,128,256]{2,1,0:T(8,128)S(1)}, f32[2,128,256]{2,1,0:T(8,128)S(1)}, u32[]{:S(2)}, u32[]{:S(2)}) collective-permute-start(f32[2,128,256]{2,1,0:T(8,128)S(1)} %maximum_maximum_fusion.1), channel_id=1, source_target_pairs={{0,1},{1,2},{2,3},{3,0},{4,5},{5,6},{6,7},{7,4},{8,9},{9,10},{10,1... | collective-permute-start | bytes 786440 | tf_op jit(solution)/shard_map/ppermute | solution.py:420
  27.1 4.1 %collective-permute-start.1 = (f32[2,128,128]{2,1,0:T(8,128)S(1)}, f32[2,128,128]{2,1,0:T(8,128)S(1)}, u32[]{:S(2)}, u32[]{:S(2)}) collective-permute-start(f32[2,128,128]{2,1,0:T(8,128)S(1)} %pad_maximum_fusion), channel_id=1, source_target_pairs={{0,2},{1,3},{2,0},{3,1},{4,6},{5,7},{6,4},{7,5},{8,10},{9,11},{10,... | collective-permute-start | bytes 393224 | tf_op jit(solution)/shard_map/ppermute | solution.py:420
  31.3 6.3 %collective-permute-done.1.two_ref = f32[2,128,128]{2,1,0:T(8,128)S(1)} collective-permute-done((f32[2,128,128]{2,1,0:T(8,128)S(1)}, f32[2,128,128]{2,1,0:T(8,128)S(1)}, u32[]{:S(2)}, u32[]{:S(2)}) %collective-permute-start.1) | collective-permute-done | bytes 131104 | tf_op jit(solution)/shard_map/ppermute | solution.py:420
  37.7 0.9 collective-permute-done.2.three_ref
  38.6 1.7 %shard_map.86 = (bf16[512,512]{1,0:T(8,128)(2,1)S(1)}, bf16[512,512]{1,0:T(8,128)(2,1)S(1)}, bf16[512,512]{1,0:T(8,128)(2,1)S(1)}, bf16[512,512]{1,0:T(8,128)(2,1)S(1)}) custom-call(s32[3]{0:T(128)S(1)} %pad_add_fusion.place_ref, f32[3,128,512]{2,1,0:T(8,128)S(1)} %copy-done, f32[3,128,512]{2,1,0:T(8,128)S(1)} %copy-done.1, ...), custom_call_target="tpu_custom_call" | custom-call | bytes 5242880 | tf_op jit(solution)/shard_map/pallas_call | solution.py:161
  42.7 1.0 shard_map.87
  43.6 7.7 %all-to-all-start.1 = ((bf16[32,64,128]{2,1,0:T(8,128)(2,1)}), bf16[32,64,128]{2,1,0:T(8,128)(2,1)S(1)}, u32[]{:S(2)}, u32[]{:S(2)}) async-start(bf16[32,64,128]{2,1,0:T(8,128)(2,1)} %bitcast.4), calls=%async_computation.1 | async-start | bytes 1048576 | tf_op jit(solution)/shard_map/all_to_all | solution.py:31
  53.8 7.2 %all-to-all-done.1 = bf16[32,64,128]{2,1,0:T(8,128)(2,1)S(1)} async-done(((bf16[32,64,128]{2,1,0:T(8,128)(2,1)}), bf16[32,64,128]{2,1,0:T(8,128)(2,1)S(1)}, u32[]{:S(2)}, u32[]{:S(2)}) %all-to-all-start.1) | async-done | bytes 524320 | tf_op jit(solution)/shard_map/all_to_all | solution.py:31
  61.0 4.0 %shard_map.88 = s16[32,17,4,128]{3,2,1,0:T(4,128)(2,1)S(1)} custom-call(s32[7]{0:T(128)S(1)} %concatenate.32.place_ref, bf16[8,4,64,128]{3,2,1,0:T(8,128)(2,1)S(1)} %bitcast.16, bf16[512,512]{1,0:T(8,128)(2,1)S(1)} %get-tuple-element.27.left_high_ref, bf16[512,512]{1,0:T(8,128)(2,1)S(1)} %copy-done.5, bf16[512,512]{1,0:T(8,128)(2,1)S(1)} %copy-done.7, ...), custom_call_target="tpu_custom_call" | custom-call | flops 1342177280 | bytes 4194304 | tf_op jit(solution)/shard_map/pallas_call | solution.py:252
  65.0 15.7 %all_to_all.20.back_ref = s16[32,17,4,128]{3,2,1,0:T(4,128)(2,1)S(1)} all-to-all(s16[32,17,4,128]{3,2,1,0:T(4,128)(2,1)S(1)} %shard_map.88), channel_id=1, replica_groups={{0,1,2,3,4,5,6,7,8,9,10,11,12,13,14,15,16,17,18,19,20,21,22,23,24,25,26..., dimensions={0} | all-to-all | bytes 1114112 | tf_op jit(solution)/shard_map/all_to_all | solution.py:31
  80.7 0.9 shard_map.89
  81.6 9.7 %all-to-all-start.3 = ((s16[16,25,4,128]{3,2,1,0:T(4,128)(2,1)}), s16[16,25,4,128]{3,2,1,0:T(4,128)(2,1)S(1)}, u32[]{:S(2)}, u32[]{:S(2)}) async-start(s16[16,25,4,128]{3,2,1,0:T(4,128)(2,1)} %shard_map.89), calls=%async_computation.3 | async-start | bytes 819200 | tf_op jit(solution)/shard_map/all_to_all | solution.py:31
  92.1 2.6 %shard_map.91 = (s16[2,144,512]{2,1,0:T(8,128)(2,1)S(1)}, s16[2,144,512]{2,1,0:T(8,128)(2,1)S(1)}, s16[2,144,512]{2,1,0:T(8,128)(2,1)S(1)}, s16[2,144,512]{2,1,0:T(8,128)(2,1)S(1)}) custom-call(s32[7]{0:T(128)S(1)} %concatenate.32.place_ref, bf16[512,512]{1,0:T(8,128)(2,1)S(1)} %bitcast.18), custom_call_target="tpu_custom_call" | custom-call | flops 536870912 | bytes 2097152 | tf_op jit(solution)/shard_map/pallas_call | solution.py:285
  94.6 2.3 %collective-permute-start.3 = (s16[2,144,512]{2,1,0:T(8,128)(2,1)S(1)}, s16[2,144,512]{2,1,0:T(8,128)(2,1)S(1)}, u32[]{:S(2)}, u32[]{:S(2)}) collective-permute-start(s16[2,144,512]{2,1,0:T(8,128)(2,1)S(1)} %get-tuple-element.34), channel_id=1, source_target_pairs={{0,1},{1,2},{2,3},{3,0},{4,5},{5,6},{6,7},{7,4},{8,9},{9,10},{10,1... | collective-permute-start | bytes 884744 | tf_op jit(solution)/shard_map/ppermute | solution.py:448
  97.0 4.4 %collective-permute-start.4 = (s16[2,144,512]{2,1,0:T(8,128)(2,1)S(1)}, s16[2,144,512]{2,1,0:T(8,128)(2,1)S(1)}, u32[]{:S(2)}, u32[]{:S(2)}) collective-permute-start(s16[2,144,512]{2,1,0:T(8,128)(2,1)S(1)} %get-tuple-element.35), channel_id=1, source_target_pairs={{0,2},{1,3},{2,0},{3,1},{4,6},{5,7},{6,4},{7,5},{8,10},{9,11},{10,... | collective-permute-start | bytes 884744 | tf_op jit(solution)/shard_map/ppermute | solution.py:448
  101.4 3.1 %collective-permute-start.5 = (s16[2,144,512]{2,1,0:T(8,128)(2,1)S(1)}, s16[2,144,512]{2,1,0:T(8,128)(2,1)S(1)}, u32[]{:S(2)}, u32[]{:S(2)}) collective-permute-start(s16[2,144,512]{2,1,0:T(8,128)(2,1)S(1)} %get-tuple-element.36), channel_id=1, source_target_pairs={{0,3},{1,0},{2,1},{3,2},{4,7},{5,4},{6,5},{7,6},{8,11},{9,8},{10,9... | collective-permute-start | bytes 884744 | tf_op jit(solution)/shard_map/ppermute | solution.py:448
  104.5 8.3 %collective-permute-done.3.one_ref = s16[2,144,512]{2,1,0:T(8,128)(2,1)S(1)} collective-permute-done((s16[2,144,512]{2,1,0:T(8,128)(2,1)S(1)}, s16[2,144,512]{2,1,0:T(8,128)(2,1)S(1)}, u32[]{:S(2)}, u32[]{:S(2)}) %collective-permute-start.3) | collective-permute-done | bytes 294944 | tf_op jit(solution)/shard_map/ppermute | solution.py:448
  112.8 2.5 %collective-permute-done.5.three_ref = s16[2,144,512]{2,1,0:T(8,128)(2,1)S(1)} collective-permute-done((s16[2,144,512]{2,1,0:T(8,128)(2,1)S(1)}, s16[2,144,512]{2,1,0:T(8,128)(2,1)S(1)}, u32[]{:S(2)}, u32[]{:S(2)}) %collective-permute-start.5) | collective-permute-done | bytes 294944 | tf_op jit(solution)/shard_map/ppermute | solution.py:448
  115.4 2.0 %shard_map.92 = (f32[3,128,512]{2,1,0:T(8,128)}, f32[3,128,512]{2,1,0:T(8,128)}) custom-call(s32[7]{0:T(128)S(1)} %concatenate.32.place_ref, s16[2,144,512]{2,1,0:T(8,128)(2,1)S(1)} %get-tuple-element.33.own_ref, s16[2,144,512]{2,1,0:T(8,128)(2,1)S(1)} %collective-permute-done.3.one_ref, s16[2,144,512]{2,1,0:T(8,128)(2,1)S(1)} %collective-permute-done.4.two_ref, ...), custom_call_target="tpu_custom_call" | custom-call | bytes 5242880 | tf_op jit(solution)/shard_map/pallas_call | solution.py:325
  117.5 2.2 %shard_map.90 = bf16[128,4,128]{2,1,0:T(4,128)(2,1)} custom-call(s32[128]{0:T(128)S(1)} %get-tuple-element.40.at_ref, s32[128,128]{1,0:T(8,128)S(1)} %broadcast_in_dim.18.spot_ref, s32[128,128]{1,0:T(8,128)S(1)} %broadcast_in_dim.19.up_ref, s16[16,25,4,128]{3,2,1,0:T(4,128)(2,1)S(1)} %all-to-all-done.3.arrived_ref), custom_call_target="tpu_custom_call" | custom-call | bytes 1048576 | tf_op jit(solution)/shard_map/pallas_call | solution.py:391
  (40 shorter events, 5.3 us)
Async XLA Ops:
  0.6 18.3 %copy-start = (f32[3,128,512]{2,1,0:T(8,128)S(1)}, f32[3,128,512]{2,1,0:T(8,128)}, u32[]{:S(2)}) copy-start(f32[3,128,512]{2,1,0:T(8,128)} %left_ref.2) | copy-start | bytes 2359300
  3.6 39.1 %all-to-all-start = ((bf16[16,8,3,4,128]{4,3,2,1,0:T(4,128)(2,1)}), bf16[16,8,3,4,128]{4,3,2,1,0:T(4,128)(2,1)S(1)}, u32[]{:S(2)}, u32[]{:S(2)}) async-start(bf16[16,8,3,4,128]{4,3,2,1,0:T(4,128)(2,1)} %bitcast), calls=%async_computation | async-start | bytes 786432 | tf_op jit(solution)/shard_map/all_to_all | solution.py:31
  20.0 18.5 %copy-start.1 = (f32[3,128,512]{2,1,0:T(8,128)S(1)}, f32[3,128,512]{2,1,0:T(8,128)}, u32[]{:S(2)}) copy-start(f32[3,128,512]{2,1,0:T(8,128)} %right_ref.2) | copy-start | bytes 2359300
  20.1 18.5 %collective-permute-start = (f32[2,128,384]{2,1,0:T(8,128)S(1)}, f32[2,128,384]{2,1,0:T(8,128)S(1)}, u32[]{:S(2)}, u32[]{:S(2)}) collective-permute-start(f32[2,128,384]{2,1,0:T(8,128)S(1)} %maximum_maximum_fusion), channel_id=1, source_target_pairs={{0,3},{1,0},{2,1},{3,2},{4,7},{5,4},{6,5},{7,6},{8,11},{9,8},{10,9... | collective-permute-start | bytes 1179656 | tf_op jit(solution)/shard_map/ppermute | solution.py:420
  25.2 13.4 %collective-permute-start.2 = (f32[2,128,256]{2,1,0:T(8,128)S(1)}, f32[2,128,256]{2,1,0:T(8,128)S(1)}, u32[]{:S(2)}, u32[]{:S(2)}) collective-permute-start(f32[2,128,256]{2,1,0:T(8,128)S(1)} %maximum_maximum_fusion.1), channel_id=1, source_target_pairs={{0,1},{1,2},{2,3},{3,0},{4,5},{5,6},{6,7},{7,4},{8,9},{9,10},{10,1... | collective-permute-start | bytes 786440 | tf_op jit(solution)/shard_map/ppermute | solution.py:420
  27.1 10.5 %collective-permute-start.1 = (f32[2,128,128]{2,1,0:T(8,128)S(1)}, f32[2,128,128]{2,1,0:T(8,128)S(1)}, u32[]{:S(2)}, u32[]{:S(2)}) collective-permute-start(f32[2,128,128]{2,1,0:T(8,128)S(1)} %pad_maximum_fusion), channel_id=1, source_target_pairs={{0,2},{1,3},{2,0},{3,1},{4,6},{5,7},{6,4},{7,5},{8,10},{9,11},{10,... | collective-permute-start | bytes 393224 | tf_op jit(solution)/shard_map/ppermute | solution.py:420
  40.3 0.8 copy-start.4
  41.1 0.8 copy-start.6
  41.9 0.8 copy-start.8
  43.6 17.3 %copy-start.5 = (bf16[512,512]{1,0:T(8,128)(2,1)S(1)}, bf16[512,512]{1,0:T(8,128)(2,1)}, u32[]{:S(2)}) copy-start(bf16[512,512]{1,0:T(8,128)(2,1)} %copy-done.4) | copy-start | bytes 1572868
  43.6 17.4 %copy-start.7 = (bf16[512,512]{1,0:T(8,128)(2,1)S(1)}, bf16[512,512]{1,0:T(8,128)(2,1)}, u32[]{:S(2)}) copy-start(bf16[512,512]{1,0:T(8,128)(2,1)} %copy-done.6) | copy-start | bytes 1572868
  43.6 17.3 %all-to-all-start.1 = ((bf16[32,64,128]{2,1,0:T(8,128)(2,1)}), bf16[32,64,128]{2,1,0:T(8,128)(2,1)S(1)}, u32[]{:S(2)}, u32[]{:S(2)}) async-start(bf16[32,64,128]{2,1,0:T(8,128)(2,1)} %bitcast.4), calls=%async_computation.1 | async-start | bytes 1048576 | tf_op jit(solution)/shard_map/all_to_all | solution.py:31
  51.3 0.7 copy-start.9
  81.6 35.7 %all-to-all-start.3 = ((s16[16,25,4,128]{3,2,1,0:T(4,128)(2,1)}), s16[16,25,4,128]{3,2,1,0:T(4,128)(2,1)S(1)}, u32[]{:S(2)}, u32[]{:S(2)}) async-start(s16[16,25,4,128]{3,2,1,0:T(4,128)(2,1)} %shard_map.89), calls=%async_computation.3 | async-start | bytes 819200 | tf_op jit(solution)/shard_map/all_to_all | solution.py:31
  92.0 23.3 %copy-start.2 = (f32[3,128,512]{2,1,0:T(8,128)S(1)}, f32[3,128,512]{2,1,0:T(8,128)}, u32[]{:S(2)}) copy-start(f32[3,128,512]{2,1,0:T(8,128)} %left_ref.3) | copy-start | bytes 2359300
  92.0 23.3 %copy-start.3 = (f32[3,128,512]{2,1,0:T(8,128)S(1)}, f32[3,128,512]{2,1,0:T(8,128)}, u32[]{:S(2)}) copy-start(f32[3,128,512]{2,1,0:T(8,128)} %right_ref.3) | copy-start | bytes 2359300
  94.6 18.2 %collective-permute-start.3 = (s16[2,144,512]{2,1,0:T(8,128)(2,1)S(1)}, s16[2,144,512]{2,1,0:T(8,128)(2,1)S(1)}, u32[]{:S(2)}, u32[]{:S(2)}) collective-permute-start(s16[2,144,512]{2,1,0:T(8,128)(2,1)S(1)} %get-tuple-element.34), channel_id=1, source_target_pairs={{0,1},{1,2},{2,3},{3,0},{4,5},{5,6},{6,7},{7,4},{8,9},{9,10},{10,1... | collective-permute-start | bytes 884744 | tf_op jit(solution)/shard_map/ppermute | solution.py:448
  97.0 15.8 %collective-permute-start.4 = (s16[2,144,512]{2,1,0:T(8,128)(2,1)S(1)}, s16[2,144,512]{2,1,0:T(8,128)(2,1)S(1)}, u32[]{:S(2)}, u32[]{:S(2)}) collective-permute-start(s16[2,144,512]{2,1,0:T(8,128)(2,1)S(1)} %get-tuple-element.35), channel_id=1, source_target_pairs={{0,2},{1,3},{2,0},{3,1},{4,6},{5,7},{6,4},{7,5},{8,10},{9,11},{10,... | collective-permute-start | bytes 884744 | tf_op jit(solution)/shard_map/ppermute | solution.py:448
  101.4 14.0 %collective-permute-start.5 = (s16[2,144,512]{2,1,0:T(8,128)(2,1)S(1)}, s16[2,144,512]{2,1,0:T(8,128)(2,1)S(1)}, u32[]{:S(2)}, u32[]{:S(2)}) collective-permute-start(s16[2,144,512]{2,1,0:T(8,128)(2,1)S(1)} %get-tuple-element.36), channel_id=1, source_target_pairs={{0,3},{1,0},{2,1},{3,2},{4,7},{5,4},{6,5},{7,6},{8,11},{9,8},{10,9... | collective-permute-start | bytes 884744 | tf_op jit(solution)/shard_map/ppermute | solution.py:448

commit v9 on v8

--- a/solution.py
+++ b/solution.py
@@ -422,10 +422,10 @@
     three = send((0, 3), 1)
     two = send((0,), 2)
     one = send((0, 2, 1), 3)
+    in_plane, one, two, three, owner_map = lax.optimization_barrier((in_plane, one, two, three, owner_map))
     my_slot = jnp.minimum(my_part, capacity - 1)
     place = jnp.stack([my_owner % near, my_part, my_slot])
     roots = spread_roots(place, left_root, right_root, (one, two, three))
-    in_plane, owner_map, *roots = lax.optimization_barrier((in_plane, owner_map, *roots))
 
     fanned = fan(in_plane).reshape(near * parts, far * row_share, col_share)
     landed = exchange(fanned, ("fsdp", "mp"), plane_groups)

time: 122 us -> 120 us (0.984)
  starting transfers between devices: 53.5 us -> 49.6 us
  local copies, waits for them, and re-layouts: 5.8 us -> 7.88 us
    all_to_all x3, starting transfers between devices: 32.5 us -> 28.8 us  [exchange(): lax.all_to_all(array, axis_name, split_axis=0, concat_axis=0, axis_index_...]
    unnamed x21, local copies, waits for them, and re-layouts: 3.14 us -> 5.22 us
  transfers between devices with their start and end apart: 9 -> 9, of which waited for: 5 -> 6; matrix products, arithmetic and copies ran while one was open for 3% -> 3% of each run, Pallas kernels for 5% -> 5%
where the time goes in v9:
time: 120 us; the launch traced here: 118 us
  starting transfers between devices  49.6 us (41%)
  waiting for transfers between devices  25.4 us (21%)
  Pallas kernels  17.2 us (14%)
  blocking collectives  15.6 us (13%)
  local copies, waits for them, and re-layouts  7.88 us (7%)
  between operations  1.6 us (1%)
    all_to_all x3, starting transfers between devices, exchange(): lax.all_to_all(array, axis_name, split_axis=0, concat_axis=0, axis_index_...  28.8 us
    all_to_all x1, blocking collectives, exchange(): lax.all_to_all(array, axis_name, split_axis=0, concat_axis=0, axis_index_...  15.6 us
    ppermute x3, starting transfers between devices, send(): return lax.ppermute(jnp.concatenate(rows, axis=0), 'mp', pairs)  10.9 us
    ppermute x3, waiting for transfers between devices, on_device(): lax.ppermute(other, 'mp', [(i, (i + k) % parts) for i in range(parts)])  10.8 us
    ppermute x3, starting transfers between devices, on_device(): lax.ppermute(other, 'mp', [(i, (i + k) % parts) for i in range(parts)])  9.85 us
    ppermute x3, waiting for transfers between devices, send(): return lax.ppermute(jnp.concatenate(rows, axis=0), 'mp', pairs)  7.29 us
    all_to_all x3, waiting for transfers between devices, exchange(): lax.all_to_all(array, axis_name, split_axis=0, concat_axis=0, axis_index_...  7.25 us
    unnamed x21, local copies, waits for them, and re-layouts  5.22 us
  transfers between devices with their start and end apart: 9, of which 6 were waited for; matrix products, arithmetic and copies ran while one was open for 3% of the time, Pallas kernels for 5%

profile of v9, /device:TPU:6, one launch (start us, length us, event | category | flops | bytes accessed | tf_op | source)
XLA Modules:
  0.0 117.8 jit_solution(8958204427109420058)
XLA Ops:
  0.6 3.0 %shard_map.85 = bf16[384,4,128]{2,1,0:T(4,128)(2,1)} custom-call(s32[128]{0:T(128)} %owner_ref.1, bf16[128,4,128]{2,1,0:T(4,128)(2,1)} %far_grad_ref.1), custom_call_target="tpu_custom_call" | custom-call | bytes 1048576 | tf_op jit(solution)/shard_map/pallas_call | solution.py:66
  3.6 15.2 %all-to-all-start = ((bf16[16,8,3,4,128]{4,3,2,1,0:T(4,128)(2,1)}), bf16[16,8,3,4,128]{4,3,2,1,0:T(4,128)(2,1)S(1)}, u32[]{:S(2)}, u32[]{:S(2)}) async-start(bf16[16,8,3,4,128]{4,3,2,1,0:T(4,128)(2,1)} %bitcast), calls=%async_computation | async-start | bytes 786432 | tf_op jit(solution)/shard_map/all_to_all | solution.py:31
  18.9 1.1 constant_dynamic-slice_fusion.1
  20.1 4.9 %collective-permute-start = (f32[2,128,384]{2,1,0:T(8,128)S(1)}, f32[2,128,384]{2,1,0:T(8,128)S(1)}, u32[]{:S(2)}, u32[]{:S(2)}) collective-permute-start(f32[2,128,384]{2,1,0:T(8,128)S(1)} %maximum_maximum_fusion), channel_id=1, source_target_pairs={{0,3},{1,0},{2,1},{3,2},{4,7},{5,4},{6,5},{7,6},{8,11},{9,8},{10,9... | collective-permute-start | bytes 1179656 | tf_op jit(solution)/shard_map/ppermute | solution.py:420
  25.0 1.9 %collective-permute-start.2 = (f32[2,128,256]{2,1,0:T(8,128)S(1)}, f32[2,128,256]{2,1,0:T(8,128)S(1)}, u32[]{:S(2)}, u32[]{:S(2)}) collective-permute-start(f32[2,128,256]{2,1,0:T(8,128)S(1)} %maximum_maximum_fusion.1), channel_id=1, source_target_pairs={{0,1},{1,2},{2,3},{3,0},{4,5},{5,6},{6,7},{7,4},{8,9},{9,10},{10,1... | collective-permute-start | bytes 786440 | tf_op jit(solution)/shard_map/ppermute | solution.py:420
  27.0 4.1 %collective-permute-start.1 = (f32[2,128,128]{2,1,0:T(8,128)S(1)}, f32[2,128,128]{2,1,0:T(8,128)S(1)}, u32[]{:S(2)}, u32[]{:S(2)}) collective-permute-start(f32[2,128,128]{2,1,0:T(8,128)S(1)} %pad_maximum_fusion), channel_id=1, source_target_pairs={{0,2},{1,3},{2,0},{3,1},{4,6},{5,7},{6,4},{7,5},{8,10},{9,11},{10,... | collective-permute-start | bytes 393224 | tf_op jit(solution)/shard_map/ppermute | solution.py:420
  31.1 6.4 %collective-permute-done.1.two_ref = f32[2,128,128]{2,1,0:T(8,128)S(1)} collective-permute-done((f32[2,128,128]{2,1,0:T(8,128)S(1)}, f32[2,128,128]{2,1,0:T(8,128)S(1)}, u32[]{:S(2)}, u32[]{:S(2)}) %collective-permute-start.1) | collective-permute-done | bytes 131104 | tf_op jit(solution)/shard_map/ppermute | solution.py:420
  38.4 4.2 %all-to-all-done.plane_ref = bf16[16,8,3,4,128]{4,3,2,1,0:T(4,128)(2,1)S(1)} async-done(((bf16[16,8,3,4,128]{4,3,2,1,0:T(4,128)(2,1)}), bf16[16,8,3,4,128]{4,3,2,1,0:T(4,128)(2,1)S(1)}, u32[]{:S(2)}, u32[]{:S(2)}) %all-to-all-start) | async-done | bytes 393248 | tf_op jit(solution)/shard_map/all_to_all | solution.py:31
  43.6 7.6 %all-to-all-start.1 = ((bf16[32,64,128]{2,1,0:T(8,128)(2,1)}), bf16[32,64,128]{2,1,0:T(8,128)(2,1)S(1)}, u32[]{:S(2)}, u32[]{:S(2)}) async-start(bf16[32,64,128]{2,1,0:T(8,128)(2,1)} %bitcast.1), calls=%async_computation.1 | async-start | bytes 1048576 | tf_op jit(solution)/shard_map/all_to_all | solution.py:31
  53.7 1.7 %shard_map.87 = (bf16[512,512]{1,0:T(8,128)(2,1)S(1)}, bf16[512,512]{1,0:T(8,128)(2,1)S(1)}, bf16[512,512]{1,0:T(8,128)(2,1)S(1)}, bf16[512,512]{1,0:T(8,128)(2,1)S(1)}) custom-call(s32[3]{0:T(128)S(1)} %pad_add_fusion.place_ref, f32[3,128,512]{2,1,0:T(8,128)S(1)} %copy-done, f32[3,128,512]{2,1,0:T(8,128)S(1)} %copy-done.1, ...), custom_call_target="tpu_custom_call" | custom-call | bytes 5242880 | tf_op jit(solution)/shard_map/pallas_call | solution.py:161
  57.8 3.1 %all-to-all-done.1 = bf16[32,64,128]{2,1,0:T(8,128)(2,1)S(1)} async-done(((bf16[32,64,128]{2,1,0:T(8,128)(2,1)}), bf16[32,64,128]{2,1,0:T(8,128)(2,1)S(1)}, u32[]{:S(2)}, u32[]{:S(2)}) %all-to-all-start.1) | async-done | bytes 524320 | tf_op jit(solution)/shard_map/all_to_all | solution.py:31
  60.9 1.0 copy-done.5
  61.9 1.0 copy-done.7
  62.9 4.0 %shard_map.88 = s16[32,17,4,128]{3,2,1,0:T(4,128)(2,1)S(1)} custom-call(s32[7]{0:T(128)S(1)} %concatenate.32.place_ref, bf16[8,4,64,128]{3,2,1,0:T(8,128)(2,1)S(1)} %bitcast.16, bf16[512,512]{1,0:T(8,128)(2,1)S(1)} %get-tuple-element.25.left_high_ref, bf16[512,512]{1,0:T(8,128)(2,1)S(1)} %copy-done.5, bf16[512,512]{1,0:T(8,128)(2,1)S(1)} %copy-done.7, ...), custom_call_target="tpu_custom_call" | custom-call | flops 1342177280 | bytes 4194304 | tf_op jit(solution)/shard_map/pallas_call | solution.py:252
  66.9 15.6 %all_to_all.20.back_ref = s16[32,17,4,128]{3,2,1,0:T(4,128)(2,1)S(1)} all-to-all(s16[32,17,4,128]{3,2,1,0:T(4,128)(2,1)S(1)} %shard_map.88), channel_id=1, replica_groups={{0,1,2,3,4,5,6,7,8,9,10,11,12,13,14,15,16,17,18,19,20,21,22,23,24,25,26..., dimensions={0} | all-to-all | bytes 1114112 | tf_op jit(solution)/shard_map/all_to_all | solution.py:31
  83.5 6.0 %all-to-all-start.3 = ((s16[16,25,4,128]{3,2,1,0:T(4,128)(2,1)}), s16[16,25,4,128]{3,2,1,0:T(4,128)(2,1)S(1)}, u32[]{:S(2)}, u32[]{:S(2)}) async-start(s16[16,25,4,128]{3,2,1,0:T(4,128)(2,1)} %shard_map.89), calls=%async_computation.3 | async-start | bytes 819200 | tf_op jit(solution)/shard_map/all_to_all | solution.py:31
  90.3 2.6 %shard_map.91 = (s16[2,144,512]{2,1,0:T(8,128)(2,1)S(1)}, s16[2,144,512]{2,1,0:T(8,128)(2,1)S(1)}, s16[2,144,512]{2,1,0:T(8,128)(2,1)S(1)}, s16[2,144,512]{2,1,0:T(8,128)(2,1)S(1)}) custom-call(s32[7]{0:T(128)S(1)} %concatenate.32.place_ref, bf16[512,512]{1,0:T(8,128)(2,1)S(1)} %bitcast.18), custom_call_target="tpu_custom_call" | custom-call | flops 536870912 | bytes 2097152 | tf_op jit(solution)/shard_map/pallas_call | solution.py:285
  92.9 2.3 %collective-permute-start.3 = (s16[2,144,512]{2,1,0:T(8,128)(2,1)S(1)}, s16[2,144,512]{2,1,0:T(8,128)(2,1)S(1)}, u32[]{:S(2)}, u32[]{:S(2)}) collective-permute-start(s16[2,144,512]{2,1,0:T(8,128)(2,1)S(1)} %get-tuple-element.32), channel_id=1, source_target_pairs={{0,1},{1,2},{2,3},{3,0},{4,5},{5,6},{6,7},{7,4},{8,9},{9,10},{10,1... | collective-permute-start | bytes 884744 | tf_op jit(solution)/shard_map/ppermute | solution.py:448
  95.3 4.4 %collective-permute-start.4 = (s16[2,144,512]{2,1,0:T(8,128)(2,1)S(1)}, s16[2,144,512]{2,1,0:T(8,128)(2,1)S(1)}, u32[]{:S(2)}, u32[]{:S(2)}) collective-permute-start(s16[2,144,512]{2,1,0:T(8,128)(2,1)S(1)} %get-tuple-element.33), channel_id=1, source_target_pairs={{0,2},{1,3},{2,0},{3,1},{4,6},{5,7},{6,4},{7,5},{8,10},{9,11},{10,... | collective-permute-start | bytes 884744 | tf_op jit(solution)/shard_map/ppermute | solution.py:448
  99.7 3.1 %collective-permute-start.5 = (s16[2,144,512]{2,1,0:T(8,128)(2,1)S(1)}, s16[2,144,512]{2,1,0:T(8,128)(2,1)S(1)}, u32[]{:S(2)}, u32[]{:S(2)}) collective-permute-start(s16[2,144,512]{2,1,0:T(8,128)(2,1)S(1)} %get-tuple-element.34), channel_id=1, source_target_pairs={{0,3},{1,0},{2,1},{3,2},{4,7},{5,4},{6,5},{7,6},{8,11},{9,8},{10,9... | collective-permute-start | bytes 884744 | tf_op jit(solution)/shard_map/ppermute | solution.py:448
  102.8 8.3 %collective-permute-done.3.one_ref = s16[2,144,512]{2,1,0:T(8,128)(2,1)S(1)} collective-permute-done((s16[2,144,512]{2,1,0:T(8,128)(2,1)S(1)}, s16[2,144,512]{2,1,0:T(8,128)(2,1)S(1)}, u32[]{:S(2)}, u32[]{:S(2)}) %collective-permute-start.3) | collective-permute-done | bytes 294944 | tf_op jit(solution)/shard_map/ppermute | solution.py:448
  111.1 2.5 %collective-permute-done.5.three_ref = s16[2,144,512]{2,1,0:T(8,128)(2,1)S(1)} collective-permute-done((s16[2,144,512]{2,1,0:T(8,128)(2,1)S(1)}, s16[2,144,512]{2,1,0:T(8,128)(2,1)S(1)}, u32[]{:S(2)}, u32[]{:S(2)}) %collective-permute-start.5) | collective-permute-done | bytes 294944 | tf_op jit(solution)/shard_map/ppermute | solution.py:448
  113.6 1.9 %shard_map.92 = (f32[3,128,512]{2,1,0:T(8,128)}, f32[3,128,512]{2,1,0:T(8,128)}) custom-call(s32[7]{0:T(128)S(1)} %concatenate.32.place_ref, s16[2,144,512]{2,1,0:T(8,128)(2,1)S(1)} %get-tuple-element.31.own_ref, s16[2,144,512]{2,1,0:T(8,128)(2,1)S(1)} %collective-permute-done.3.one_ref, s16[2,144,512]{2,1,0:T(8,128)(2,1)S(1)} %collective-permute-done.4.two_ref, ...), custom_call_target="tpu_custom_call" | custom-call | bytes 5242880 | tf_op jit(solution)/shard_map/pallas_call | solution.py:325
  115.7 2.2 %shard_map.90 = bf16[128,4,128]{2,1,0:T(4,128)(2,1)} custom-call(s32[128]{0:T(128)S(1)} %get-tuple-element.38.at_ref, s32[128,128]{1,0:T(8,128)S(1)} %broadcast_in_dim.18.spot_ref, s32[128,128]{1,0:T(8,128)S(1)} %broadcast_in_dim.19.up_ref, s16[16,25,4,128]{3,2,1,0:T(4,128)(2,1)S(1)} %all-to-all-done.3.arrived_ref), custom_call_target="tpu_custom_call" | custom-call | bytes 1048576 | tf_op jit(solution)/shard_map/pallas_call | solution.py:391
  (40 shorter events, 8.1 us)
Async XLA Ops:
  0.6 18.3 %copy-start = (f32[3,128,512]{2,1,0:T(8,128)S(1)}, f32[3,128,512]{2,1,0:T(8,128)}, u32[]{:S(2)}) copy-start(f32[3,128,512]{2,1,0:T(8,128)} %left_ref.2) | copy-start | bytes 2359300
  3.6 39.0 %all-to-all-start = ((bf16[16,8,3,4,128]{4,3,2,1,0:T(4,128)(2,1)}), bf16[16,8,3,4,128]{4,3,2,1,0:T(4,128)(2,1)S(1)}, u32[]{:S(2)}, u32[]{:S(2)}) async-start(bf16[16,8,3,4,128]{4,3,2,1,0:T(4,128)(2,1)} %bitcast), calls=%async_computation | async-start | bytes 786432 | tf_op jit(solution)/shard_map/all_to_all | solution.py:31
  20.1 18.4 %collective-permute-start = (f32[2,128,384]{2,1,0:T(8,128)S(1)}, f32[2,128,384]{2,1,0:T(8,128)S(1)}, u32[]{:S(2)}, u32[]{:S(2)}) collective-permute-start(f32[2,128,384]{2,1,0:T(8,128)S(1)} %maximum_maximum_fusion), channel_id=1, source_target_pairs={{0,3},{1,0},{2,1},{3,2},{4,7},{5,4},{6,5},{7,6},{8,11},{9,8},{10,9... | collective-permute-start | bytes 1179656 | tf_op jit(solution)/shard_map/ppermute | solution.py:420
  25.0 13.4 %collective-permute-start.2 = (f32[2,128,256]{2,1,0:T(8,128)S(1)}, f32[2,128,256]{2,1,0:T(8,128)S(1)}, u32[]{:S(2)}, u32[]{:S(2)}) collective-permute-start(f32[2,128,256]{2,1,0:T(8,128)S(1)} %maximum_maximum_fusion.1), channel_id=1, source_target_pairs={{0,1},{1,2},{2,3},{3,0},{4,5},{5,6},{6,7},{7,4},{8,9},{9,10},{10,1... | collective-permute-start | bytes 786440 | tf_op jit(solution)/shard_map/ppermute | solution.py:420
  27.0 10.5 %collective-permute-start.1 = (f32[2,128,128]{2,1,0:T(8,128)S(1)}, f32[2,128,128]{2,1,0:T(8,128)S(1)}, u32[]{:S(2)}, u32[]{:S(2)}) collective-permute-start(f32[2,128,128]{2,1,0:T(8,128)S(1)} %pad_maximum_fusion), channel_id=1, source_target_pairs={{0,2},{1,3},{2,0},{3,1},{4,6},{5,7},{6,4},{7,5},{8,10},{9,11},{10,... | collective-permute-start | bytes 393224 | tf_op jit(solution)/shard_map/ppermute | solution.py:420
  31.1 22.6 %copy-start.1 = (f32[3,128,512]{2,1,0:T(8,128)S(1)}, f32[3,128,512]{2,1,0:T(8,128)}, u32[]{:S(2)}) copy-start(f32[3,128,512]{2,1,0:T(8,128)} %right_ref.2) | copy-start | bytes 2359300
  43.6 17.3 %all-to-all-start.1 = ((bf16[32,64,128]{2,1,0:T(8,128)(2,1)}), bf16[32,64,128]{2,1,0:T(8,128)(2,1)S(1)}, u32[]{:S(2)}, u32[]{:S(2)}) async-start(bf16[32,64,128]{2,1,0:T(8,128)(2,1)} %bitcast.1), calls=%async_computation.1 | async-start | bytes 1048576 | tf_op jit(solution)/shard_map/all_to_all | solution.py:31
  51.3 0.7 copy-start.9
  55.4 0.8 copy-start.4
  56.2 0.8 copy-start.6
  57.0 0.8 copy-start.8
  60.9 1.0 copy-start.5
  61.9 1.0 copy-start.7
  83.5 32.0 %all-to-all-start.3 = ((s16[16,25,4,128]{3,2,1,0:T(4,128)(2,1)}), s16[16,25,4,128]{3,2,1,0:T(4,128)(2,1)S(1)}, u32[]{:S(2)}, u32[]{:S(2)}) async-start(s16[16,25,4,128]{3,2,1,0:T(4,128)(2,1)} %shard_map.89), calls=%async_computation.3 | async-start | bytes 819200 | tf_op jit(solution)/shard_map/all_to_all | solution.py:31
  90.3 23.3 %copy-start.2 = (f32[3,128,512]{2,1,0:T(8,128)S(1)}, f32[3,128,512]{2,1,0:T(8,128)}, u32[]{:S(2)}) copy-start(f32[3,128,512]{2,1,0:T(8,128)} %left_ref.3) | copy-start | bytes 2359300
  90.3 23.3 %copy-start.3 = (f32[3,128,512]{2,1,0:T(8,128)S(1)}, f32[3,128,512]{2,1,0:T(8,128)}, u32[]{:S(2)}) copy-start(f32[3,128,512]{2,1,0:T(8,128)} %right_ref.3) | copy-start | bytes 2359300
  92.9 18.2 %collective-permute-start.3 = (s16[2,144,512]{2,1,0:T(8,128)(2,1)S(1)}, s16[2,144,512]{2,1,0:T(8,128)(2,1)S(1)}, u32[]{:S(2)}, u32[]{:S(2)}) collective-permute-start(s16[2,144,512]{2,1,0:T(8,128)(2,1)S(1)} %get-tuple-element.32), channel_id=1, source_target_pairs={{0,1},{1,2},{2,3},{3,0},{4,5},{5,6},{6,7},{7,4},{8,9},{9,10},{10,1... | collective-permute-start | bytes 884744 | tf_op jit(solution)/shard_map/ppermute | solution.py:448
  95.3 15.8 %collective-permute-start.4 = (s16[2,144,512]{2,1,0:T(8,128)(2,1)S(1)}, s16[2,144,512]{2,1,0:T(8,128)(2,1)S(1)}, u32[]{:S(2)}, u32[]{:S(2)}) collective-permute-start(s16[2,144,512]{2,1,0:T(8,128)(2,1)S(1)} %get-tuple-element.33), channel_id=1, source_target_pairs={{0,2},{1,3},{2,0},{3,1},{4,6},{5,7},{6,4},{7,5},{8,10},{9,11},{10,... | collective-permute-start | bytes 884744 | tf_op jit(solution)/shard_map/ppermute | solution.py:448
  99.7 14.0 %collective-permute-start.5 = (s16[2,144,512]{2,1,0:T(8,128)(2,1)S(1)}, s16[2,144,512]{2,1,0:T(8,128)(2,1)S(1)}, u32[]{:S(2)}, u32[]{:S(2)}) collective-permute-start(s16[2,144,512]{2,1,0:T(8,128)(2,1)S(1)} %get-tuple-element.34), channel_id=1, source_target_pairs={{0,3},{1,0},{2,1},{3,2},{4,7},{5,4},{6,5},{7,6},{8,11},{9,8},{10,9... | collective-permute-start | bytes 884744 | tf_op jit(solution)/shard_map/ppermute | solution.py:448

commit v10 on v9

--- a/solution.py
+++ b/solution.py
@@ -198,18 +198,25 @@
 
 
 def precondition_kernel(
-    place_ref, grad_ref, left_high_ref, left_low_ref, right_high_ref, right_low_ref, message_ref, late_ref, sem
+    place_ref, grad_ref, left_high_ref, left_low_ref, right_high_ref, right_low_ref, message_ref, late_ref, sems
 ):
     order = left_high_ref.shape[0]
-    late = pltpu.make_async_copy(right_low_ref, late_ref, sem)
-    late.start()
+    far_refs = (left_low_ref, right_high_ref, right_low_ref)
+    left_late, right_late, last = [
+        pltpu.make_async_copy(far_refs[i], late_ref.at[i], sems.at[i]) for i in range(3)
+    ]
+    for copy in (left_late, right_late, last):
+        copy.start()
     grad = jnp.concatenate([grad_ref[:, m].reshape(order, -1) for m in range(parts)], axis=1)
-    half = dot(left_high_ref[...], grad, nn) + dot(left_low_ref[...], grad, nn)
+    half = dot(left_high_ref[...], grad, nn)
+    left_late.wait()
+    half += dot(late_ref[0], grad, nn)
     half_high, half_low = split_two(half)
-    right_high = right_high_ref[...]
+    right_late.wait()
+    right_high = late_ref[1]
     result = dot(half_high, right_high, nn) + dot(half_low, right_high, nn)
-    late.wait()
-    result += dot(half_high, late_ref[...], nn)
+    last.wait()
+    result += dot(half_high, late_ref[2], nn)
     taken = place_ref[3]
     result = jnp.where(taken > 0, result, 0.0)
     top = jnp.maximum(jnp.max(jnp.abs(result)), 1e-30)
@@ -251,13 +258,13 @@
     message = (near * parts, far + 1, rows // far, width)
     return pl.pallas_call(
         precondition_kernel,
-        in_specs=[in_smem] + [in_vmem] * 4 + [pl.BlockSpec(memory_space=pltpu.HBM)],
+        in_specs=[in_smem] + [in_vmem] * 2 + [pl.BlockSpec(memory_space=pltpu.HBM)] * 3,
         out_specs=in_vmem,
-        scratch_shapes=[pltpu.VMEM((order, order), jnp.bfloat16), pltpu.SemaphoreType.DMA],
+        scratch_shapes=[pltpu.VMEM((3, order, order), jnp.bfloat16), pltpu.SemaphoreType.DMA((3,))],
         out_shape=jax.ShapeDtypeStruct(message, jnp.int16),
         compiler_params=pltpu.CompilerParams(vmem_limit_bytes=32 * 1024 * 1024),
         cost_estimate=pl.CostEstimate(flops=10 * order**3, bytes_accessed=4 << 20, transcendentals=0),
-    )(place, landed, *roots[:3], pltpu.with_memory_space_constraint(roots[3], pltpu.HBM))
+    )(place, landed, roots[0], *(pltpu.with_memory_space_constraint(root, pltpu.HBM) for root in roots[1:]))
 
 
 def terms_kernel(place_ref, block_ref, own_ref, one_ref, two_ref, three_ref, term_ref):
@@ -442,7 +449,8 @@
     back = exchange(message, ("fsdp", "mp"), plane_groups)
 
     block = landed.reshape(near, parts, far, row_share, col_share).transpose(2, 0, 3, 1, 4)
-    own_terms, *other_terms = terms(place, block.reshape(block_size, block_size))
+    made = terms(place, block.reshape(block_size, block_size))
+    back, own_terms, *other_terms = lax.optimization_barrier((back, *made))
     coded_terms = [own_terms]
     for k, other in enumerate(other_terms, 1):
         coded_terms.append(lax.ppermute(other, "mp", [(i, (i + k) % parts) for i in range(parts)]))

time: 120 us -> 119 us (level)
  blocking collectives: 15.6 us -> 0 us
  waiting for transfers between devices: 25.4 us -> 32.8 us
  starting transfers between devices: 49.6 us -> 55.6 us
  Pallas kernels: 17.2 us -> 18.7 us
    all_to_all x1 -> x0, blocking collectives: 15.6 us -> none  [exchange(): lax.all_to_all(array, axis_name, split_axis=0, concat_axis=0, axis_index_...]
    all_to_all x3 -> x4, waiting for transfers between devices: 7.25 us -> 14.5 us  [exchange(): lax.all_to_all(array, axis_name, split_axis=0, concat_axis=0, axis_index_...]
    all_to_all x3 -> x4, starting transfers between devices: 28.8 us -> 34.8 us  [exchange(): lax.all_to_all(array, axis_name, split_axis=0, concat_axis=0, axis_index_...]
    pallas_call x1, Pallas kernels: 4 us -> 5.38 us  [precondition(): pl.pallas_call(precondition_kernel, in_specs=[in_smem] + [in_vmem] * 2 +...]
  transfers between devices with their start and end apart: 9 -> 10, of which waited for: 6 -> 8; matrix products, arithmetic and copies ran while one was open for 3% -> 3% of each run, Pallas kernels for 5% -> 5%
where the time goes in v10:
time: 119 us; the launch traced here: 118 us
  starting transfers between devices  55.6 us (47%)
  waiting for transfers between devices  32.8 us (28%)
  Pallas kernels  18.7 us (16%)
  local copies, waits for them, and re-layouts  7.57 us (6%)
  between operations  1.6 us (1%)
  other arithmetic  1.24 us (1%)
    all_to_all x4, starting transfers between devices, exchange(): lax.all_to_all(array, axis_name, split_axis=0, concat_axis=0, axis_index_...  34.8 us
    all_to_all x4, waiting for transfers between devices, exchange(): lax.all_to_all(array, axis_name, split_axis=0, concat_axis=0, axis_index_...  14.5 us
    ppermute x3, starting transfers between devices, send(): return lax.ppermute(jnp.concatenate(rows, axis=0), 'mp', pairs)  10.9 us
    ppermute x3, waiting for transfers between devices, on_device(): lax.ppermute(other, 'mp', [(i, (i + k) % parts) for i in range(parts)])  10.8 us
    ppermute x3, starting transfers between devices, on_device(): lax.ppermute(other, 'mp', [(i, (i + k) % parts) for i in range(parts)])  9.86 us
    ppermute x3, waiting for transfers between devices, send(): return lax.ppermute(jnp.concatenate(rows, axis=0), 'mp', pairs)  7.5 us
    pallas_call x1, Pallas kernels, precondition(): pl.pallas_call(precondition_kernel, in_specs=[in_smem] + [in_vmem] * 2 +...  5.38 us
    unnamed x21, local copies, waits for them, and re-layouts  4.98 us
  transfers between devices with their start and end apart: 10, of which 8 were waited for; matrix products, arithmetic and copies ran while one was open for 3% of the time, Pallas kernels for 5%

profile of v10, /device:TPU:6, one launch (start us, length us, event | category | flops | bytes accessed | tf_op | source)
XLA Modules:
  0.0 117.5 jit_solution(16198237852619789442)
XLA Ops:
  0.6 3.0 %shard_map.85 = bf16[384,4,128]{2,1,0:T(4,128)(2,1)} custom-call(s32[128]{0:T(128)} %owner_ref.1, bf16[128,4,128]{2,1,0:T(4,128)(2,1)} %far_grad_ref.1), custom_call_target="tpu_custom_call" | custom-call | bytes 1048576 | tf_op jit(solution)/shard_map/pallas_call | solution.py:66
  3.6 15.2 %all-to-all-start = ((bf16[16,8,3,4,128]{4,3,2,1,0:T(4,128)(2,1)}), bf16[16,8,3,4,128]{4,3,2,1,0:T(4,128)(2,1)S(1)}, u32[]{:S(2)}, u32[]{:S(2)}) async-start(bf16[16,8,3,4,128]{4,3,2,1,0:T(4,128)(2,1)} %bitcast), calls=%async_computation | async-start | bytes 786432 | tf_op jit(solution)/shard_map/all_to_all | solution.py:31
  18.9 1.1 constant_dynamic-slice_fusion.1
  20.1 4.9 %collective-permute-start = (f32[2,128,384]{2,1,0:T(8,128)S(1)}, f32[2,128,384]{2,1,0:T(8,128)S(1)}, u32[]{:S(2)}, u32[]{:S(2)}) collective-permute-start(f32[2,128,384]{2,1,0:T(8,128)S(1)} %maximum_maximum_fusion), channel_id=1, source_target_pairs={{0,3},{1,0},{2,1},{3,2},{4,7},{5,4},{6,5},{7,6},{8,11},{9,8},{10,9... | collective-permute-start | bytes 1179656 | tf_op jit(solution)/shard_map/ppermute | solution.py:427
  25.7 1.9 %collective-permute-start.2 = (f32[2,128,256]{2,1,0:T(8,128)}, f32[2,128,256]{2,1,0:T(8,128)S(1)}, u32[]{:S(2)}, u32[]{:S(2)}) collective-permute-start(f32[2,128,256]{2,1,0:T(8,128)} %maximum_maximum_fusion.1), channel_id=1, source_target_pairs={{0,1},{1,2},{2,3},{3,0},{4,5},{5,6},{6,7},{7,4},{8,9},{9,10},{10,1... | collective-permute-start | bytes 786440 | tf_op jit(solution)/shard_map/ppermute | solution.py:427
  27.7 4.1 %collective-permute-start.1 = (f32[2,128,128]{2,1,0:T(8,128)S(1)}, f32[2,128,128]{2,1,0:T(8,128)S(1)}, u32[]{:S(2)}, u32[]{:S(2)}) collective-permute-start(f32[2,128,128]{2,1,0:T(8,128)S(1)} %pad_maximum_fusion), channel_id=1, source_target_pairs={{0,2},{1,3},{2,0},{3,1},{4,6},{5,7},{6,4},{7,5},{8,10},{9,11},{10,... | collective-permute-start | bytes 393224 | tf_op jit(solution)/shard_map/ppermute | solution.py:427
  31.8 6.6 %collective-permute-done.1.two_ref = f32[2,128,128]{2,1,0:T(8,128)S(1)} collective-permute-done((f32[2,128,128]{2,1,0:T(8,128)S(1)}, f32[2,128,128]{2,1,0:T(8,128)S(1)}, u32[]{:S(2)}, u32[]{:S(2)}) %collective-permute-start.1) | collective-permute-done | bytes 131104 | tf_op jit(solution)/shard_map/ppermute | solution.py:427
  39.3 3.3 %all-to-all-done.plane_ref = bf16[16,8,3,4,128]{4,3,2,1,0:T(4,128)(2,1)S(1)} async-done(((bf16[16,8,3,4,128]{4,3,2,1,0:T(4,128)(2,1)}), bf16[16,8,3,4,128]{4,3,2,1,0:T(4,128)(2,1)S(1)}, u32[]{:S(2)}, u32[]{:S(2)}) %all-to-all-start) | async-done | bytes 393248 | tf_op jit(solution)/shard_map/all_to_all | solution.py:31
  43.6 7.6 %all-to-all-start.1 = ((bf16[32,64,128]{2,1,0:T(8,128)(2,1)}), bf16[32,64,128]{2,1,0:T(8,128)(2,1)S(1)}, u32[]{:S(2)}, u32[]{:S(2)}) async-start(bf16[32,64,128]{2,1,0:T(8,128)(2,1)} %bitcast.1), calls=%async_computation.1 | async-start | bytes 1048576 | tf_op jit(solution)/shard_map/all_to_all | solution.py:31
  53.7 1.7 %shard_map.87 = (bf16[512,512]{1,0:T(8,128)(2,1)S(1)}, bf16[512,512]{1,0:T(8,128)(2,1)S(1)}, bf16[512,512]{1,0:T(8,128)(2,1)S(1)}, bf16[512,512]{1,0:T(8,128)(2,1)S(1)}) custom-call(s32[3]{0:T(128)S(1)} %pad_add_fusion.place_ref, f32[3,128,512]{2,1,0:T(8,128)S(1)} %copy-done, f32[3,128,512]{2,1,0:T(8,128)S(1)} %copy-done.1, ...), custom_call_target="tpu_custom_call" | custom-call | bytes 5242880 | tf_op jit(solution)/shard_map/pallas_call | solution.py:161
  58.6 2.3 %all-to-all-done.1 = bf16[32,64,128]{2,1,0:T(8,128)(2,1)S(1)} async-done(((bf16[32,64,128]{2,1,0:T(8,128)(2,1)}), bf16[32,64,128]{2,1,0:T(8,128)(2,1)S(1)}, u32[]{:S(2)}, u32[]{:S(2)}) %all-to-all-start.1) | async-done | bytes 524320 | tf_op jit(solution)/shard_map/all_to_all | solution.py:31
  61.9 5.4 %shard_map.88 = s16[32,17,4,128]{3,2,1,0:T(4,128)(2,1)} custom-call(s32[7]{0:T(128)S(1)} %concatenate.32.place_ref, bf16[8,4,64,128]{3,2,1,0:T(8,128)(2,1)S(1)} %bitcast.16, bf16[512,512]{1,0:T(8,128)(2,1)S(1)} %copy-done.5, bf16[512,512]{1,0:T(8,128)(2,1)} %copy-done.6, bf16[512,512]{1,0:T(8,128)(2,1)} %copy-done.7, bf16[512,512]{1,0:T(8,128)(2,1)} %copy-done.8), custom_call_target="tpu_custom_call" | custom-call | flops 1342177280 | bytes 4194304 | tf_op jit(solution)/shard_map/pallas_call | solution.py:259
  67.3 6.0 %all-to-all-start.2 = ((s16[32,17,4,128]{3,2,1,0:T(4,128)(2,1)}), s16[32,17,4,128]{3,2,1,0:T(4,128)(2,1)S(1)}, u32[]{:S(2)}, u32[]{:S(2)}) async-start(s16[32,17,4,128]{3,2,1,0:T(4,128)(2,1)} %shard_map.88), calls=%async_computation.2 | async-start | bytes 1114112 | tf_op jit(solution)/shard_map/all_to_all | solution.py:31
  74.1 2.6 %shard_map.89 = (s16[2,144,512]{2,1,0:T(8,128)(2,1)S(1)}, s16[2,144,512]{2,1,0:T(8,128)(2,1)S(1)}, s16[2,144,512]{2,1,0:T(8,128)(2,1)S(1)}, s16[2,144,512]{2,1,0:T(8,128)(2,1)S(1)}) custom-call(s32[7]{0:T(128)S(1)} %concatenate.32.place_ref, bf16[512,512]{1,0:T(8,128)(2,1)S(1)} %bitcast.18), custom_call_target="tpu_custom_call" | custom-call | flops 536870912 | bytes 2097152 | tf_op jit(solution)/shard_map/pallas_call | solution.py:292
  76.7 6.5 %all-to-all-done.2.back_ref = s16[32,17,4,128]{3,2,1,0:T(4,128)(2,1)S(1)} async-done(((s16[32,17,4,128]{3,2,1,0:T(4,128)(2,1)}), s16[32,17,4,128]{3,2,1,0:T(4,128)(2,1)S(1)}, u32[]{:S(2)}, u32[]{:S(2)}) %all-to-all-start.2) | async-done | bytes 557088 | tf_op jit(solution)/shard_map/all_to_all | solution.py:31
  84.2 6.0 %all-to-all-start.3 = ((s16[16,25,4,128]{3,2,1,0:T(4,128)(2,1)}), s16[16,25,4,128]{3,2,1,0:T(4,128)(2,1)S(1)}, u32[]{:S(2)}, u32[]{:S(2)}) async-start(s16[16,25,4,128]{3,2,1,0:T(4,128)(2,1)} %shard_map.90), calls=%async_computation.3 | async-start | bytes 819200 | tf_op jit(solution)/shard_map/all_to_all | solution.py:31
  90.2 2.5 %collective-permute-start.3 = (s16[2,144,512]{2,1,0:T(8,128)(2,1)S(1)}, s16[2,144,512]{2,1,0:T(8,128)(2,1)S(1)}, u32[]{:S(2)}, u32[]{:S(2)}) collective-permute-start(s16[2,144,512]{2,1,0:T(8,128)(2,1)S(1)} %get-tuple-element.42), channel_id=1, source_target_pairs={{0,1},{1,2},{2,3},{3,0},{4,5},{5,6},{6,7},{7,4},{8,9},{9,10},{10,1... | collective-permute-start | bytes 884744 | tf_op jit(solution)/shard_map/ppermute | solution.py:456
  92.7 4.2 %collective-permute-start.4 = (s16[2,144,512]{2,1,0:T(8,128)(2,1)S(1)}, s16[2,144,512]{2,1,0:T(8,128)(2,1)S(1)}, u32[]{:S(2)}, u32[]{:S(2)}) collective-permute-start(s16[2,144,512]{2,1,0:T(8,128)(2,1)S(1)} %get-tuple-element.43), channel_id=1, source_target_pairs={{0,2},{1,3},{2,0},{3,1},{4,6},{5,7},{6,4},{7,5},{8,10},{9,11},{10,... | collective-permute-start | bytes 884744 | tf_op jit(solution)/shard_map/ppermute | solution.py:456
  96.9 3.1 %collective-permute-start.5 = (s16[2,144,512]{2,1,0:T(8,128)(2,1)S(1)}, s16[2,144,512]{2,1,0:T(8,128)(2,1)S(1)}, u32[]{:S(2)}, u32[]{:S(2)}) collective-permute-start(s16[2,144,512]{2,1,0:T(8,128)(2,1)S(1)} %get-tuple-element.44), channel_id=1, source_target_pairs={{0,3},{1,0},{2,1},{3,2},{4,7},{5,4},{6,5},{7,6},{8,11},{9,8},{10,9... | collective-permute-start | bytes 884744 | tf_op jit(solution)/shard_map/ppermute | solution.py:456
  100.0 8.3 %collective-permute-done.3.one_ref = s16[2,144,512]{2,1,0:T(8,128)(2,1)S(1)} collective-permute-done((s16[2,144,512]{2,1,0:T(8,128)(2,1)S(1)}, s16[2,144,512]{2,1,0:T(8,128)(2,1)S(1)}, u32[]{:S(2)}, u32[]{:S(2)}) %collective-permute-start.3) | collective-permute-done | bytes 294944 | tf_op jit(solution)/shard_map/ppermute | solution.py:456
  108.3 2.5 %collective-permute-done.5.three_ref = s16[2,144,512]{2,1,0:T(8,128)(2,1)S(1)} collective-permute-done((s16[2,144,512]{2,1,0:T(8,128)(2,1)S(1)}, s16[2,144,512]{2,1,0:T(8,128)(2,1)S(1)}, u32[]{:S(2)}, u32[]{:S(2)}) %collective-permute-start.5) | collective-permute-done | bytes 294944 | tf_op jit(solution)/shard_map/ppermute | solution.py:456
  110.9 2.0 %shard_map.92 = (f32[3,128,512]{2,1,0:T(8,128)}, f32[3,128,512]{2,1,0:T(8,128)}) custom-call(s32[7]{0:T(128)S(1)} %concatenate.32.place_ref, s16[2,144,512]{2,1,0:T(8,128)(2,1)S(1)} %get-tuple-element.41.own_ref, s16[2,144,512]{2,1,0:T(8,128)(2,1)S(1)} %collective-permute-done.3.one_ref, s16[2,144,512]{2,1,0:T(8,128)(2,1)S(1)} %collective-permute-done.4.two_ref, ...), custom_call_target="tpu_custom_call" | custom-call | bytes 5242880 | tf_op jit(solution)/shard_map/pallas_call | solution.py:332
  112.8 2.4 %all-to-all-done.3.arrived_ref = s16[16,25,4,128]{3,2,1,0:T(4,128)(2,1)S(1)} async-done(((s16[16,25,4,128]{3,2,1,0:T(4,128)(2,1)}), s16[16,25,4,128]{3,2,1,0:T(4,128)(2,1)S(1)}, u32[]{:S(2)}, u32[]{:S(2)}) %all-to-all-start.3) | async-done | bytes 409632 | tf_op jit(solution)/shard_map/all_to_all | solution.py:31
  115.4 2.2 %shard_map.91 = bf16[128,4,128]{2,1,0:T(4,128)(2,1)} custom-call(s32[128]{0:T(128)S(1)} %get-tuple-element.48.at_ref, s32[128,128]{1,0:T(8,128)S(1)} %broadcast_in_dim.18.spot_ref, s32[128,128]{1,0:T(8,128)S(1)} %broadcast_in_dim.19.up_ref, s16[16,25,4,128]{3,2,1,0:T(4,128)(2,1)S(1)} %all-to-all-done.3.arrived_ref), custom_call_target="tpu_custom_call" | custom-call | bytes 1048576 | tf_op jit(solution)/shard_map/pallas_call | solution.py:398
  (41 shorter events, 10.5 us)
Async XLA Ops:
  0.6 18.3 %copy-start = (f32[3,128,512]{2,1,0:T(8,128)S(1)}, f32[3,128,512]{2,1,0:T(8,128)}, u32[]{:S(2)}) copy-start(f32[3,128,512]{2,1,0:T(8,128)} %left_ref.2) | copy-start | bytes 2359300
  3.6 39.0 %all-to-all-start = ((bf16[16,8,3,4,128]{4,3,2,1,0:T(4,128)(2,1)}), bf16[16,8,3,4,128]{4,3,2,1,0:T(4,128)(2,1)S(1)}, u32[]{:S(2)}, u32[]{:S(2)}) async-start(bf16[16,8,3,4,128]{4,3,2,1,0:T(4,128)(2,1)} %bitcast), calls=%async_computation | async-start | bytes 786432 | tf_op jit(solution)/shard_map/all_to_all | solution.py:31
  20.1 19.3 %collective-permute-start = (f32[2,128,384]{2,1,0:T(8,128)S(1)}, f32[2,128,384]{2,1,0:T(8,128)S(1)}, u32[]{:S(2)}, u32[]{:S(2)}) collective-permute-start(f32[2,128,384]{2,1,0:T(8,128)S(1)} %maximum_maximum_fusion), channel_id=1, source_target_pairs={{0,3},{1,0},{2,1},{3,2},{4,7},{5,4},{6,5},{7,6},{8,11},{9,8},{10,9... | collective-permute-start | bytes 1179656 | tf_op jit(solution)/shard_map/ppermute | solution.py:427
  25.7 13.6 %collective-permute-start.2 = (f32[2,128,256]{2,1,0:T(8,128)}, f32[2,128,256]{2,1,0:T(8,128)S(1)}, u32[]{:S(2)}, u32[]{:S(2)}) collective-permute-start(f32[2,128,256]{2,1,0:T(8,128)} %maximum_maximum_fusion.1), channel_id=1, source_target_pairs={{0,1},{1,2},{2,3},{3,0},{4,5},{5,6},{6,7},{7,4},{8,9},{9,10},{10,1... | collective-permute-start | bytes 786440 | tf_op jit(solution)/shard_map/ppermute | solution.py:427
  27.7 10.7 %collective-permute-start.1 = (f32[2,128,128]{2,1,0:T(8,128)S(1)}, f32[2,128,128]{2,1,0:T(8,128)S(1)}, u32[]{:S(2)}, u32[]{:S(2)}) collective-permute-start(f32[2,128,128]{2,1,0:T(8,128)S(1)} %pad_maximum_fusion), channel_id=1, source_target_pairs={{0,2},{1,3},{2,0},{3,1},{4,6},{5,7},{6,4},{7,5},{8,10},{9,11},{10,... | collective-permute-start | bytes 393224 | tf_op jit(solution)/shard_map/ppermute | solution.py:427
  31.8 21.8 %copy-start.1 = (f32[3,128,512]{2,1,0:T(8,128)S(1)}, f32[3,128,512]{2,1,0:T(8,128)}, u32[]{:S(2)}) copy-start(f32[3,128,512]{2,1,0:T(8,128)} %right_ref.2) | copy-start | bytes 2359300
  43.6 17.3 %all-to-all-start.1 = ((bf16[32,64,128]{2,1,0:T(8,128)(2,1)}), bf16[32,64,128]{2,1,0:T(8,128)(2,1)S(1)}, u32[]{:S(2)}, u32[]{:S(2)}) async-start(bf16[32,64,128]{2,1,0:T(8,128)(2,1)} %bitcast.1), calls=%async_computation.1 | async-start | bytes 1048576 | tf_op jit(solution)/shard_map/all_to_all | solution.py:31
  51.3 0.7 copy-start.9
  55.4 0.8 copy-start.4
  56.2 0.8 copy-start.6
  57.0 0.8 copy-start.7
  57.8 0.8 copy-start.8
  60.9 1.0 copy-start.5
  67.3 15.9 %all-to-all-start.2 = ((s16[32,17,4,128]{3,2,1,0:T(4,128)(2,1)}), s16[32,17,4,128]{3,2,1,0:T(4,128)(2,1)S(1)}, u32[]{:S(2)}, u32[]{:S(2)}) async-start(s16[32,17,4,128]{3,2,1,0:T(4,128)(2,1)} %shard_map.88), calls=%async_computation.2 | async-start | bytes 1114112 | tf_op jit(solution)/shard_map/all_to_all | solution.py:31
  83.2 27.6 %copy-start.2 = (f32[3,128,512]{2,1,0:T(8,128)S(1)}, f32[3,128,512]{2,1,0:T(8,128)}, u32[]{:S(2)}) copy-start(f32[3,128,512]{2,1,0:T(8,128)} %left_ref.3) | copy-start | bytes 2359300
  83.2 27.6 %copy-start.3 = (f32[3,128,512]{2,1,0:T(8,128)S(1)}, f32[3,128,512]{2,1,0:T(8,128)}, u32[]{:S(2)}) copy-start(f32[3,128,512]{2,1,0:T(8,128)} %right_ref.3) | copy-start | bytes 2359300
  84.2 31.1 %all-to-all-start.3 = ((s16[16,25,4,128]{3,2,1,0:T(4,128)(2,1)}), s16[16,25,4,128]{3,2,1,0:T(4,128)(2,1)S(1)}, u32[]{:S(2)}, u32[]{:S(2)}) async-start(s16[16,25,4,128]{3,2,1,0:T(4,128)(2,1)} %shard_map.90), calls=%async_computation.3 | async-start | bytes 819200 | tf_op jit(solution)/shard_map/all_to_all | solution.py:31
  90.2 18.2 %collective-permute-start.3 = (s16[2,144,512]{2,1,0:T(8,128)(2,1)S(1)}, s16[2,144,512]{2,1,0:T(8,128)(2,1)S(1)}, u32[]{:S(2)}, u32[]{:S(2)}) collective-permute-start(s16[2,144,512]{2,1,0:T(8,128)(2,1)S(1)} %get-tuple-element.42), channel_id=1, source_target_pairs={{0,1},{1,2},{2,3},{3,0},{4,5},{5,6},{6,7},{7,4},{8,9},{9,10},{10,1... | collective-permute-start | bytes 884744 | tf_op jit(solution)/shard_map/ppermute | solution.py:456
  92.7 15.6 %collective-permute-start.4 = (s16[2,144,512]{2,1,0:T(8,128)(2,1)S(1)}, s16[2,144,512]{2,1,0:T(8,128)(2,1)S(1)}, u32[]{:S(2)}, u32[]{:S(2)}) collective-permute-start(s16[2,144,512]{2,1,0:T(8,128)(2,1)S(1)} %get-tuple-element.43), channel_id=1, source_target_pairs={{0,2},{1,3},{2,0},{3,1},{4,6},{5,7},{6,4},{7,5},{8,10},{9,11},{10,... | collective-permute-start | bytes 884744 | tf_op jit(solution)/shard_map/ppermute | solution.py:456
  96.9 14.0 %collective-permute-start.5 = (s16[2,144,512]{2,1,0:T(8,128)(2,1)S(1)}, s16[2,144,512]{2,1,0:T(8,128)(2,1)S(1)}, u32[]{:S(2)}, u32[]{:S(2)}) collective-permute-start(s16[2,144,512]{2,1,0:T(8,128)(2,1)S(1)} %get-tuple-element.44), channel_id=1, source_target_pairs={{0,3},{1,0},{2,1},{3,2},{4,7},{5,4},{6,5},{7,6},{8,11},{9,8},{10,9... | collective-permute-start | bytes 884744 | tf_op jit(solution)/shard_map/ppermute | solution.py:456

commit v11 on v9

--- a/solution.py
+++ b/solution.py
@@ -198,18 +198,21 @@
 
 
 def precondition_kernel(
-    place_ref, grad_ref, left_high_ref, left_low_ref, right_high_ref, right_low_ref, message_ref, late_ref, sem
+    place_ref, grad_ref, left_high_ref, left_low_ref, right_high_ref, right_low_ref, message_ref, late_ref, sems
 ):
     order = left_high_ref.shape[0]
-    late = pltpu.make_async_copy(right_low_ref, late_ref, sem)
+    late = pltpu.make_async_copy(right_high_ref, late_ref.at[0], sems.at[0])
+    last = pltpu.make_async_copy(right_low_ref, late_ref.at[1], sems.at[1])
     late.start()
+    last.start()
     grad = jnp.concatenate([grad_ref[:, m].reshape(order, -1) for m in range(parts)], axis=1)
     half = dot(left_high_ref[...], grad, nn) + dot(left_low_ref[...], grad, nn)
     half_high, half_low = split_two(half)
-    right_high = right_high_ref[...]
+    late.wait()
+    right_high = late_ref[0]
     result = dot(half_high, right_high, nn) + dot(half_low, right_high, nn)
-    late.wait()
-    result += dot(half_high, late_ref[...], nn)
+    last.wait()
+    result += dot(half_high, late_ref[1], nn)
     taken = place_ref[3]
     result = jnp.where(taken > 0, result, 0.0)
     top = jnp.maximum(jnp.max(jnp.abs(result)), 1e-30)
@@ -251,13 +254,13 @@
     message = (near * parts, far + 1, rows // far, width)
     return pl.pallas_call(
         precondition_kernel,
-        in_specs=[in_smem] + [in_vmem] * 4 + [pl.BlockSpec(memory_space=pltpu.HBM)],
+        in_specs=[in_smem] + [in_vmem] * 3 + [pl.BlockSpec(memory_space=pltpu.HBM)] * 2,
         out_specs=in_vmem,
-        scratch_shapes=[pltpu.VMEM((order, order), jnp.bfloat16), pltpu.SemaphoreType.DMA],
+        scratch_shapes=[pltpu.VMEM((2, order, order), jnp.bfloat16), pltpu.SemaphoreType.DMA((2,))],
         out_shape=jax.ShapeDtypeStruct(message, jnp.int16),
         compiler_params=pltpu.CompilerParams(vmem_limit_bytes=32 * 1024 * 1024),
         cost_estimate=pl.CostEstimate(flops=10 * order**3, bytes_accessed=4 << 20, transcendentals=0),
-    )(place, landed, *roots[:3], pltpu.with_memory_space_constraint(roots[3], pltpu.HBM))
+    )(place, landed, *roots[:2], *(pltpu.with_memory_space_constraint(root, pltpu.HBM) for root in roots[2:]))
 
 
 def terms_kernel(place_ref, block_ref, own_ref, one_ref, two_ref, three_ref, term_ref):
@@ -360,8 +363,8 @@
 
 
 def finish_kernel(at_ref, spot_ref, up_ref, arrived_ref, update_ref, factor_ref):
-    cells = arrived_ref.shape[1] - 1
-    facts = [arrived_ref[z, cells].astype(jnp.int32).astype(jnp.float32) for z in range(far)]
+    groups = arrived_ref.shape[0] // far
+    facts = [arrived_ref[z * groups + groups - 1].astype(jnp.int32).astype(jnp.float32) for z in range(far)]
     row = lambda r: jnp.concatenate([fact[r : r + 1] for fact in facts], axis=0)
     sums = jnp.sum(decoded(row(0), row(1), row(2)), axis=0, keepdims=True)
     kind = lax.rem(lax.broadcasted_iota(jnp.int32, sums.shape, 1), 4)
@@ -381,8 +384,7 @@
     factor_ref[...] = jnp.where(up_ref[...] > 0, up_scale, gate_scale) * step
 
     for b in range(update_ref.shape[0]):
-        at = at_ref[b]
-        code = arrived_ref[at // cells, lax.rem(at, cells)].astype(jnp.int32).astype(jnp.float32)
+        code = arrived_ref[at_ref[b]].astype(jnp.int32).astype(jnp.float32)
         update_ref[b] = (code * jnp.abs(code) * factor_ref[b : b + 1, :]).astype(jnp.bfloat16)
 
 
@@ -392,8 +394,8 @@
         finish_kernel,
         in_specs=[in_smem] + [in_vmem] * 3,
         out_specs=in_vmem,
-        scratch_shapes=[pltpu.VMEM((blocks, arrived.shape[3]), jnp.float32)],
-        out_shape=jax.ShapeDtypeStruct((blocks,) + arrived.shape[2:], jnp.bfloat16),
+        scratch_shapes=[pltpu.VMEM((blocks, arrived.shape[2]), jnp.float32)],
+        out_shape=jax.ShapeDtypeStruct((blocks,) + arrived.shape[1:], jnp.bfloat16),
         compiler_params=pltpu.CompilerParams(vmem_limit_bytes=16 * 1024 * 1024),
         cost_estimate=pl.CostEstimate(flops=0, bytes_accessed=1 << 20, transcendentals=0),
     )(cell_ids, spot, up, arrived)
@@ -442,7 +444,8 @@
     back = exchange(message, ("fsdp", "mp"), plane_groups)
 
     block = landed.reshape(near, parts, far, row_share, col_share).transpose(2, 0, 3, 1, 4)
-    own_terms, *other_terms = terms(place, block.reshape(block_size, block_size))
+    made = terms(place, block.reshape(block_size, block_size))
+    back, own_terms, *other_terms = lax.optimization_barrier((back, *made))
     coded_terms = [own_terms]
     for k, other in enumerate(other_terms, 1):
         coded_terms.append(lax.ppermute(other, "mp", [(i, (i + k) % parts) for i in range(parts)]))
@@ -452,7 +455,8 @@
     cells = near * capacity
     spot = cell_ids // cells * 128 + cell_ids % cells // capacity * 16 + cell_ids % capacity * 3
     across = lambda array: jnp.broadcast_to(array.astype(jnp.int32)[:, None], (block_count, 128))
-    update = finish(cell_ids, across(spot), across(up_block), arrived)
+    arrived = arrived.reshape(far * (cells + 1), row_share, col_share)
+    update = finish(cell_ids + cell_ids // cells, across(spot), across(up_block), arrived)
     return (update, left_new, right_new)
 
 

time: 120 us -> 120 us (level)
  blocking collectives: 15.6 us -> 0 us
  waiting for transfers between devices: 25.4 us -> 32.7 us
  starting transfers between devices: 49.6 us -> 55.6 us
    all_to_all x1 -> x0, blocking collectives: 15.6 us -> none  [exchange(): lax.all_to_all(array, axis_name, split_axis=0, concat_axis=0, axis_index_...]
    all_to_all x3 -> x4, waiting for transfers between devices: 7.25 us -> 14.4 us  [exchange(): lax.all_to_all(array, axis_name, split_axis=0, concat_axis=0, axis_index_...]
    all_to_all x3 -> x4, starting transfers between devices: 28.8 us -> 34.8 us  [exchange(): lax.all_to_all(array, axis_name, split_axis=0, concat_axis=0, axis_index_...]
    pallas_call x1, Pallas kernels: 4 us -> 5.24 us  [precondition(): pl.pallas_call(precondition_kernel, in_specs=[in_smem] + [in_vmem] * 3 +...]
    unnamed x21 -> x23, local copies, waits for them, and re-layouts: 5.22 us -> 6.03 us
  transfers between devices with their start and end apart: 9 -> 10, of which waited for: 6 -> 8; matrix products, arithmetic and copies ran while one was open for 3% -> 3% of each run, Pallas kernels for 5% -> 5%
where the time goes in v11:
time: 120 us; the launch traced here: 118 us
  starting transfers between devices  55.6 us (46%)
  waiting for transfers between devices  32.7 us (27%)
  Pallas kernels  18.1 us (15%)
  local copies, waits for them, and re-layouts  8.62 us (7%)
  between operations  1.61 us (1%)
  other arithmetic  1.25 us (1%)
    all_to_all x4, starting transfers between devices, exchange(): lax.all_to_all(array, axis_name, split_axis=0, concat_axis=0, axis_index_...  34.8 us
    all_to_all x4, waiting for transfers between devices, exchange(): lax.all_to_all(array, axis_name, split_axis=0, concat_axis=0, axis_index_...  14.4 us
    ppermute x3, starting transfers between devices, send(): return lax.ppermute(jnp.concatenate(rows, axis=0), 'mp', pairs)  10.9 us
    ppermute x3, waiting for transfers between devices, on_device(): lax.ppermute(other, 'mp', [(i, (i + k) % parts) for i in range(parts)])  10.8 us
    ppermute x3, starting transfers between devices, on_device(): lax.ppermute(other, 'mp', [(i, (i + k) % parts) for i in range(parts)])  9.86 us
    ppermute x3, waiting for transfers between devices, send(): return lax.ppermute(jnp.concatenate(rows, axis=0), 'mp', pairs)  7.5 us
    unnamed x23, local copies, waits for them, and re-layouts  6.03 us
    pallas_call x1, Pallas kernels, precondition(): pl.pallas_call(precondition_kernel, in_specs=[in_smem] + [in_vmem] * 3 +...  5.24 us
  transfers between devices with their start and end apart: 10, of which 8 were waited for; matrix products, arithmetic and copies ran while one was open for 3% of the time, Pallas kernels for 5%

profile of v11, /device:TPU:6, one launch (start us, length us, event | category | flops | bytes accessed | tf_op | source)
XLA Modules:
  0.0 117.9 jit_solution(511345547673394158)
XLA Ops:
  0.6 3.0 %shard_map.85 = bf16[384,4,128]{2,1,0:T(4,128)(2,1)} custom-call(s32[128]{0:T(128)} %owner_ref.1, bf16[128,4,128]{2,1,0:T(4,128)(2,1)} %far_grad_ref.1), custom_call_target="tpu_custom_call" | custom-call | bytes 1048576 | tf_op jit(solution)/shard_map/pallas_call | solution.py:66
  3.6 15.2 %all-to-all-start = ((bf16[16,8,3,4,128]{4,3,2,1,0:T(4,128)(2,1)}), bf16[16,8,3,4,128]{4,3,2,1,0:T(4,128)(2,1)S(1)}, u32[]{:S(2)}, u32[]{:S(2)}) async-start(bf16[16,8,3,4,128]{4,3,2,1,0:T(4,128)(2,1)} %bitcast), calls=%async_computation | async-start | bytes 786432 | tf_op jit(solution)/shard_map/all_to_all | solution.py:31
  18.9 1.1 constant_dynamic-slice_fusion.1
  20.1 4.9 %collective-permute-start = (f32[2,128,384]{2,1,0:T(8,128)S(1)}, f32[2,128,384]{2,1,0:T(8,128)S(1)}, u32[]{:S(2)}, u32[]{:S(2)}) collective-permute-start(f32[2,128,384]{2,1,0:T(8,128)S(1)} %maximum_maximum_fusion), channel_id=1, source_target_pairs={{0,3},{1,0},{2,1},{3,2},{4,7},{5,4},{6,5},{7,6},{8,11},{9,8},{10,9... | collective-permute-start | bytes 1179656 | tf_op jit(solution)/shard_map/ppermute | solution.py:422
  25.7 1.9 %collective-permute-start.2 = (f32[2,128,256]{2,1,0:T(8,128)}, f32[2,128,256]{2,1,0:T(8,128)S(1)}, u32[]{:S(2)}, u32[]{:S(2)}) collective-permute-start(f32[2,128,256]{2,1,0:T(8,128)} %maximum_maximum_fusion.1), channel_id=1, source_target_pairs={{0,1},{1,2},{2,3},{3,0},{4,5},{5,6},{6,7},{7,4},{8,9},{9,10},{10,1... | collective-permute-start | bytes 786440 | tf_op jit(solution)/shard_map/ppermute | solution.py:422
  27.7 4.1 %collective-permute-start.1 = (f32[2,128,128]{2,1,0:T(8,128)S(1)}, f32[2,128,128]{2,1,0:T(8,128)S(1)}, u32[]{:S(2)}, u32[]{:S(2)}) collective-permute-start(f32[2,128,128]{2,1,0:T(8,128)S(1)} %pad_maximum_fusion), channel_id=1, source_target_pairs={{0,2},{1,3},{2,0},{3,1},{4,6},{5,7},{6,4},{7,5},{8,10},{9,11},{10,... | collective-permute-start | bytes 393224 | tf_op jit(solution)/shard_map/ppermute | solution.py:422
  31.8 6.6 %collective-permute-done.1.two_ref = f32[2,128,128]{2,1,0:T(8,128)S(1)} collective-permute-done((f32[2,128,128]{2,1,0:T(8,128)S(1)}, f32[2,128,128]{2,1,0:T(8,128)S(1)}, u32[]{:S(2)}, u32[]{:S(2)}) %collective-permute-start.1) | collective-permute-done | bytes 131104 | tf_op jit(solution)/shard_map/ppermute | solution.py:422
  39.3 3.3 %all-to-all-done.plane_ref = bf16[16,8,3,4,128]{4,3,2,1,0:T(4,128)(2,1)S(1)} async-done(((bf16[16,8,3,4,128]{4,3,2,1,0:T(4,128)(2,1)}), bf16[16,8,3,4,128]{4,3,2,1,0:T(4,128)(2,1)S(1)}, u32[]{:S(2)}, u32[]{:S(2)}) %all-to-all-start) | async-done | bytes 393248 | tf_op jit(solution)/shard_map/all_to_all | solution.py:31
  43.6 7.6 %all-to-all-start.1 = ((bf16[32,64,128]{2,1,0:T(8,128)(2,1)}), bf16[32,64,128]{2,1,0:T(8,128)(2,1)S(1)}, u32[]{:S(2)}, u32[]{:S(2)}) async-start(bf16[32,64,128]{2,1,0:T(8,128)(2,1)} %bitcast.1), calls=%async_computation.1 | async-start | bytes 1048576 | tf_op jit(solution)/shard_map/all_to_all | solution.py:31
  53.7 1.7 %shard_map.87 = (bf16[512,512]{1,0:T(8,128)(2,1)S(1)}, bf16[512,512]{1,0:T(8,128)(2,1)S(1)}, bf16[512,512]{1,0:T(8,128)(2,1)S(1)}, bf16[512,512]{1,0:T(8,128)(2,1)S(1)}) custom-call(s32[3]{0:T(128)S(1)} %pad_add_fusion.place_ref, f32[3,128,512]{2,1,0:T(8,128)S(1)} %copy-done, f32[3,128,512]{2,1,0:T(8,128)S(1)} %copy-done.1, ...), custom_call_target="tpu_custom_call" | custom-call | bytes 5242880 | tf_op jit(solution)/shard_map/pallas_call | solution.py:161
  58.6 2.3 %all-to-all-done.1 = bf16[32,64,128]{2,1,0:T(8,128)(2,1)S(1)} async-done(((bf16[32,64,128]{2,1,0:T(8,128)(2,1)}), bf16[32,64,128]{2,1,0:T(8,128)(2,1)S(1)}, u32[]{:S(2)}, u32[]{:S(2)}) %all-to-all-start.1) | async-done | bytes 524320 | tf_op jit(solution)/shard_map/all_to_all | solution.py:31
  62.9 5.2 %shard_map.88 = s16[32,17,4,128]{3,2,1,0:T(4,128)(2,1)} custom-call(s32[7]{0:T(128)S(1)} %concatenate.32.place_ref, bf16[8,4,64,128]{3,2,1,0:T(8,128)(2,1)S(1)} %bitcast.17, bf16[512,512]{1,0:T(8,128)(2,1)S(1)} %copy-done.5, bf16[512,512]{1,0:T(8,128)(2,1)S(1)} %copy-done.7, bf16[512,512]{1,0:T(8,128)(2,1)} %copy-done.8, bf16[512,512]{1,0:T(8,128)(2,1)} %copy-done.9), custom_call_target="tpu_custom_call" | custom-call | flops 1342177280 | bytes 4194304 | tf_op jit(solution)/shard_map/pallas_call | solution.py:255
  68.2 6.0 %all-to-all-start.2 = ((s16[32,17,4,128]{3,2,1,0:T(4,128)(2,1)}), s16[32,17,4,128]{3,2,1,0:T(4,128)(2,1)S(1)}, u32[]{:S(2)}, u32[]{:S(2)}) async-start(s16[32,17,4,128]{3,2,1,0:T(4,128)(2,1)} %shard_map.88), calls=%async_computation.2 | async-start | bytes 1114112 | tf_op jit(solution)/shard_map/all_to_all | solution.py:31
  75.0 2.6 %shard_map.89 = (s16[2,144,512]{2,1,0:T(8,128)(2,1)S(1)}, s16[2,144,512]{2,1,0:T(8,128)(2,1)S(1)}, s16[2,144,512]{2,1,0:T(8,128)(2,1)S(1)}, s16[2,144,512]{2,1,0:T(8,128)(2,1)S(1)}) custom-call(s32[7]{0:T(128)S(1)} %concatenate.32.place_ref, bf16[512,512]{1,0:T(8,128)(2,1)S(1)} %bitcast.20), custom_call_target="tpu_custom_call" | custom-call | flops 536870912 | bytes 2097152 | tf_op jit(solution)/shard_map/pallas_call | solution.py:288
  77.6 6.5 %all-to-all-done.2.back_ref = s16[32,17,4,128]{3,2,1,0:T(4,128)(2,1)S(1)} async-done(((s16[32,17,4,128]{3,2,1,0:T(4,128)(2,1)}), s16[32,17,4,128]{3,2,1,0:T(4,128)(2,1)S(1)}, u32[]{:S(2)}, u32[]{:S(2)}) %all-to-all-start.2) | async-done | bytes 557088 | tf_op jit(solution)/shard_map/all_to_all | solution.py:31
  85.0 6.0 %all-to-all-start.3 = ((s16[16,25,4,128]{3,2,1,0:T(4,128)(2,1)}), s16[16,25,4,128]{3,2,1,0:T(4,128)(2,1)S(1)}, u32[]{:S(2)}, u32[]{:S(2)}) async-start(s16[16,25,4,128]{3,2,1,0:T(4,128)(2,1)} %shard_map.90), calls=%async_computation.3 | async-start | bytes 819200 | tf_op jit(solution)/shard_map/all_to_all | solution.py:31
  91.1 2.5 %collective-permute-start.3 = (s16[2,144,512]{2,1,0:T(8,128)(2,1)S(1)}, s16[2,144,512]{2,1,0:T(8,128)(2,1)S(1)}, u32[]{:S(2)}, u32[]{:S(2)}) collective-permute-start(s16[2,144,512]{2,1,0:T(8,128)(2,1)S(1)} %get-tuple-element.42), channel_id=1, source_target_pairs={{0,1},{1,2},{2,3},{3,0},{4,5},{5,6},{6,7},{7,4},{8,9},{9,10},{10,1... | collective-permute-start | bytes 884744 | tf_op jit(solution)/shard_map/ppermute | solution.py:451
  93.6 4.2 %collective-permute-start.4 = (s16[2,144,512]{2,1,0:T(8,128)(2,1)S(1)}, s16[2,144,512]{2,1,0:T(8,128)(2,1)S(1)}, u32[]{:S(2)}, u32[]{:S(2)}) collective-permute-start(s16[2,144,512]{2,1,0:T(8,128)(2,1)S(1)} %get-tuple-element.43), channel_id=1, source_target_pairs={{0,2},{1,3},{2,0},{3,1},{4,6},{5,7},{6,4},{7,5},{8,10},{9,11},{10,... | collective-permute-start | bytes 884744 | tf_op jit(solution)/shard_map/ppermute | solution.py:451
  97.8 3.1 %collective-permute-start.5 = (s16[2,144,512]{2,1,0:T(8,128)(2,1)S(1)}, s16[2,144,512]{2,1,0:T(8,128)(2,1)S(1)}, u32[]{:S(2)}, u32[]{:S(2)}) collective-permute-start(s16[2,144,512]{2,1,0:T(8,128)(2,1)S(1)} %get-tuple-element.44), channel_id=1, source_target_pairs={{0,3},{1,0},{2,1},{3,2},{4,7},{5,4},{6,5},{7,6},{8,11},{9,8},{10,9... | collective-permute-start | bytes 884744 | tf_op jit(solution)/shard_map/ppermute | solution.py:451
  101.0 8.3 %collective-permute-done.3.one_ref = s16[2,144,512]{2,1,0:T(8,128)(2,1)S(1)} collective-permute-done((s16[2,144,512]{2,1,0:T(8,128)(2,1)S(1)}, s16[2,144,512]{2,1,0:T(8,128)(2,1)S(1)}, u32[]{:S(2)}, u32[]{:S(2)}) %collective-permute-start.3) | collective-permute-done | bytes 294944 | tf_op jit(solution)/shard_map/ppermute | solution.py:451
  109.2 2.5 %collective-permute-done.5.three_ref = s16[2,144,512]{2,1,0:T(8,128)(2,1)S(1)} collective-permute-done((s16[2,144,512]{2,1,0:T(8,128)(2,1)S(1)}, s16[2,144,512]{2,1,0:T(8,128)(2,1)S(1)}, u32[]{:S(2)}, u32[]{:S(2)}) %collective-permute-start.5) | collective-permute-done | bytes 294944 | tf_op jit(solution)/shard_map/ppermute | solution.py:451
  111.8 2.1 %shard_map.92 = (f32[3,128,512]{2,1,0:T(8,128)}, f32[3,128,512]{2,1,0:T(8,128)}) custom-call(s32[7]{0:T(128)S(1)} %concatenate.32.place_ref, s16[2,144,512]{2,1,0:T(8,128)(2,1)S(1)} %get-tuple-element.41.own_ref, s16[2,144,512]{2,1,0:T(8,128)(2,1)S(1)} %collective-permute-done.3.one_ref, s16[2,144,512]{2,1,0:T(8,128)(2,1)S(1)} %collective-permute-done.4.two_ref, ...), custom_call_target="tpu_custom_call" | custom-call | bytes 5242880 | tf_op jit(solution)/shard_map/pallas_call | solution.py:328
  113.8 2.3 %all-to-all-done.3 = s16[16,25,4,128]{3,2,1,0:T(4,128)(2,1)S(1)} async-done(((s16[16,25,4,128]{3,2,1,0:T(4,128)(2,1)}), s16[16,25,4,128]{3,2,1,0:T(4,128)(2,1)S(1)}, u32[]{:S(2)}, u32[]{:S(2)}) %all-to-all-start.3) | async-done | bytes 409632 | tf_op jit(solution)/shard_map/all_to_all | solution.py:31
  116.3 1.6 %shard_map.91 = bf16[128,4,128]{2,1,0:T(4,128)(2,1)} custom-call(s32[128]{0:T(128)S(1)} %add.141.at_ref, s32[128,128]{1,0:T(8,128)S(1)} %broadcast_in_dim.18.spot_ref, s32[128,128]{1,0:T(8,128)S(1)} %broadcast_in_dim.19.up_ref, s16[400,4,128]{2,1,0:T(4,128)(2,1)S(1)} %bitcast.19), custom_call_target="tpu_custom_call" | custom-call | bytes 1048576 | tf_op jit(solution)/shard_map/pallas_call | solution.py:393
  (44 shorter events, 11.6 us)
Async XLA Ops:
  0.6 18.3 %copy-start = (f32[3,128,512]{2,1,0:T(8,128)S(1)}, f32[3,128,512]{2,1,0:T(8,128)}, u32[]{:S(2)}) copy-start(f32[3,128,512]{2,1,0:T(8,128)} %left_ref.2) | copy-start | bytes 2359300
  3.6 39.0 %all-to-all-start = ((bf16[16,8,3,4,128]{4,3,2,1,0:T(4,128)(2,1)}), bf16[16,8,3,4,128]{4,3,2,1,0:T(4,128)(2,1)S(1)}, u32[]{:S(2)}, u32[]{:S(2)}) async-start(bf16[16,8,3,4,128]{4,3,2,1,0:T(4,128)(2,1)} %bitcast), calls=%async_computation | async-start | bytes 786432 | tf_op jit(solution)/shard_map/all_to_all | solution.py:31
  20.1 19.3 %collective-permute-start = (f32[2,128,384]{2,1,0:T(8,128)S(1)}, f32[2,128,384]{2,1,0:T(8,128)S(1)}, u32[]{:S(2)}, u32[]{:S(2)}) collective-permute-start(f32[2,128,384]{2,1,0:T(8,128)S(1)} %maximum_maximum_fusion), channel_id=1, source_target_pairs={{0,3},{1,0},{2,1},{3,2},{4,7},{5,4},{6,5},{7,6},{8,11},{9,8},{10,9... | collective-permute-start | bytes 1179656 | tf_op jit(solution)/shard_map/ppermute | solution.py:422
  25.7 13.6 %collective-permute-start.2 = (f32[2,128,256]{2,1,0:T(8,128)}, f32[2,128,256]{2,1,0:T(8,128)S(1)}, u32[]{:S(2)}, u32[]{:S(2)}) collective-permute-start(f32[2,128,256]{2,1,0:T(8,128)} %maximum_maximum_fusion.1), channel_id=1, source_target_pairs={{0,1},{1,2},{2,3},{3,0},{4,5},{5,6},{6,7},{7,4},{8,9},{9,10},{10,1... | collective-permute-start | bytes 786440 | tf_op jit(solution)/shard_map/ppermute | solution.py:422
  27.7 10.7 %collective-permute-start.1 = (f32[2,128,128]{2,1,0:T(8,128)S(1)}, f32[2,128,128]{2,1,0:T(8,128)S(1)}, u32[]{:S(2)}, u32[]{:S(2)}) collective-permute-start(f32[2,128,128]{2,1,0:T(8,128)S(1)} %pad_maximum_fusion), channel_id=1, source_target_pairs={{0,2},{1,3},{2,0},{3,1},{4,6},{5,7},{6,4},{7,5},{8,10},{9,11},{10,... | collective-permute-start | bytes 393224 | tf_op jit(solution)/shard_map/ppermute | solution.py:422
  31.8 21.8 %copy-start.1 = (f32[3,128,512]{2,1,0:T(8,128)S(1)}, f32[3,128,512]{2,1,0:T(8,128)}, u32[]{:S(2)}) copy-start(f32[3,128,512]{2,1,0:T(8,128)} %right_ref.2) | copy-start | bytes 2359300
  43.6 17.3 %all-to-all-start.1 = ((bf16[32,64,128]{2,1,0:T(8,128)(2,1)}), bf16[32,64,128]{2,1,0:T(8,128)(2,1)S(1)}, u32[]{:S(2)}, u32[]{:S(2)}) async-start(bf16[32,64,128]{2,1,0:T(8,128)(2,1)} %bitcast.1), calls=%async_computation.1 | async-start | bytes 1048576 | tf_op jit(solution)/shard_map/all_to_all | solution.py:31
  51.3 0.7 copy-start.10
  55.4 0.8 copy-start.4
  56.2 0.8 copy-start.6
  57.0 0.8 copy-start.8
  57.8 0.8 copy-start.9
  60.9 1.0 copy-start.5
  61.9 1.0 copy-start.7
  68.2 15.9 %all-to-all-start.2 = ((s16[32,17,4,128]{3,2,1,0:T(4,128)(2,1)}), s16[32,17,4,128]{3,2,1,0:T(4,128)(2,1)S(1)}, u32[]{:S(2)}, u32[]{:S(2)}) async-start(s16[32,17,4,128]{3,2,1,0:T(4,128)(2,1)} %shard_map.88), calls=%async_computation.2 | async-start | bytes 1114112 | tf_op jit(solution)/shard_map/all_to_all | solution.py:31
  84.1 27.6 %copy-start.2 = (f32[3,128,512]{2,1,0:T(8,128)S(1)}, f32[3,128,512]{2,1,0:T(8,128)}, u32[]{:S(2)}) copy-start(f32[3,128,512]{2,1,0:T(8,128)} %left_ref.3) | copy-start | bytes 2359300
  84.1 27.6 %copy-start.3 = (f32[3,128,512]{2,1,0:T(8,128)S(1)}, f32[3,128,512]{2,1,0:T(8,128)}, u32[]{:S(2)}) copy-start(f32[3,128,512]{2,1,0:T(8,128)} %right_ref.3) | copy-start | bytes 2359300
  85.0 31.1 %all-to-all-start.3 = ((s16[16,25,4,128]{3,2,1,0:T(4,128)(2,1)}), s16[16,25,4,128]{3,2,1,0:T(4,128)(2,1)S(1)}, u32[]{:S(2)}, u32[]{:S(2)}) async-start(s16[16,25,4,128]{3,2,1,0:T(4,128)(2,1)} %shard_map.90), calls=%async_computation.3 | async-start | bytes 819200 | tf_op jit(solution)/shard_map/all_to_all | solution.py:31
  91.1 18.2 %collective-permute-start.3 = (s16[2,144,512]{2,1,0:T(8,128)(2,1)S(1)}, s16[2,144,512]{2,1,0:T(8,128)(2,1)S(1)}, u32[]{:S(2)}, u32[]{:S(2)}) collective-permute-start(s16[2,144,512]{2,1,0:T(8,128)(2,1)S(1)} %get-tuple-element.42), channel_id=1, source_target_pairs={{0,1},{1,2},{2,3},{3,0},{4,5},{5,6},{6,7},{7,4},{8,9},{9,10},{10,1... | collective-permute-start | bytes 884744 | tf_op jit(solution)/shard_map/ppermute | solution.py:451
  93.6 15.6 %collective-permute-start.4 = (s16[2,144,512]{2,1,0:T(8,128)(2,1)S(1)}, s16[2,144,512]{2,1,0:T(8,128)(2,1)S(1)}, u32[]{:S(2)}, u32[]{:S(2)}) collective-permute-start(s16[2,144,512]{2,1,0:T(8,128)(2,1)S(1)} %get-tuple-element.43), channel_id=1, source_target_pairs={{0,2},{1,3},{2,0},{3,1},{4,6},{5,7},{6,4},{7,5},{8,10},{9,11},{10,... | collective-permute-start | bytes 884744 | tf_op jit(solution)/shard_map/ppermute | solution.py:451
  97.8 14.0 %collective-permute-start.5 = (s16[2,144,512]{2,1,0:T(8,128)(2,1)S(1)}, s16[2,144,512]{2,1,0:T(8,128)(2,1)S(1)}, u32[]{:S(2)}, u32[]{:S(2)}) collective-permute-start(s16[2,144,512]{2,1,0:T(8,128)(2,1)S(1)} %get-tuple-element.44), channel_id=1, source_target_pairs={{0,3},{1,0},{2,1},{3,2},{4,7},{5,4},{6,5},{7,6},{8,11},{9,8},{10,9... | collective-permute-start | bytes 884744 | tf_op jit(solution)/shard_map/ppermute | solution.py:451
